TPU v7x, 32 devices: a whole 2x2x4 slice. The times are simulated.
32 devices in a mesh: lat: 4 (over y, x), lon: 8 (over z, core).
Axes of the slice: x: 2, y: 2, z: 4, core: 2. Of those that a mesh axis runs over, the one named last changes fastest.
Arguments:
- coarse: bfloat16 [73, 16, 64], P(None, 'lat', 'lon'), may hold values from -6 to 6
- row_src: int32 [128], P('lat'), may hold values from 0 to 14, as said below
- row_frac: float32 [128], P('lat'), may hold values from 0 to 1
- col_src: int32 [1024], P('lon'), may hold values from 0 to 63, as said below
- col_frac: float32 [1024], P('lon'), may hold values from 0 to 1
- embed_weight: bfloat16 [73, 128], replicated, may hold values from -0.75 to 0.75
- conv1_weight: bfloat16 [3, 3, 128, 128], replicated, may hold values from -0.1875 to 0.1875
- conv2_weight: bfloat16 [3, 3, 128, 128], replicated, may hold values from -0.1875 to 0.1875
- cotangent: bfloat16 [128, 1024, 128], P('lat', 'lon'), may hold values from -6 to 6
Outputs:
- features: bfloat16 [128, 1024, 128], P('lat', 'lon')
- grad_embed: float32 [73, 128], replicated
- grad_conv1: float32 [3, 3, 128, 128], replicated
- grad_conv2: float32 [3, 3, 128, 128], replicated
Inputs may be any that keep to these rules, and one draw needn't show every extreme that they name: row_src[r] differs from (r * 16) // 128 by at most 1; both bounds are reached. col_src[c] differs cyclically (mod 64) from (c * 64) // 1024 by at most 1; both bounds are reached.
All inputs are finite; a program needn't handle non-finite values.
Results may differ from a plain program's by a relative error of at most 0.0062.
Values may be sent and summed in bfloat16 or wider, within the bound.
No kernel may reach another device: no remote copies, remote signals or barrier semaphores. Data moves between devices by JAX's collectives and lax.ppermute only.
A program may use at most 128 MiB of HBM per device.

v0:
```python
import math

import jax
import jax.numpy as jnp
from jax import lax
from jax.sharding import PartitionSpec as P


def with_halo(x, sides, width):
    for axis, dim in sides:
        peers, length = (lax.axis_size(axis), x.shape[dim])
        up = [(i, (i + 1) % peers) for i in range(peers)]
        down = [(j, i) for i, j in up]
        last = lax.slice_in_dim(x, length - width, length, axis=dim)
        first = lax.slice_in_dim(x, 0, width, axis=dim)
        before = lax.ppermute(last, axis, up)
        after = lax.ppermute(first, axis, down)
        x = jnp.concatenate([before, x, after], axis=dim)
    return x


def edge_zero(padded, depth, lat_place, lat_count):
    line = jnp.arange(padded.shape[0])
    keep = ((line >= depth) | (lat_place > 0)) & (
        (line < padded.shape[0] - depth) | (lat_place < lat_count - 1)
    )
    return padded * keep.astype(padded.dtype)[:, None, None]


def convolve(padded, weight, span_rows, span_cols):
    channels = weight.shape[2]
    total = jnp.zeros((span_rows * span_cols, weight.shape[3]), jnp.float32)
    for tap_row in range(3):
        for tap_col in range(3):
            window = padded[tap_row : tap_row + span_rows, tap_col : tap_col + span_cols].reshape(
                -1, channels
            )
            total = total + jnp.dot(
                window, weight[tap_row, tap_col], preferred_element_type=jnp.float32
            )
    return total.reshape(span_rows, span_cols, -1)


def convolve_back(padded, weight, span_rows, span_cols):
    channels = weight.shape[3]
    total = jnp.zeros((span_rows * span_cols, weight.shape[2]), jnp.float32)
    for tap_row in range(3):
        for tap_col in range(3):
            window = padded[
                2 - tap_row : 2 - tap_row + span_rows, 2 - tap_col : 2 - tap_col + span_cols
            ].reshape(-1, channels)
            total = total + jnp.dot(
                window, weight[tap_row, tap_col].T, preferred_element_type=jnp.float32
            )
    return total.reshape(span_rows, span_cols, -1)


def weight_grads(padded, delta, span_rows, span_cols):
    channels = padded.shape[2]
    flat_delta = delta.reshape(-1, delta.shape[2])
    blocks = []
    for tap_row in range(3):
        line = []
        for tap_col in range(3):
            window = padded[tap_row : tap_row + span_rows, tap_col : tap_col + span_cols].reshape(
                -1, channels
            )
            line.append(
                lax.dot_general(
                    window, flat_delta, (((0,), (0,)), ((), ())), preferred_element_type=jnp.float32
                )
            )
        blocks.append(jnp.stack(line))
    return jnp.stack(blocks)


def blend_matrix(local_index, fraction, length):
    line = jnp.arange(length, dtype=jnp.int32)
    lower = (line[None, :] == local_index[:, None]).astype(jnp.float32)
    upper = (line[None, :] == local_index[:, None] + 1).astype(jnp.float32)
    return (1.0 - fraction)[:, None] * lower + fraction[:, None] * upper


def lift_cells(
    widened,
    row_index,
    row_weight,
    col_index,
    col_weight,
    embed_weight,
    lat_place,
    lon_place,
    band_rows,
    band_cols,
    lon_count,
):
    row_local = row_index - (lat_place * band_rows - 3)
    col_local = jnp.mod(col_index - lon_place * band_cols + 3, band_cols * lon_count)
    row_blend = blend_matrix(row_local, row_weight, band_rows + 6)
    col_blend = blend_matrix(col_local, col_weight, band_cols + 6)
    row_mixed = jnp.einsum("rj,kjl->krl", row_blend, widened, precision=lax.Precision.HIGHEST)
    fine_input = jnp.einsum(
        "krl,cl->krc", row_mixed, col_blend, precision=lax.Precision.HIGHEST
    ).astype(jnp.bfloat16)
    lifted = jnp.einsum(
        "krc,kh->rch", fine_input, embed_weight, preferred_element_type=jnp.float32
    ).astype(jnp.bfloat16)
    return (fine_input, lifted)


def on_device(
    coarse,
    row_src,
    row_frac,
    col_src,
    col_frac,
    embed_weight,
    conv1_weight,
    conv2_weight,
    cotangent,
):
    lat_count = lax.axis_size("lat")
    lon_count = lax.axis_size("lon")
    lat_place = lax.axis_index("lat")
    lon_place = lax.axis_index("lon")
    band_rows = coarse.shape[1]
    band_cols = coarse.shape[2]
    tile_rows = cotangent.shape[0]
    tile_cols = cotangent.shape[1]
    widened = with_halo(coarse, (("lat", 1), ("lon", 2)), 3).astype(jnp.float32)
    fine_input, lifted = lift_cells(
        widened,
        row_src,
        row_frac,
        col_src,
        col_frac,
        embed_weight,
        lat_place,
        lon_place,
        band_rows,
        band_cols,
        lon_count,
    )
    lifted_pad = edge_zero(with_halo(lifted, (("lat", 0), ("lon", 1)), 1), 1, lat_place, lat_count)
    pre_first = convolve(lifted_pad, conv1_weight, tile_rows, tile_cols)
    hidden = jax.nn.silu(pre_first).astype(jnp.bfloat16)
    hidden_pad = edge_zero(with_halo(hidden, (("lat", 0), ("lon", 1)), 1), 1, lat_place, lat_count)
    features = (
        lifted.astype(jnp.float32) + convolve(hidden_pad, conv2_weight, tile_rows, tile_cols)
    ).astype(jnp.bfloat16)
    cot_pad = edge_zero(with_halo(cotangent, (("lat", 0), ("lon", 1)), 1), 1, lat_place, lat_count)
    grad_second = weight_grads(hidden_pad, cotangent, tile_rows, tile_cols)
    back_hidden = convolve_back(cot_pad, conv2_weight, tile_rows, tile_cols)
    sig = jax.nn.sigmoid(pre_first)
    delta = (back_hidden * sig * (1.0 + pre_first * (1.0 - sig))).astype(jnp.bfloat16)
    delta_pad = edge_zero(with_halo(delta, (("lat", 0), ("lon", 1)), 1), 1, lat_place, lat_count)
    grad_first = weight_grads(lifted_pad, delta, tile_rows, tile_cols)
    back_lifted = (
        cotangent.astype(jnp.float32) + convolve_back(delta_pad, conv1_weight, tile_rows, tile_cols)
    ).astype(jnp.bfloat16)
    grad_lift = jnp.einsum(
        "krc,rch->kh", fine_input, back_lifted, preferred_element_type=jnp.float32
    )
    norm_scale = 1.0 / math.sqrt(tile_rows * lat_count * tile_cols * lon_count)
    terms = (grad_lift * norm_scale, grad_first * norm_scale, grad_second * norm_scale)
    totals = lax.psum((terms[0], terms[1], terms[2]), ("lat", "lon"))
    return (features, totals[0], totals[1], totals[2])


def solution(mesh):
    in_specs = (
        P(None, "lat", "lon"),
        P("lat"),
        P("lat"),
        P("lon"),
        P("lon"),
        P(),
        P(),
        P(),
        P("lat", "lon", None),
    )
    out_specs = (P("lat", "lon", None), P(), P(), P())
    return jax.shard_map(
        on_device, mesh=mesh, in_specs=in_specs, out_specs=out_specs, check_vma=False
    )
```

profile of v0, /device:TPU:0, one launch (start us, length us, event | category | flops | bytes accessed | tf_op | source)
XLA Modules:
  0.0 292.1 jit_solution(5616198827418184282)
XLA Ops:
  8.0 3.9 %collective-permute-start.1 = (bf16[73,3,8]{0,2,1:T(8,128)(2,1)S(1)}, bf16[73,3,8]{0,2,1:T(8,128)(2,1)S(1)}, u32[]{:S(2)}, u32[]{:S(2)}) collective-permute-start(bf16[73,3,8]{0,2,1:T(8,128)(2,1)S(1)} %get-tuple-element.66), channel_id=1, source_target_pairs={{8,0},{16,8},{24,16},{0,24},{9,1},{17,9},{25,17},{1,25},{10,2},{18... | collective-permute-start | bytes 10520 | tf_op jit(solution)/shard_map/ppermute | solution.py:17
  12.7 2.9 %collective-permute-start.13 = (bf16[1,128,128]{2,1,0:T(8,128)(2,1)S(1)}, bf16[1,128,128]{2,1,0:T(8,128)(2,1)S(1)}, u32[]{:S(2)}, u32[]{:S(2)}) collective-permute-start(bf16[1,128,128]{2,1,0:T(8,128)(2,1)S(1)} %get-tuple-element.58), channel_id=1, source_target_pairs={{8,0},{16,8},{24,16},{0,24},{9,1},{17,9},{25,17},{1,25},{10,2},{18... | collective-permute-start | bytes 98312 | tf_op jit(solution)/shard_map/ppermute | solution.py:17
  18.4 3.5 %collective-permute-start.3 = (bf16[73,10,3]{0,2,1:T(4,128)(2,1)S(1)}, bf16[73,10,3]{0,2,1:T(4,128)(2,1)S(1)}, u32[]{:S(2)}, u32[]{:S(2)}) collective-permute-start(bf16[73,10,3]{0,2,1:T(4,128)(2,1)S(1)} %get-tuple-element.65), channel_id=1, source_target_pairs={{1,0},{2,1},{3,2},{4,3},{5,4},{6,5},{7,6},{0,7},{9,8},{10,9},{11,1... | collective-permute-start | bytes 13148 | tf_op jit(solution)/shard_map/ppermute | solution.py:17
  23.3 1.1 fusion.4
  24.8 2.7 convolution_convert_fusion.1
  28.0 2.0 collective-permute-start.4
  30.0 1.0 collective-permute-start.5
  31.3 3.5 %collective-permute-start.15 = (bf16[34,1,128]{2,1,0:T(2,128)(2,1)S(1)}, bf16[34,1,128]{2,1,0:T(2,128)(2,1)S(1)}, u32[]{:S(2)}, u32[]{:S(2)}) collective-permute-start(bf16[34,1,128]{2,1,0:T(2,128)(2,1)S(1)} %get-tuple-element.51), channel_id=1, source_target_pairs={{1,0},{2,1},{3,2},{4,3},{5,4},{6,5},{7,6},{0,7},{9,8},{10,9},{11,1... | collective-permute-start | bytes 26120 | tf_op jit(solution)/shard_map/ppermute | solution.py:17
  35.0 3.5 %collective-permute-start.7 = (bf16[34,1,128]{2,1,0:T(2,128)(2,1)S(1)}, bf16[34,1,128]{2,1,0:T(2,128)(2,1)S(1)}, u32[]{:S(2)}, u32[]{:S(2)}) collective-permute-start(bf16[34,1,128]{2,1,0:T(2,128)(2,1)S(1)} %get-tuple-element.55), channel_id=1, source_target_pairs={{1,0},{2,1},{3,2},{4,3},{5,4},{6,5},{7,6},{0,7},{9,8},{10,9},{11,1... | collective-permute-start | bytes 26120 | tf_op jit(solution)/shard_map/ppermute | solution.py:17
  38.5 1.4 collective-permute-done.6
  40.0 1.9 maximum_multiply_fusion.2
  41.9 5.8 %fusion.123 = (bf16[32,128,128]{2,1,0:T(8,128)(2,1)S(1)}, bf16[32,128,128]{2,1,0:T(8,128)(2,1)S(1)}, bf16[32,128,128]{2,1,0:T(8,128)(2,1)}, bf16[32,128,128]{2,1...) fusion(bf16[34,130,128]{2,1,0:T(8,128)(2,1)S(1)} %get-tuple-ele, ...), kind=kLoop, calls=%fused_computation.222 | loop fusion | bytes 37748736 | tf_op jit(solution)/shard_map/slice | solution.py:49
  58.1 0.8 copy-done.11
  61.8 1.0 multiply_convert_fusion
  67.3 1.1 collective-permute-start.8
  68.4 1.9 collective-permute-start.9
  70.4 2.8 collective-permute-start.17
  73.4 3.5 %collective-permute-start.11 = (bf16[34,1,128]{2,1,0:T(2,128)(2,1)S(1)}, bf16[34,1,128]{2,1,0:T(2,128)(2,1)S(1)}, u32[]{:S(2)}, u32[]{:S(2)}) collective-permute-start(bf16[34,1,128]{2,1,0:T(2,128)(2,1)S(1)} %get-tuple-element.53), channel_id=1, source_target_pairs={{1,0},{2,1},{3,2},{4,3},{5,4},{6,5},{7,6},{0,7},{9,8},{10,9},{11,1... | collective-permute-start | bytes 26120 | tf_op jit(solution)/shard_map/ppermute | solution.py:17
  77.0 3.5 %collective-permute-start.19 = (bf16[34,1,128]{2,1,0:T(2,128)(2,1)S(1)}, bf16[34,1,128]{2,1,0:T(2,128)(2,1)S(1)}, u32[]{:S(2)}, u32[]{:S(2)}) collective-permute-start(bf16[34,1,128]{2,1,0:T(2,128)(2,1)S(1)} %get-tuple-element.49), channel_id=1, source_target_pairs={{1,0},{2,1},{3,2},{4,3},{5,4},{6,5},{7,6},{0,7},{9,8},{10,9},{11,1... | collective-permute-start | bytes 26120 | tf_op jit(solution)/shard_map/ppermute | solution.py:17
  80.6 0.9 maximum_multiply_fusion.4
  82.0 2.5 maximum_multiply_fusion.3
  84.5 1.1 convolution_bitcast_fusion
  85.6 1.1 convolution_bitcast_fusion.8
  86.7 1.1 convolution_bitcast_fusion.7
  87.8 1.1 convolution_bitcast_fusion.6
  88.9 1.1 convolution_bitcast_fusion.5
  90.0 1.1 convolution_bitcast_fusion.4
  91.1 1.1 convolution_bitcast_fusion.3
  92.2 1.1 convolution_bitcast_fusion.2
  93.3 1.1 convolution_bitcast_fusion.1
  94.4 3.8 %fusion.124 = (bf16[32,128,128]{2,1,0:T(8,128)(2,1)}, bf16[32,128,128]{2,1,0:T(8,128)(2,1)}, bf16[32,128,128]{2,1,0:T(8,128)(2,1)}, bf16[32,128,128]{2,1,0:T(8,1...) fusion(bf16[34,130,128]{2,1,0:T(8,128)(2,1)S(1)} %get-tuple-ele, ...), kind=kLoop, calls=%fused_computation.223 | loop fusion | bytes 18874368 | tf_op jit(solution)/shard_map/slice | solution.py:35
  98.7 1.9 fusion.122
  105.8 39.3 %psum.21 = f32[73,128]{1,0:T(8,128)} all-reduce(f32[73,128]{1,0:T(8,128)S(1)} %fusion), channel_id=1, replica_groups=mesh['lat'=4,'lon'=8] {'lat','lon'}, use_global_device_ids=true, to_apply=%region_0.1 | all-reduce | flops 9344 | bytes 74752 | tf_op jit(solution)/shard_map/psum | solution.py:166
  145.2 0.9 maximum_bitcast_fusion.3
  146.1 0.9 maximum_bitcast_fusion.4
  147.0 0.9 maximum_bitcast_fusion.5
  147.9 0.9 maximum_multiply_fusion.5
  148.8 1.7 convolution_add_fusion.23
  151.0 0.8 copy-done.9
  152.2 0.8 copy-done.8
  153.5 0.8 copy-done.7
  154.7 0.8 copy-done.6
  155.9 0.8 copy-done.5
  157.2 0.8 copy-done.4
  158.4 1.3 add_convert_fusion.1
  159.7 121.7 %all-reduce.3.cloned.1.call-done = (f32[3,3,128,128]{3,2,1,0:T(8,128)}, f32[3,3,128,128]{3,2,1,0:T(8,128)}) async-done(((f32[3,3,128,128]{3,2,1,0:T(8,128)}, f32[3,3,128,128]{3,2,1,0:T(8,128)}), (f32[3,3,128,128]{3,2,1,0:T(8,128)}, f32[3,3,128,128]{3,2,1,0:T(8,128)})) %all-reduce.3.cloned.1.call-update) | async-done | bytes 1179664 | tf_op jit(solution)/shard_map/psum | solution.py:166
  281.4 1.9 copy.65
  283.4 1.9 copy.66
  (138 shorter events, 34.0 us)
Async XLA Ops:
  7.2 20.3 %copy-start = (bf16[73,128]{1,0:T(8,128)(2,1)S(1)}, bf16[73,128]{1,0:T(8,128)(2,1)}, u32[]{:S(2)}) copy-start(bf16[73,128]{1,0:T(8,128)(2,1)} %param.14) | copy-start | bytes 56068
  7.2 274.3 %all-reduce.3.cloned.1.call-start = ((), (), s32[]{:S(2)}) async-start(), calls=%async_computation | async-start | bytes 2359296 | tf_op jit(solution)/shard_map/psum | solution.py:166
  8.0 10.3 %collective-permute-start.1 = (bf16[73,3,8]{0,2,1:T(8,128)(2,1)S(1)}, bf16[73,3,8]{0,2,1:T(8,128)(2,1)S(1)}, u32[]{:S(2)}, u32[]{:S(2)}) collective-permute-start(bf16[73,3,8]{0,2,1:T(8,128)(2,1)S(1)} %get-tuple-element.66), channel_id=1, source_target_pairs={{8,0},{16,8},{24,16},{0,24},{9,1},{17,9},{25,17},{1,25},{10,2},{18... | collective-permute-start | bytes 10520 | tf_op jit(solution)/shard_map/ppermute | solution.py:17
  11.9 5.7 %collective-permute-start = (bf16[73,3,8]{0,2,1:T(8,128)(2,1)S(1)}, bf16[73,3,8]{0,2,1:T(8,128)(2,1)S(1)}, u32[]{:S(2)}, u32[]{:S(2)}) collective-permute-start(bf16[73,3,8]{0,2,1:T(8,128)(2,1)S(1)} %get-tuple-element.67), channel_id=1, source_target_pairs={{0,8},{8,16},{16,24},{24,0},{1,9},{9,17},{17,25},{25,1},{2,10},{10... | collective-permute-start | bytes 10520 | tf_op jit(solution)/shard_map/ppermute | solution.py:16
  12.7 18.5 %collective-permute-start.13 = (bf16[1,128,128]{2,1,0:T(8,128)(2,1)S(1)}, bf16[1,128,128]{2,1,0:T(8,128)(2,1)S(1)}, u32[]{:S(2)}, u32[]{:S(2)}) collective-permute-start(bf16[1,128,128]{2,1,0:T(8,128)(2,1)S(1)} %get-tuple-element.58), channel_id=1, source_target_pairs={{8,0},{16,8},{24,16},{0,24},{9,1},{17,9},{25,17},{1,25},{10,2},{18... | collective-permute-start | bytes 98312 | tf_op jit(solution)/shard_map/ppermute | solution.py:17
  15.6 15.5 %collective-permute-start.12 = (bf16[1,128,128]{2,1,0:T(8,128)(2,1)S(1)}, bf16[1,128,128]{2,1,0:T(8,128)(2,1)S(1)}, u32[]{:S(2)}, u32[]{:S(2)}) collective-permute-start(bf16[1,128,128]{2,1,0:T(8,128)(2,1)S(1)} %get-tuple-element.59), channel_id=1, source_target_pairs={{0,8},{8,16},{16,24},{24,0},{1,9},{9,17},{17,25},{25,1},{2,10},{10... | collective-permute-start | bytes 98312 | tf_op jit(solution)/shard_map/ppermute | solution.py:16
  18.3 4.9 %collective-permute-start.2 = (bf16[73,10,3]{0,2,1:T(4,128)(2,1)S(1)}, bf16[73,10,3]{0,2,1:T(4,128)(2,1)S(1)}, u32[]{:S(2)}, u32[]{:S(2)}) collective-permute-start(bf16[73,10,3]{0,2,1:T(4,128)(2,1)S(1)} %get-tuple-element.64), channel_id=1, source_target_pairs={{0,1},{1,2},{2,3},{3,4},{4,5},{5,6},{6,7},{7,0},{8,9},{9,10},{10,1... | collective-permute-start | bytes 13148 | tf_op jit(solution)/shard_map/ppermute | solution.py:16
  18.4 4.9 %collective-permute-start.3 = (bf16[73,10,3]{0,2,1:T(4,128)(2,1)S(1)}, bf16[73,10,3]{0,2,1:T(4,128)(2,1)S(1)}, u32[]{:S(2)}, u32[]{:S(2)}) collective-permute-start(bf16[73,10,3]{0,2,1:T(4,128)(2,1)S(1)} %get-tuple-element.65), channel_id=1, source_target_pairs={{1,0},{2,1},{3,2},{4,3},{5,4},{6,5},{7,6},{0,7},{9,8},{10,9},{11,1... | collective-permute-start | bytes 13148 | tf_op jit(solution)/shard_map/ppermute | solution.py:17
  23.3 7.7 %copy-start.2 = (bf16[32,128,128]{2,1,0:T(8,128)(2,1)S(1)}, bf16[32,128,128]{2,1,0:T(8,128)(2,1)}, u32[]{:S(2)}) copy-start(bf16[32,128,128]{2,1,0:T(8,128)(2,1)} %param.17) | copy-start | bytes 3145732
  28.0 6.9 %collective-permute-start.4 = (bf16[1,128,128]{2,1,0:T(8,128)(2,1)S(1)}, bf16[1,128,128]{2,1,0:T(8,128)(2,1)S(1)}, u32[]{:S(2)}, u32[]{:S(2)}) collective-permute-start(bf16[1,128,128]{2,1,0:T(8,128)(2,1)S(1)} %get-tuple-element.62), channel_id=1, source_target_pairs={{0,8},{8,16},{16,24},{24,0},{1,9},{9,17},{17,25},{25,1},{2,10},{10... | collective-permute-start | bytes 98312 | tf_op jit(solution)/shard_map/ppermute | solution.py:16
  30.0 4.8 %collective-permute-start.5 = (bf16[1,128,128]{2,1,0:T(8,128)(2,1)S(1)}, bf16[1,128,128]{2,1,0:T(8,128)(2,1)S(1)}, u32[]{:S(2)}, u32[]{:S(2)}) collective-permute-start(bf16[1,128,128]{2,1,0:T(8,128)(2,1)S(1)} %get-tuple-element.63), channel_id=1, source_target_pairs={{8,0},{16,8},{24,16},{0,24},{9,1},{17,9},{25,17},{1,25},{10,2},{18... | collective-permute-start | bytes 98312 | tf_op jit(solution)/shard_map/ppermute | solution.py:17
  31.3 7.2 %collective-permute-start.14 = (bf16[34,1,128]{2,1,0:T(2,128)(2,1)S(1)}, bf16[34,1,128]{2,1,0:T(2,128)(2,1)S(1)}, u32[]{:S(2)}, u32[]{:S(2)}) collective-permute-start(bf16[34,1,128]{2,1,0:T(2,128)(2,1)S(1)} %get-tuple-element.50), channel_id=1, source_target_pairs={{0,1},{1,2},{2,3},{3,4},{4,5},{5,6},{6,7},{7,0},{8,9},{9,10},{10,1... | collective-permute-start | bytes 26120 | tf_op jit(solution)/shard_map/ppermute | solution.py:16
  31.3 7.2 %collective-permute-start.15 = (bf16[34,1,128]{2,1,0:T(2,128)(2,1)S(1)}, bf16[34,1,128]{2,1,0:T(2,128)(2,1)S(1)}, u32[]{:S(2)}, u32[]{:S(2)}) collective-permute-start(bf16[34,1,128]{2,1,0:T(2,128)(2,1)S(1)} %get-tuple-element.51), channel_id=1, source_target_pairs={{1,0},{2,1},{3,2},{4,3},{5,4},{6,5},{7,6},{0,7},{9,8},{10,9},{11,1... | collective-permute-start | bytes 26120 | tf_op jit(solution)/shard_map/ppermute | solution.py:17
  34.9 5.0 %collective-permute-start.6 = (bf16[34,1,128]{2,1,0:T(2,128)(2,1)S(1)}, bf16[34,1,128]{2,1,0:T(2,128)(2,1)S(1)}, u32[]{:S(2)}, u32[]{:S(2)}) collective-permute-start(bf16[34,1,128]{2,1,0:T(2,128)(2,1)S(1)} %get-tuple-element.54), channel_id=1, source_target_pairs={{0,1},{1,2},{2,3},{3,4},{4,5},{5,6},{6,7},{7,0},{8,9},{9,10},{10,1... | collective-permute-start | bytes 26120 | tf_op jit(solution)/shard_map/ppermute | solution.py:16
  35.0 5.0 %collective-permute-start.7 = (bf16[34,1,128]{2,1,0:T(2,128)(2,1)S(1)}, bf16[34,1,128]{2,1,0:T(2,128)(2,1)S(1)}, u32[]{:S(2)}, u32[]{:S(2)}) collective-permute-start(bf16[34,1,128]{2,1,0:T(2,128)(2,1)S(1)} %get-tuple-element.55), channel_id=1, source_target_pairs={{1,0},{2,1},{3,2},{4,3},{5,4},{6,5},{7,6},{0,7},{9,8},{10,9},{11,1... | collective-permute-start | bytes 26120 | tf_op jit(solution)/shard_map/ppermute | solution.py:17
  41.9 5.8 %copy-start.21 = (bf16[3,3,128,128]{3,2,1,0:T(8,128)(2,1)S(1)}, bf16[3,3,128,128]{3,2,1,0:T(8,128)(2,1)}, u32[]{:S(2)}) copy-start(bf16[3,3,128,128]{3,2,1,0:T(8,128)(2,1)} %param.16) | copy-start | bytes 884740
  47.7 1.2 copy-start.19
  48.9 1.2 copy-start.18
  50.1 1.2 copy-start.17
  51.3 1.2 copy-start.16
  52.6 1.2 copy-start.15
  53.8 1.2 copy-start.14
  55.9 1.2 copy-start.13
  55.9 1.3 copy-start.20
  56.3 1.3 copy-start.12
  57.7 1.2 copy-start.11
  67.3 6.0 %collective-permute-start.8 = (bf16[1,128,128]{2,1,0:T(8,128)(2,1)S(1)}, bf16[1,128,128]{2,1,0:T(8,128)(2,1)S(1)}, u32[]{:S(2)}, u32[]{:S(2)}) collective-permute-start(bf16[1,128,128]{2,1,0:T(8,128)(2,1)S(1)} %get-tuple-element.60), channel_id=1, source_target_pairs={{0,8},{8,16},{16,24},{24,0},{1,9},{9,17},{17,25},{25,1},{2,10},{10... | collective-permute-start | bytes 98312 | tf_op jit(solution)/shard_map/ppermute | solution.py:16
  68.4 4.9 %collective-permute-start.9 = (bf16[1,128,128]{2,1,0:T(8,128)(2,1)S(1)}, bf16[1,128,128]{2,1,0:T(8,128)(2,1)S(1)}, u32[]{:S(2)}, u32[]{:S(2)}) collective-permute-start(bf16[1,128,128]{2,1,0:T(8,128)(2,1)S(1)} %get-tuple-element.61), channel_id=1, source_target_pairs={{8,0},{16,8},{24,16},{0,24},{9,1},{17,9},{25,17},{1,25},{10,2},{18... | collective-permute-start | bytes 98312 | tf_op jit(solution)/shard_map/ppermute | solution.py:17
  70.3 6.7 %collective-permute-start.16 = (bf16[1,128,128]{2,1,0:T(8,128)(2,1)S(1)}, bf16[1,128,128]{2,1,0:T(8,128)(2,1)S(1)}, u32[]{:S(2)}, u32[]{:S(2)}) collective-permute-start(bf16[1,128,128]{2,1,0:T(8,128)(2,1)S(1)} %get-tuple-element.56), channel_id=1, source_target_pairs={{0,8},{8,16},{16,24},{24,0},{1,9},{9,17},{17,25},{25,1},{2,10},{10... | collective-permute-start | bytes 98312 | tf_op jit(solution)/shard_map/ppermute | solution.py:16
  70.4 6.5 %collective-permute-start.17 = (bf16[1,128,128]{2,1,0:T(8,128)(2,1)S(1)}, bf16[1,128,128]{2,1,0:T(8,128)(2,1)S(1)}, u32[]{:S(2)}, u32[]{:S(2)}) collective-permute-start(bf16[1,128,128]{2,1,0:T(8,128)(2,1)S(1)} %get-tuple-element.57), channel_id=1, source_target_pairs={{8,0},{16,8},{24,16},{0,24},{9,1},{17,9},{25,17},{1,25},{10,2},{18... | collective-permute-start | bytes 98312 | tf_op jit(solution)/shard_map/ppermute | solution.py:17
  73.3 8.1 %collective-permute-start.10 = (bf16[34,1,128]{2,1,0:T(2,128)(2,1)S(1)}, bf16[34,1,128]{2,1,0:T(2,128)(2,1)S(1)}, u32[]{:S(2)}, u32[]{:S(2)}) collective-permute-start(bf16[34,1,128]{2,1,0:T(2,128)(2,1)S(1)} %get-tuple-element.52), channel_id=1, source_target_pairs={{0,1},{1,2},{2,3},{3,4},{4,5},{5,6},{6,7},{7,0},{8,9},{9,10},{10,1... | collective-permute-start | bytes 26120 | tf_op jit(solution)/shard_map/ppermute | solution.py:16
  73.4 8.0 %collective-permute-start.11 = (bf16[34,1,128]{2,1,0:T(2,128)(2,1)S(1)}, bf16[34,1,128]{2,1,0:T(2,128)(2,1)S(1)}, u32[]{:S(2)}, u32[]{:S(2)}) collective-permute-start(bf16[34,1,128]{2,1,0:T(2,128)(2,1)S(1)} %get-tuple-element.53), channel_id=1, source_target_pairs={{1,0},{2,1},{3,2},{4,3},{5,4},{6,5},{7,6},{0,7},{9,8},{10,9},{11,1... | collective-permute-start | bytes 26120 | tf_op jit(solution)/shard_map/ppermute | solution.py:17
  77.0 5.0 %collective-permute-start.18 = (bf16[34,1,128]{2,1,0:T(2,128)(2,1)S(1)}, bf16[34,1,128]{2,1,0:T(2,128)(2,1)S(1)}, u32[]{:S(2)}, u32[]{:S(2)}) collective-permute-start(bf16[34,1,128]{2,1,0:T(2,128)(2,1)S(1)} %get-tuple-element.48), channel_id=1, source_target_pairs={{0,1},{1,2},{2,3},{3,4},{4,5},{5,6},{6,7},{7,0},{8,9},{9,10},{10,1... | collective-permute-start | bytes 26120 | tf_op jit(solution)/shard_map/ppermute | solution.py:16
  77.0 5.0 %collective-permute-start.19 = (bf16[34,1,128]{2,1,0:T(2,128)(2,1)S(1)}, bf16[34,1,128]{2,1,0:T(2,128)(2,1)S(1)}, u32[]{:S(2)}, u32[]{:S(2)}) collective-permute-start(bf16[34,1,128]{2,1,0:T(2,128)(2,1)S(1)} %get-tuple-element.49), channel_id=1, source_target_pairs={{1,0},{2,1},{3,2},{4,3},{5,4},{6,5},{7,6},{0,7},{9,8},{10,9},{11,1... | collective-permute-start | bytes 26120 | tf_op jit(solution)/shard_map/ppermute | solution.py:17
  104.1 1.2 copy-start.3
  148.8 1.8 copy-start.10
  150.6 1.2 copy-start.9
  151.8 1.2 copy-start.8
  153.0 1.2 copy-start.7
  154.3 1.2 copy-start.6
  155.5 1.2 copy-start.5
  156.7 1.2 copy-start.4
  158.4 126.9 %copy-start.1 = (bf16[73,128]{1,0:T(8,128)(2,1)S(1)}, bf16[73,128]{1,0:T(8,128)(2,1)}, u32[]{:S(2)}) copy-start(bf16[73,128]{1,0:T(8,128)(2,1)} %param.14) | copy-start | bytes 56068
Sparse Core Ops, SparseCore 0:
  148.9 132.4 all-reduce.2
where the time goes:
time: 293 us; the launch traced here: 292 us
  waiting for transfers between devices  125 us (43%)
  blocking collectives  39.3 us (13%)
  matrix products  35.5 us (12%)
  starting transfers between devices  33.7 us (12%)
  local copies, waits for them, and re-layouts  30.3 us (10%)
  between operations  14.6 us (5%)
  other arithmetic  14 us (5%)
    psum x1, waiting for transfers between devices, on_device(): totals = lax.psum((terms[0], terms[1], terms[2]), ('lat', 'lon'))  122 us
    psum x1, blocking collectives, on_device(): totals = lax.psum((terms[0], terms[1], terms[2]), ('lat', 'lon'))  39.3 us
    ppermute x10, starting transfers between devices, with_halo(): after = lax.ppermute(first, axis, down)  30.2 us
    unnamed x50, local copies, waits for them, and re-layouts  16.8 us
    dot_general x18, matrix products, weight_grads(): lax.dot_general(window, flat_delta, (((0,), (0,)), ((), ())), preferred_e...  14.3 us
    dot_general x18, matrix products, convolve(): jnp.dot(window, weight[tap_row, tap_col], preferred_element_type=jnp.floa...  8.78 us
    dot_general x18, matrix products, convolve_back(): jnp.dot(window, weight[tap_row, tap_col].T, preferred_element_type=jnp.fl...  7.74 us
    slice x2, local copies, waits for them, and re-layouts, convolve_back(): padded[2 - tap_row:2 - tap_row + span_rows, 2 - tap_col:2 - tap_col + spa...  7.71 us
  transfers between devices with their start and end apart: 21, of which 4 were waited for; matrix products, arithmetic and copies ran while one was open for 5% of the time, Pallas kernels for 0%

commit v1 on v0

v1 whole, which is shorter than its diff:
```python
import math

import jax
import jax.numpy as jnp
from jax import lax
from jax.experimental import pallas as pl
from jax.experimental.pallas import tpu as pltpu
from jax.sharding import PartitionSpec as P

F32 = jnp.float32
BF16 = jnp.bfloat16
LANES = 128
ROW_HALO = 3
COL_HALO = 4
SPAN = 16
GRAD_ROWS = 80
VMEM_BYTES = 36 * 1024 * 1024


def split_two(value):
    high = value.astype(BF16)
    return high, (value - high.astype(F32)).astype(BF16)


def prepare_kernel(
    cot_hbm, w2_hbm, w1_hbm, embed_hbm,
    shift_ref, back_ref, fore_ref, turned_ref, first_ref, cot_ref, w1_ref, padded_ref,
    w2_ref, embed_ref, line_ref, sems
):
    rows, cols, _ = cot_ref.shape
    wide = cols + 16
    pairs = rows // 2 + 1
    chunks = sems.shape[0] - 3
    share = rows // chunks
    weight_copy = pltpu.make_async_copy(w2_hbm, w2_ref, sems.at[chunks])
    weight_copy.start()
    copies = []
    for n in range(chunks):
        part = pl.ds(n * share, share)
        copies.append(pltpu.make_async_copy(cot_hbm.at[part], cot_ref.at[part], sems.at[n]))
        copies[-1].start()
    other_copy = pltpu.make_async_copy(w1_hbm, w1_ref, sems.at[chunks + 1])
    other_copy.start()
    embed_copy = pltpu.make_async_copy(embed_hbm, embed_ref, sems.at[chunks + 2])
    embed_copy.start()
    line_ref[...] = jnp.zeros_like(line_ref)
    back_ref[...] = jnp.zeros_like(back_ref)
    fore_ref[...] = jnp.zeros_like(fore_ref)
    blank = jnp.zeros((wide, LANES), BF16)
    for b in range(3):
        for parity in range(2):
            shift_ref[b, parity, 0:wide] = blank
            shift_ref[b, parity, pairs * wide : (pairs + 1) * wide] = blank
    weight_copy.wait()
    for a in range(3):
        for b in range(3):
            straight = w2_ref[a * 3 + b]
            turned = straight.astype(F32).T.astype(BF16)
            for q in range(2):
                column = slice(q * LANES, (q + 1) * LANES)
                at = (b * 4 + 2 + q - a) * LANES
                back_ref[at : at + LANES, column] = turned
                at = (b * 4 + a + q) * LANES
                fore_ref[at : at + LANES, column] = straight
    for r in range(rows):
        slot = r % 4
        if r % share == 0:
            copies[r // share].wait()
        line = cot_ref[r].astype(F32)
        line_ref[slot, 8 : 8 + cols] = line
        start = (r // 2 + 1) * wide
        for b in range(3):
            shift_ref[b, r % 2, start : start + wide] = line_ref[slot, 8 - b : 8 - b + wide].astype(BF16)
        turned_ref[(r % 2) * LANES : (r % 2 + 1) * LANES, (r // 2) * cols : (r // 2 + 1) * cols] = line.T.astype(BF16)
    embed_copy.wait()
    padded_ref[...] = padded_embed(embed_ref, line_ref)
    other_copy.wait()
    for tap in range(9):
        first_ref[tap * LANES : (tap + 1) * LANES] = w1_ref[tap].astype(F32).T.astype(BF16)


def edge_line(block, at):
    index = block[at : at + 1]
    return index, block[at + 1 : at + 2] + block[at + 2 : at + 3] + block[at + 3 : at + 4]


def row_spots(place_ref, rsrc_ref, rfrac_ref, before_ref, after_ref, rows, band_rows, lat_count):
    lat = place_ref[0]
    line_of = lax.broadcasted_iota(jnp.int32, (1, LANES), 1)

    def one_of(value, at):
        return jnp.sum(jnp.where(line_of == at, value, 0.0))

    before_line = edge_line(before_ref[ROW_HALO].astype(F32), 0)
    after_line = edge_line(after_ref[ROW_HALO].astype(F32), 0)
    spots = []
    for q in range(rows + 4):
        line_at = lat * rows + q - 2
        inside = jnp.logical_and(line_at >= 0, line_at < lat_count * rows)
        if q < 2:
            index, f = (one_of(v, rows - 2 + q) for v in before_line)
            index = index.astype(jnp.int32)
        elif q < rows + 2:
            index, f = rsrc_ref[0, q - 2], rfrac_ref[0, q - 2]
        else:
            index, f = (one_of(v, q - rows - 2) for v in after_line)
            index = index.astype(jnp.int32)
        j0 = jnp.clip(index - lat * band_rows + ROW_HALO, 0, band_rows + 2 * ROW_HALO - 2)
        spots.append((j0, jnp.where(inside, 1.0 - f, 0.0), jnp.where(inside, f, 0.0)))
    return spots


def blend_rows(cells_ref, spots):
    return jnp.concatenate(
        [w0 * cells_ref[j0] + w1 * cells_ref[j0 + 1] for j0, w0, w1 in spots], axis=0
    )


def lift_rows(mixed, embed):
    pair = jnp.concatenate(list(split_two(mixed)), axis=1)
    return jnp.dot(pair, jnp.concatenate([embed, embed], axis=0), preferred_element_type=F32)


def turned_rows(mixed, width):
    fill = jnp.zeros((width - mixed.shape[0], LANES), F32)
    turned = jnp.concatenate([mixed, fill], axis=0).T[:GRAD_ROWS]
    step = 2 * COL_HALO
    lines = [turned] + [pltpu.roll(turned, width - a * step, 1) for a in (1, 2)]
    return split_two(jnp.concatenate(lines, axis=0))


def tap_rows(lifted, w1_ref, cells):
    count = lifted.shape[0] - 2 * cells
    pairs = [split_two(lifted[a * cells : a * cells + count]) for a in range(3)]
    left = jnp.concatenate([p[0] for p in pairs] + [p[1] for p in pairs], axis=1)
    lines = [jnp.concatenate([w1_ref[a * 3 + b] for b in range(3)], axis=1) for a in range(3)]
    return jnp.dot(left, jnp.concatenate(lines + lines, axis=0), preferred_element_type=F32)


def blend_cols(src, frac, lon, band_cols, coarse_cols):
    shape = (SPAN, src.shape[1])
    local = jnp.broadcast_to(src, shape) - lon * band_cols
    frac = jnp.broadcast_to(frac, shape)
    local = jnp.where(local < -COL_HALO, local + coarse_cols, local)
    local = jnp.where(local >= band_cols + COL_HALO, local - coarse_cols, local)
    line = lax.broadcasted_iota(jnp.int32, shape, 0)

    def spot(at):
        east = jnp.where(at >= band_cols, at + COL_HALO, at)
        return jnp.where(at < 0, at + band_cols + COL_HALO, east)

    return jnp.where(line == spot(local), 1.0 - frac, 0.0) + jnp.where(
        line == spot(local + 1), frac, 0.0
    )


def back_kernel(
    place_ref,
    rsrc_ref,
    rfrac_ref,
    shift_ref,
    weight_ref,
    before_ref,
    own_ref,
    after_ref,
    csrc_ref,
    cfrac_ref,
    embed_ref,
    w1_ref,
    cot_ref,
    bh_ref,
    rows_ref,
    lifted_ref,
    tap_ref,
    cot_col_ref,
    cells_ref,
    *,
    lat_count,
    coarse_cols,
):
    rows, cols, _ = cot_ref.shape
    wide = bh_ref.shape[1]
    pairs = bh_ref.shape[0] // 2
    band_rows, band_cols = own_ref.shape[0] - 1, own_ref.shape[1]
    step = 6
    for first in range(0, pairs, step):
        count = min(step, pairs - first)
        blocks = []
        for b in range(3):
            for i in range(4):
                start = (first + i // 2) * wide
                blocks.append(shift_ref[b, i % 2, start : start + count * wide])
        out = jnp.dot(jnp.concatenate(blocks, axis=1), weight_ref[...], preferred_element_type=F32)
        for m in range(count):
            for q in range(2):
                bh_ref[2 * (first + m) + q] = out[m * wide : (m + 1) * wide, q * LANES : (q + 1) * LANES]

    for j in range(cells_ref.shape[0]):
        if j < ROW_HALO:
            middle = before_ref[j]
        elif j < ROW_HALO + band_rows:
            middle = own_ref[j - ROW_HALO]
        else:
            middle = after_ref[j - ROW_HALO - band_rows]
        cells_ref[j] = middle.astype(F32)
    spots = row_spots(place_ref, rsrc_ref, rfrac_ref, before_ref, after_ref, rows, band_rows, lat_count)
    mixed = blend_rows(cells_ref, spots)
    rows_ref[0], rows_ref[1] = turned_rows(mixed, rows_ref.shape[2])
    lifted = lift_rows(mixed, embed_ref[...])
    lifted_ref[...] = lifted
    tap_ref[...] = tap_rows(lifted, w1_ref, band_cols)

    blend = blend_cols(csrc_ref[...], cfrac_ref[...], place_ref[1], band_cols, coarse_cols)
    own_t = jnp.concatenate(list(split_two(blend)), axis=0)
    every = jnp.concatenate([cot_ref[r] for r in range(rows)], axis=1)
    back = jnp.dot(own_t, every, preferred_element_type=F32)
    back = back[:SPAN] + back[SPAN:]
    for r in range(rows):
        cot_col_ref[r] = back[:, r * LANES : (r + 1) * LANES]


def pack_kernel(cells_hbm, rsrc_hbm, rfrac_hbm, csrc_hbm, cfrac_hbm, out_ref, *space):
    sources = (cells_hbm, rsrc_hbm, rfrac_hbm, csrc_hbm, cfrac_hbm)
    *lines, cells_ref, sems = space
    targets = (cells_ref, *lines)
    copies = [
        pltpu.make_async_copy(source, target, sems.at[n])
        for n, (source, target) in enumerate(zip(sources, targets))
    ]
    for copy in copies:
        copy.start()
    cells_ref, rsrc_ref, rfrac_ref, csrc_ref, cfrac_ref = targets
    depth, span, fields = cells_ref.shape
    out_ref[...] = jnp.zeros_like(out_ref)
    for copy in copies:
        copy.wait()
    for j in range(depth):
        out_ref[j, :, :fields] = cells_ref[j].astype(F32)
    at = 0
    for index_ref, fraction_ref in ((rsrc_ref, rfrac_ref), (csrc_ref, cfrac_ref)):
        width = index_ref.shape[1]
        fraction = fraction_ref[...]
        one = fraction.astype(BF16).astype(F32)
        two = (fraction - one).astype(BF16).astype(F32)
        for value in (index_ref[...].astype(F32), one, two, fraction - one - two):
            out_ref[depth, at : at + 1, :width] = value
            at += 1


def main_kernel(
    place_ref,
    rsrc_ref,
    rfrac_ref,
    before_ref,
    after_ref,
    west_ref,
    east_ref,
    csrc_ref,
    cfrac_ref,
    embed_ref,
    w1_ref,
    turned_ref,
    bh_ref,
    rows_ref,
    lifted_ref,
    tap_ref,
    cot_col_ref,
    hid_ref,
    lift_ref,
    msg_ref,
    cells_ref,
    side_tap_ref,
    line_ref,
    right_ref,
    lift_right_ref,
    delta_ref,
    back_ref,
    *,
    lat_count,
    coarse_cols,
    band_rows,
    band_cols,
):
    rows, cols, _ = lift_ref.shape
    wide = bh_ref.shape[1]
    pairs = bh_ref.shape[0] // 2
    depth = cells_ref.shape[0]
    half_rows = msg_ref.shape[1]
    lat = place_ref[0]
    lon = place_ref[1]
    core = place_ref[2]
    taps = 3 * SPAN

    def send(at, value):
        side = lax.rem(at // half_rows + core, 2)
        at = at % half_rows
        msg_ref[side, at : at + value.shape[0]] = value.astype(BF16)

    for j in range(depth):
        cells_ref[j, :COL_HALO] = west_ref[j].astype(F32)
        cells_ref[j, COL_HALO:] = east_ref[j].astype(F32)
    spots = row_spots(place_ref, rsrc_ref, rfrac_ref, before_ref, after_ref, rows, band_rows, lat_count)
    side_mixed = blend_rows(cells_ref, spots)
    side_lifted = lift_rows(side_mixed, embed_ref[...])
    side_tap_ref[...] = tap_rows(side_lifted, w1_ref, band_cols)

    lane_count = 2 * LANES
    lane = lax.broadcasted_iota(jnp.int32, (1, lane_count), 1)
    west_line = edge_line(jnp.concatenate([west_ref[j] for j in (depth, depth + 1)], axis=0).astype(F32), 4)
    east_line = edge_line(jnp.concatenate([east_ref[j] for j in (depth, depth + 1)], axis=0).astype(F32), 4)
    own_line = (csrc_ref[...].astype(F32), cfrac_ref[...])
    blank = jnp.zeros((1, lane_count - cols), F32)
    lines = []
    for parts in zip(west_line, own_line, east_line):
        out = []
        for part, shift in zip(parts, (lane_count - cols + 2, 2, cols + 2)):
            part = jnp.concatenate([part, blank], axis=1)
            out.append(pltpu.roll(jnp.broadcast_to(part, (8, lane_count)), shift, 1)[:1])
        lines.append(jnp.where(lane < 2, out[0], jnp.where(lane < cols + 2, out[1], out[2])))
    known = lane < cols + 4
    src = jnp.where(known, lines[0], -1e6).astype(jnp.int32)
    blend = blend_cols(src, jnp.where(known, lines[1], 0.0), lon, band_cols, coarse_cols)
    rolled = [blend] + [pltpu.roll(blend, lane_count - b, 1) for b in (1, 2)]
    stack = jnp.concatenate(rolled, axis=0)[:, :wide]
    high, low = split_two(stack)
    high_f, low_f = high.astype(F32), low.astype(F32)
    col_t = jnp.concatenate([high_f, low_f], axis=0).astype(BF16)
    col_lhs = jnp.concatenate([high_f.T, low_f.T, high_f.T], axis=1).astype(BF16)
    own_hi, own_lo = split_two(rolled[2][:, :cols])
    own_hi, own_lo = own_hi.astype(F32).T, own_lo.astype(F32).T
    own_lhs = jnp.concatenate([own_hi, own_lo, own_hi], axis=1).astype(BF16)

    def stacked(value):
        one, two = split_two(value)
        return jnp.concatenate([one, one, two], axis=0)

    for t in range(2 * pairs):
        part = slice(t * band_cols, (t + 1) * band_cols)
        blocks = []
        for b in range(3):
            column = slice(b * LANES, (b + 1) * LANES)
            blocks += [tap_ref[part, column], side_tap_ref[part, column]]
        right_ref[:, t * LANES : (t + 1) * LANES] = stacked(jnp.concatenate(blocks, axis=0))
    for r in range(rows):
        part = slice((r + 2) * band_cols, (r + 3) * band_cols)
        lift_right_ref[:, r * LANES : (r + 1) * LANES] = stacked(
            jnp.concatenate([lifted_ref[part], side_lifted[part]], axis=0)
        )
    pre = jnp.dot(col_lhs, right_ref[...], preferred_element_type=F32)
    for t in range(2 * pairs):
        v = pre[:, t * LANES : (t + 1) * LANES]
        s = 0.5 + 0.5 * jnp.tanh(0.5 * v)
        if t == 0:
            s = s * jnp.where(lat > 0, 1.0, 0.0)
        elif t == 2 * pairs - 1:
            s = s * jnp.where(lat < lat_count - 1, 1.0, 0.0)
        h = v * s
        slope = s + h * (1.0 - s)
        line_ref[t] = h
        delta_ref[:, t * LANES : (t + 1) * LANES] = (bh_ref[t] * slope).astype(BF16)
    for t in range(2 * pairs):
        for b in range(3):
            at = (t // 2) * cols
            hid_ref[b, t % 2, at : at + cols] = line_ref[t, b : b + cols].astype(BF16)
    own = jnp.dot(own_lhs, lift_right_ref[...], preferred_element_type=F32)
    for r in range(rows):
        lift_ref[r] = own[:, r * LANES : (r + 1) * LANES]

    back = jnp.dot(col_t, delta_ref[...], preferred_element_type=F32)
    back = back[:taps] + back[taps:]
    width = rows_ref.shape[2]
    used = 2 * pairs * band_cols
    blank = jnp.zeros((2, width - used, back_ref.shape[2]), BF16)
    back_ref[:, used:width] = blank
    back_ref[:, width + used :] = blank
    nothing = jnp.zeros((SPAN, LANES), F32)
    for p in range(pairs):
        for b in range(4):
            lines = []
            for t in (2 * p, 2 * p + 1):
                if b < 3:
                    lines.append(back[b * SPAN : (b + 1) * SPAN, t * LANES : (t + 1) * LANES])
                else:
                    lines.append(cot_col_ref[t - 1] if 1 <= t <= rows else nothing)
            column = slice(b * LANES, (b + 1) * LANES)
            for side in range(2):
                cells = slice(side * band_cols, (side + 1) * band_cols)
                one, two = split_two(jnp.concatenate([v[cells] for v in lines], axis=0))
                at = side * width + p * SPAN
                back_ref[0, at : at + SPAN, column] = one
                back_ref[1, at : at + SPAN, column] = two
    side_hi, side_lo = turned_rows(side_mixed, width)
    upper = jnp.concatenate([rows_ref[0], side_hi], axis=1)
    lower = jnp.concatenate([rows_ref[1], side_lo], axis=1)
    g = jnp.dot(jnp.concatenate([upper, lower], axis=0), back_ref[0], preferred_element_type=F32)
    g = g[: 3 * GRAD_ROWS] + g[3 * GRAD_ROWS :]
    g = g + jnp.dot(upper, back_ref[1], preferred_element_type=F32)
    for a in range(3):
        line = g[a * GRAD_ROWS : (a + 1) * GRAD_ROWS]
        for b in range(3):
            send(9 * LANES + (a * 3 + b) * GRAD_ROWS, line[:, b * LANES : (b + 1) * LANES])
    send(9 * LANES + 9 * GRAD_ROWS, g[GRAD_ROWS : 2 * GRAD_ROWS, 3 * LANES:])
    tail = 9 * LANES + 10 * GRAD_ROWS
    if 2 * half_rows > tail:
        send(tail, jnp.zeros((2 * half_rows - tail, LANES), F32))

    half = (rows // 2) * cols
    left_t = turned_ref[...]
    for b in range(3):
        right = jnp.concatenate(
            [hid_ref[b, i % 2, (i // 2) * cols : (i // 2) * cols + half] for i in range(4)], axis=1
        )
        out = jnp.dot(left_t, right, preferred_element_type=F32)
        for a in range(3):
            upper = out[:LANES, a * LANES : (a + 1) * LANES]
            lower = out[LANES:, (a + 1) * LANES : (a + 2) * LANES]
            tap = a * 3 + b
            send(tap * LANES, (upper + lower).T)


def features_kernel(weight_ref, hid_ref, lift_ref, *refs, first, last):
    out_hbm, feat_ref, sems = refs[-3:]
    cols = feat_ref.shape[1]
    step = (last - first) // sems.shape[0]
    copies = []
    for n in range(sems.shape[0]):
        top = first + n * step
        blocks = []
        for b in range(3):
            for i in range(4):
                start = (top + i // 2) * cols
                blocks.append(hid_ref[b, i % 2, start : start + step * cols])
        out = jnp.dot(jnp.concatenate(blocks, axis=1), weight_ref[...], preferred_element_type=F32)
        for m in range(step):
            for q in range(2):
                piece = out[m * cols : (m + 1) * cols, q * LANES : (q + 1) * LANES]
                r = 2 * (top + m) + q
                feat_ref[r - 2 * first] = (lift_ref[r] + piece).astype(BF16)
        part = feat_ref.at[pl.ds(2 * n * step, 2 * step)]
        copies.append(pltpu.make_async_copy(part, out_hbm.at[pl.ds(2 * top, 2 * step)], sems.at[n]))
        copies[-1].start()
    for copy in copies:
        copy.wait()


def reduce_kernel(in_ref, out_ref):
    total = in_ref[0].astype(F32)
    for d in range(1, in_ref.shape[0]):
        total = total + in_ref[d].astype(F32)
    total = total.astype(BF16)
    for d in range(out_ref.shape[0]):
        out_ref[d] = total


def padded_embed(embed_ref, space_ref):
    fields = embed_ref.shape[0]
    space_ref[0, :LANES] = jnp.zeros((LANES, LANES), F32)
    space_ref[0, :fields] = embed_ref[...].astype(F32)
    return space_ref[0, :LANES].astype(BF16)


def last_kernel(
    place_ref, mine_ref, other_ref, embed_ref, first_ref, ge_hbm, g1_hbm, g2_hbm,
    sum_ref, ge_ref, g1_ref, g2_ref, sems, *, scale
):
    core = place_ref[2]
    half_rows = mine_ref.shape[0]
    sum_ref[core] = mine_ref[...]
    sum_ref[1 - core] = other_ref[...]

    def read(at, count):
        return sum_ref[at // half_rows, at % half_rows : at % half_rows + count]

    copies = []

    def leave(source, target):
        copies.append(pltpu.make_async_copy(source, target, sems.at[len(copies)]))
        copies[-1].start()

    for a in range(3):
        for tap in range(3 * a, 3 * a + 3):
            g2_ref[tap] = read(tap * LANES, LANES).astype(F32) * scale
        leave(g2_ref.at[pl.ds(3 * a, 3)], g2_hbm.at[pl.ds(3 * a, 3)])
    embed_t = embed_ref[...].astype(F32).T.astype(BF16)[:, :GRAD_ROWS]
    base = 9 * LANES
    g = jnp.concatenate([read(base + tap * GRAD_ROWS, GRAD_ROWS) for tap in range(9)], axis=1)
    for a in range(3):
        part = g[:, 3 * a * LANES : (3 * a + 3) * LANES]
        out = jnp.dot(embed_t, part, preferred_element_type=F32) * scale
        for b in range(3):
            g1_ref[3 * a + b] = out[:, b * LANES : (b + 1) * LANES]
        leave(g1_ref.at[pl.ds(3 * a, 3)], g1_hbm.at[pl.ds(3 * a, 3)])
    lift = read(base + 9 * GRAD_ROWS, GRAD_ROWS).astype(F32)
    lift = lift + jnp.dot(g, first_ref[...], preferred_element_type=F32)
    ge_ref[...] = lift[: ge_ref.shape[0]] * scale
    leave(ge_ref, ge_hbm)
    for copy in copies:
        copy.wait()


def from_hbm(value):
    return pltpu.with_memory_space_constraint(value, pltpu.HBM)


def on_device(
    coarse,
    row_src,
    row_frac,
    col_src,
    col_frac,
    embed_weight,
    conv1_weight,
    conv2_weight,
    cotangent,
):
    lat_count = lax.axis_size("lat")
    ring_count = lax.axis_size("ring")
    core_count = lax.axis_size("core")
    lon_count = ring_count * core_count
    lat_place = lax.axis_index("lat")
    core_place = lax.axis_index("core")
    lon_place = lax.axis_index("ring") * core_count + core_place
    fields, band_rows, band_cols = coarse.shape
    rows, cols, hidden = cotangent.shape
    group = lat_count * ring_count
    wide = cols + 16
    pairs = rows // 2 + 1
    depth = band_rows + 2 * ROW_HALO
    params = pltpu.CompilerParams(vmem_limit_bytes=VMEM_BYTES)
    vmem = pl.BlockSpec(memory_space=pltpu.VMEM)
    smem = pl.BlockSpec(memory_space=pltpu.SMEM)
    far = pl.BlockSpec(memory_space=pltpu.HBM)

    w1 = conv1_weight.reshape(9, hidden, hidden)
    w2 = conv2_weight.reshape(9, hidden, hidden)
    place = jnp.stack([lat_place, lon_place, core_place]).astype(jnp.int32)
    row_line = (row_src.reshape(1, rows), row_frac.reshape(1, rows))
    col_line = (col_src.reshape(1, cols), col_frac.reshape(1, cols))

    pack_inputs = (
        jnp.transpose(coarse, (1, 2, 0)),
        *row_line,
        *col_line,
    )
    own, *lines = pl.pallas_call(
        pack_kernel,
        in_specs=[far] * 5,
        out_shape=[jax.ShapeDtypeStruct((band_rows + 1, band_cols, LANES), F32)]
        + [jax.ShapeDtypeStruct(x.shape, x.dtype) for x in pack_inputs[1:]],
        scratch_shapes=[
            pltpu.VMEM(pack_inputs[0].shape, BF16),
            pltpu.SemaphoreType.DMA((5,)),
        ],
        compiler_params=params,
        name="pack",
    )(*(from_hbm(x) for x in pack_inputs))
    own = own.astype(BF16)
    row_line, col_line = lines[:2], lines[2:]
    edge = own[band_rows:]
    to_next = own[band_rows - ROW_HALO :]
    to_last = jnp.concatenate([own[:ROW_HALO], edge])
    even = lat_place % 2 == 0
    inner = [(i, i ^ 1) for i in range(lat_count)]
    outer = [(i, i + 1) for i in range(1, lat_count - 1, 2)]
    outer = outer + [(j, i) for i, j in outer]
    got_outer = lax.ppermute(jnp.where(even, to_last, to_next), "lat", outer)
    got_inner = lax.ppermute(jnp.where(even, to_next, to_last), "lat", inner)
    before, after = got_outer, got_inner

    shift, back_weight, fore_weight, turned, first_weight, cot, near_w1, embed = pl.pallas_call(
        prepare_kernel,
        out_shape=[
            jax.ShapeDtypeStruct((3, 2, (pairs + 1) * wide, hidden), BF16),
            jax.ShapeDtypeStruct((12 * hidden, 2 * hidden), BF16),
            jax.ShapeDtypeStruct((12 * hidden, 2 * hidden), BF16),
            jax.ShapeDtypeStruct((2 * hidden, rows // 2 * cols), BF16),
            jax.ShapeDtypeStruct((9 * hidden, hidden), BF16),
            jax.ShapeDtypeStruct((rows, cols, hidden), BF16),
            jax.ShapeDtypeStruct((9, hidden, hidden), BF16),
            jax.ShapeDtypeStruct((LANES, hidden), BF16),
        ],
        in_specs=[far] * 4,
        scratch_shapes=[
            pltpu.VMEM((9, hidden, hidden), BF16),
            pltpu.VMEM((fields, hidden), BF16),
            pltpu.VMEM((4, wide + 16, hidden), F32),
            pltpu.SemaphoreType.DMA((11,)),
        ],
        compiler_params=params,
        name="prepare",
    )(from_hbm(cotangent), from_hbm(w2), from_hbm(w1), from_hbm(embed_weight))
    before, after, shift, back_weight = lax.optimization_barrier((before, after, shift, back_weight))
    before, after = jnp.where(even, before, after), jnp.where(even, after, before)

    def back_body(*refs):
        back_kernel(*refs, lat_count=lat_count, coarse_cols=band_cols * lon_count)

    reach = rows + 4
    width = -(-reach * band_cols // LANES) * LANES
    bh, mixed, lifted, tap, cot_col = pl.pallas_call(
        back_body,
        in_specs=[smem] * 3 + [vmem] * 10,
        out_shape=[
            jax.ShapeDtypeStruct((2 * pairs, wide, hidden), F32),
            jax.ShapeDtypeStruct((2, 3 * GRAD_ROWS, width), BF16),
            jax.ShapeDtypeStruct((reach * band_cols, hidden), F32),
            jax.ShapeDtypeStruct(((reach - 2) * band_cols, 3 * hidden), F32),
            jax.ShapeDtypeStruct((rows, SPAN, hidden), F32),
        ],
        scratch_shapes=[
            pltpu.VMEM((depth, band_cols, LANES), F32),
        ],
        compiler_params=params,
        name="back_hidden",
    )(
        place, *row_line, shift, back_weight, before, own, after, *col_line,
        embed, near_w1, cot,
    )

    tall = jnp.concatenate([before[:ROW_HALO], own[:band_rows], after[:ROW_HALO]])
    lines = edge.reshape(band_cols // COL_HALO, COL_HALO, LANES)
    lon = ("ring", "core")
    to_next = jnp.concatenate([tall[:, band_cols - COL_HALO :], lines])
    to_last = jnp.concatenate([tall[:, :COL_HALO], lines])
    first = core_place == 0
    inner = [(i, i ^ 1) for i in range(lon_count)]
    outer = [(i, (i + (1 if i % 2 else -1)) % lon_count) for i in range(lon_count)]
    got_outer = lax.ppermute(jnp.where(first, to_last, to_next), lon, outer)
    got_inner = lax.ppermute(jnp.where(first, to_next, to_last), lon, inner)
    west = jnp.where(first, got_outer, got_inner)
    east = jnp.where(first, got_inner, got_outer)

    blocks = 9 * LANES + 10 * GRAD_ROWS
    chunk = -(-blocks // (core_count * group * 16)) * 16
    half_rows = max(group * chunk, -(-blocks // (2 * LANES)) * LANES)

    def body(*refs):
        main_kernel(
            *refs,
            lat_count=lat_count,
            coarse_cols=band_cols * lon_count,
            band_rows=band_rows,
            band_cols=band_cols,
        )

    hid, lift, message = pl.pallas_call(
        body,
        in_specs=[smem] * 3 + [vmem] * 14,
        out_specs=[vmem] * 3,
        out_shape=[
            jax.ShapeDtypeStruct((3, 2, pairs * cols, hidden), BF16),
            jax.ShapeDtypeStruct((rows, cols, hidden), F32),
            jax.ShapeDtypeStruct((2, half_rows, LANES), BF16),
        ],
        scratch_shapes=[
            pltpu.VMEM((depth, 2 * COL_HALO, LANES), F32),
            pltpu.VMEM(((reach - 2) * band_cols, 3 * hidden), F32),
            pltpu.VMEM((2 * pairs, wide, hidden), F32),
            pltpu.VMEM((9 * SPAN, 2 * pairs * hidden), BF16),
            pltpu.VMEM((3 * SPAN, rows * hidden), BF16),
            pltpu.VMEM((wide, 2 * pairs * hidden), BF16),
            pltpu.VMEM((2, 2 * width, 4 * hidden), BF16),
        ],
        compiler_params=params,
        name="tile",
    )(
        place, *row_line, before, after, west, east, *col_line,
        embed, near_w1, turned, bh, mixed, lifted, tap, cot_col,
    )

    def half_features(first, last, *arrays):
        def body(*refs):
            features_kernel(*refs, first=first, last=last)

        return pl.pallas_call(
            body,
            in_specs=[vmem] * 3 + [far] * (len(arrays) - 3),
            out_specs=far,
            out_shape=jax.ShapeDtypeStruct((rows, cols, hidden), BF16),
            input_output_aliases={n: 0 for n in range(3, len(arrays))},
            scratch_shapes=[
                pltpu.VMEM((2 * (last - first), cols, hidden), BF16),
                pltpu.SemaphoreType.DMA((2,)),
            ],
            compiler_params=params,
            name=f"features_{first}",
        )(*arrays)

    swap = [(0, 1), (1, 0)]
    received = lax.ppermute(message[1], "core", swap)
    middle = rows // 4
    part = half_features(0, middle, fore_weight, hid, lift)
    received, part = lax.optimization_barrier((received, part))
    pair = (message[0].astype(F32) + received.astype(F32)).astype(BF16)
    axes = ("lat", "ring")
    chunk = half_rows // group
    parts = lax.all_to_all(pair, axes, 0, 0, tiled=True)
    copies = pl.pallas_call(
        reduce_kernel,
        out_shape=jax.ShapeDtypeStruct((group, chunk, LANES), BF16),
        compiler_params=params,
        name="sum_chunks",
    )(parts.reshape(group, chunk, LANES))
    mine = lax.all_to_all(copies.reshape(half_rows, LANES), axes, 0, 0, tiled=True)
    other = lax.ppermute(mine, "core", swap)
    _, part = lax.optimization_barrier((mine, part))
    features = half_features(middle, rows // 2, fore_weight, hid, lift, part)
    scale = 1.0 / math.sqrt(rows * lat_count * cols * lon_count)

    def finish(*refs):
        last_kernel(*refs, scale=scale)

    grad_embed, grad_first, grad_second = pl.pallas_call(
        finish,
        in_specs=[smem] + [vmem] * 4,
        out_specs=[far] * 3,
        out_shape=[
            jax.ShapeDtypeStruct((fields, hidden), F32),
            jax.ShapeDtypeStruct((9, hidden, hidden), F32),
            jax.ShapeDtypeStruct((9, hidden, hidden), F32),
        ],
        scratch_shapes=[
            pltpu.VMEM((2, half_rows, LANES), BF16),
            pltpu.VMEM((fields, hidden), F32),
            pltpu.VMEM((9, hidden, hidden), F32),
            pltpu.VMEM((9, hidden, hidden), F32),
            pltpu.SemaphoreType.DMA((7,)),
        ],
        compiler_params=params,
        name="finish",
    )(place, mine, other, embed, first_weight)
    shape = (3, 3, hidden, hidden)
    return (features, grad_embed, grad_first.reshape(shape), grad_second.reshape(shape))


def solution(mesh):
    lat_count, lon_count = mesh.devices.shape
    inner = jax.sharding.Mesh(
        mesh.devices.reshape(lat_count, lon_count // 2, 2), ("lat", "ring", "core")
    )
    lon = ("ring", "core")
    in_specs = (
        P(None, "lat", lon),
        P("lat"),
        P("lat"),
        P(lon),
        P(lon),
        P(),
        P(),
        P(),
        P("lat", lon, None),
    )
    out_specs = (P("lat", lon, None), P(), P(), P())
    return jax.shard_map(
        on_device, mesh=inner, in_specs=in_specs, out_specs=out_specs, check_vma=False
    )
```

time: 293 us -> 57 us (0.19)
  waiting for transfers between devices: 125 us -> 0.02 us
  matrix products: 35.5 us -> 0 us
  local copies, waits for them, and re-layouts: 30.3 us -> 0.04 us
  starting transfers between devices: 33.7 us -> 7.5 us
  Pallas kernels: 0 us -> 17 us
  other arithmetic: 14 us -> 0.21 us
  between operations: 14.6 us -> 0.88 us
  blocking collectives: 39.3 us -> 31 us
    psum x1 -> x0, waiting for transfers between devices: 122 us -> none  [on_device(): totals = lax.psum((terms[0], terms[1], terms[2]), ('lat', 'lon'))]
    psum x1 -> x0, blocking collectives: 39.3 us -> none  [on_device(): totals = lax.psum((terms[0], terms[1], terms[2]), ('lat', 'lon'))]
    dot_general x58 -> x0, matrix products: 35.5 us -> none  [the longest x18 14.3 us: weight_grads(): lax.dot_general(window, flat_delta, (((0,), (0,)), ((), ())), preferred_e...]
    all_to_all x0 -> x2, blocking collectives: none -> 31 us  [the longest x1 18.2 us: on_device(): parts = lax.all_to_all(pair, axes, 0, 0, tiled=True)]
    ppermute x20 -> x6, starting transfers between devices: 33.7 us -> 7.5 us  [the longest x1 3.7 us: on_device(): got_outer = lax.ppermute(jnp.where(first, to_last, to_next), lon, outer)]
    pallas_call x0 -> x8, Pallas kernels: none -> 17 us  [the longest x1 5.24 us: on_device(): pl.pallas_call(body, in_specs=[smem] * 3 + [vmem] * 14, out_specs=[vmem]...]
    unnamed x50 -> x0, local copies, waits for them, and re-layouts: 16.8 us -> none
    slice x10 -> x5, local copies, waits for them, and re-layouts: 13.1 us -> 0.02 us  [the longest x1 0.01 us: on_device(): to_next = jnp.concatenate([tall[:, band_cols - COL_HALO:], lines])]
  transfers between devices with their start and end apart: 21 -> 6, of which waited for: 4 -> 0; matrix products, arithmetic and copies ran while one was open for 5% -> 0% of each run, Pallas kernels for 0% -> 16%
where the time goes in v1:
time: 57 us; the launch traced here: 56.7 us
  blocking collectives  31 us (54%)
  Pallas kernels  17 us (30%)
  starting transfers between devices  7.5 us (13%)
  between operations  0.88 us (2%)
    all_to_all x1, blocking collectives, on_device(): parts = lax.all_to_all(pair, axes, 0, 0, tiled=True)  18.2 us
    all_to_all x1, blocking collectives, on_device(): lax.all_to_all(copies.reshape(half_rows, LANES), axes, 0, 0, tiled=True)  12.8 us
    pallas_call x1, Pallas kernels, on_device(): pl.pallas_call(body, in_specs=[smem] * 3 + [vmem] * 14, out_specs=[vmem]...  5.24 us
    ppermute x1, starting transfers between devices, on_device(): got_outer = lax.ppermute(jnp.where(first, to_last, to_next), lon, outer)  3.7 us
    pallas_call x2, Pallas kernels, half_features(): pl.pallas_call(body, in_specs=[vmem] * 3 + [far] * (len(arrays) - 3), out...  3.57 us
    pallas_call x1, Pallas kernels, on_device(): pl.pallas_call(back_body, in_specs=[smem] * 3 + [vmem] * 10, out_shape=[j...  3.13 us
    ppermute x1, starting transfers between devices, on_device(): got_inner = lax.ppermute(jnp.where(even, to_next, to_last), 'lat', inner)  3 us
    pallas_call x1, Pallas kernels, on_device(): pl.pallas_call(prepare_kernel, out_shape=[jax.ShapeDtypeStruct((3, 2, (pa...  2.45 us
  transfers between devices with their start and end apart: 6, of which 0 were waited for; matrix products, arithmetic and copies ran while one was open for 0% of the time, Pallas kernels for 16%

profile of v1, /device:TPU:0, one launch (start us, length us, event | category | flops | bytes accessed | tf_op | source)
XLA Modules:
  0.0 56.7 jit_solution(16841390729924110851)
XLA Ops:
  0.6 0.8 %pack.1 = (f32[5,8,128]{2,1,0:T(8,128)S(1)}, s32[1,32]{1,0:T(1,128)S(1)}, f32[1,32]{1,0:T(1,128)S(1)}, s32[1,128]{1,0:T(1,128)S(1)}, f32[1,128]{1,0:T(1,128)S(1)}) custom-call(bf16[4,8,73]{2,1,0:T(8,128)(2,1)} %bitcast.34, s32[1,32]{1,0:T(1,128)} %bitcast.35, f32[1,32]{1,0:T(1,128)} %bitcast.36, s32[1,128]{1,0:T(1,128)} %bitcast.37, f32[1,128]{1,0:T(1,128)} %bitcast.38), custom_call_target="tpu_custom_call" | custom-call | tf_op jit(solution)/shard_map/pack/pallas_call | solution.py:545
  1.5 3.0 %collective-permute-start.1 = (bf16[4,8,128]{2,1,0:T(8,128)(2,1)S(1)}, bf16[4,8,128]{2,1,0:T(8,128)(2,1)S(1)}, u32[]{:S(2)}, u32[]{:S(2)}) collective-permute-start(bf16[4,8,128]{2,1,0:T(8,128)(2,1)S(1)} %get-tuple-element.72), channel_id=1, source_target_pairs={{0,8},{8,0},{16,24},{24,16},{1,9},{9,1},{17,25},{25,17},{2,10},{10... | collective-permute-start | bytes 24584 | tf_op jit(solution)/shard_map/ppermute | solution.py:567
  4.5 0.6 %collective-permute-start = (bf16[4,8,128]{2,1,0:T(8,128)(2,1)S(1)}, bf16[4,8,128]{2,1,0:T(8,128)(2,1)S(1)}, u32[]{:S(2)}, u32[]{:S(2)}) collective-permute-start(bf16[4,8,128]{2,1,0:T(8,128)(2,1)S(1)} %get-tuple-element.73), channel_id=1, source_target_pairs={{8,16},{16,8},{9,17},{17,9},{10,18},{18,10},{11,19},{19,11},{12,20... | collective-permute-start | bytes 24584 | tf_op jit(solution)/shard_map/ppermute | solution.py:566
  5.2 2.4 %prepare.1 = (bf16[3,2,2592,128]{3,2,1,0:T(8,128)(2,1)S(1)}, bf16[1536,256]{1,0:T(8,128)(2,1)S(1)}, bf16[1536,256]{1,0:T(8,128)(2,1)S(1)}, bf16[256,2048]{1,0:T(...) custom-call(bf16[32,128,128]{2,1,0:T(8,128)(2,1)} %cot_hbm.1, ...), custom_call_target="tpu_custom_call" | custom-call | tf_op jit(solution)/shard_map/prepare/pallas_call | solution.py:570
  7.6 0.0 collective-permute-done.1
  7.6 0.0 collective-permute-done
  7.7 0.1 collective-permute-start.3
  7.8 3.7 %collective-permute-start.2 = (bf16[12,4,128]{2,1,0:T(4,128)(2,1)S(1)}, bf16[12,4,128]{2,1,0:T(4,128)(2,1)S(1)}, u32[]{:S(2)}, u32[]{:S(2)}) collective-permute-start(bf16[12,4,128]{2,1,0:T(4,128)(2,1)S(1)} %get-tuple-element.69), channel_id=1, source_target_pairs={{0,7},{1,2},{2,1},{3,4},{4,3},{5,6},{6,5},{7,0},{8,15},{9,10},{10,... | collective-permute-start | bytes 36872 | tf_op jit(solution)/shard_map/ppermute | solution.py:628
  11.5 0.1 pad_add_fusion.refs_0_
  11.6 3.1 %back_hidden.1 = (f32[34,144,128]{2,1,0:T(8,128)S(1)}, bf16[2,240,384]{2,1,0:T(8,128)(2,1)S(1)}, f32[288,128]{1,0:T(8,128)S(1)}, f32[272,384]{1,0:T(8,128)S(1)}, f32[32,16,128]{2,1,0:T(8,128)S(1)}) custom-call(s32[3]{0:T(128)S(1)} %pad_add_fusion.refs_0_, s32[1,32]{1,0:T(1,128)S(1)} %get-tuple-element.36.refs_1_, f32[1,32]{1,0:T(1,128)S(1)} %get-tuple-element.37.refs_2_, ...), custom_call_target="tpu_custom_call" | custom-call | tf_op jit(solution)/shard_map/back_hidden/pallas_call | solution.py:600
  14.7 0.0 collective-permute-done.3
  14.7 0.0 collective-permute-done.2
  14.7 5.2 %tile.1 = (bf16[3,2,2176,128]{3,2,1,0:T(8,128)(2,1)S(1)}, f32[32,128,128]{2,1,0:T(8,128)S(1)}, bf16[2,1024,128]{2,1,0:T(8,128)(2,1)S(1)}) custom-call(s32[3]{0:T(128)S(1)} %pad_add_fusion.refs_0_, s32[1,32]{1,0:T(1,128)S(1)} %get-tuple-element.36.refs_1_, f32[1,32]{1,0:T(1,128)S(1)} %get-tuple-element.37.refs_2_, ...), custom_call_target="tpu_custom_call" | custom-call | tf_op jit(solution)/shard_map/tile/pallas_call | solution.py:646
  20.0 0.1 collective-permute-start.4
  20.1 1.8 %features_0.1.refs_3_ = bf16[32,128,128]{2,1,0:T(8,128)(2,1)} custom-call(bf16[1536,256]{1,0:T(8,128)(2,1)S(1)} %get-tuple-element.35.refs_0_, bf16[3,2,2176,128]{3,2,1,0:T(8,128)(2,1)S(1)} %get-tuple-element.56.refs_1_, f32[32,128,128]{2,1,0:T(8,128)S(1)} %get-tuple-element.57.refs_2_), custom_call_target="tpu_custom_call" | custom-call | tf_op jit(solution)/shard_map/features_0/pallas_call | solution.py:675
  21.9 0.0 collective-permute-done.4
  21.9 0.1 fusion
  22.0 18.2 %all_to_all.17.in_ref = bf16[16,64,128]{2,1,0:T(8,128)(2,1)S(1)} all-to-all(bf16[16,64,128]{2,1,0:T(8,128)(2,1)S(1)} %bitcast.28), channel_id=1, replica_groups=mesh['lat'=4,'ring'=4,'core'=2] {'lat','ring'}, dimensions={0} | all-to-all | bytes 524288 | tf_op jit(solution)/shard_map/all_to_all | solution.py:697
  40.3 12.8 %all_to_all.18 = bf16[16,64,128]{2,1,0:T(8,128)(2,1)S(1)} all-to-all(bf16[16,64,128]{2,1,0:T(8,128)(2,1)S(1)} %sum_chunks.1), channel_id=1, replica_groups=mesh['lat'=4,'ring'=4,'core'=2] {'lat','ring'}, dimensions={0} | all-to-all | bytes 524288 | tf_op jit(solution)/shard_map/all_to_all | solution.py:704
  53.1 0.0 collective-permute-start.5
  53.1 1.8 %features_8.1 = bf16[32,128,128]{2,1,0:T(8,128)(2,1)} custom-call(bf16[1536,256]{1,0:T(8,128)(2,1)S(1)} %get-tuple-element.35.refs_0_, bf16[3,2,2176,128]{3,2,1,0:T(8,128)(2,1)S(1)} %get-tuple-element.56.refs_1_, f32[32,128,128]{2,1,0:T(8,128)S(1)} %get-tuple-element.57.refs_2_, bf16[32,128,128]{2,1,0:T(8,128)(2,1)} %features_0.1.refs_3_), custom_call_target="tpu_custom_call", output_to_operand_aliasing={{}: (3, {})} | custom-call | tf_op jit(solution)/shard_map/features_8/pallas_call | solution.py:675
  54.9 0.0 collective-permute-done.5.refs_2_
  54.9 1.8 %finish.1 = (f32[73,128]{1,0:T(8,128)}, f32[9,128,128]{2,1,0:T(8,128)}, f32[9,128,128]{2,1,0:T(8,128)}) custom-call(s32[3]{0:T(128)S(1)} %pad_add_fusion.refs_0_, bf16[1024,128]{1,0:T(8,128)(2,1)S(1)} %bitcast.25, bf16[1024,128]{1,0:T(8,128)(2,1)S(1)} %collective-permute-done.5.refs_2_, bf16[128,128]{1,0:T(8,128)(2,1)S(1)} %get-tuple-element.45.refs_10_.refs_9_.refs_3_, ...), custom_call_target="tpu_custom_call" | custom-call | tf_op jit(solution)/shard_map/finish/pallas_call | solution.py:713
  (13 shorter events, 0.1 us)
Async XLA Ops:
  1.5 6.1 %collective-permute-start.1 = (bf16[4,8,128]{2,1,0:T(8,128)(2,1)S(1)}, bf16[4,8,128]{2,1,0:T(8,128)(2,1)S(1)}, u32[]{:S(2)}, u32[]{:S(2)}) collective-permute-start(bf16[4,8,128]{2,1,0:T(8,128)(2,1)S(1)} %get-tuple-element.72), channel_id=1, source_target_pairs={{0,8},{8,0},{16,24},{24,16},{1,9},{9,1},{17,25},{25,17},{2,10},{10... | collective-permute-start | bytes 24584 | tf_op jit(solution)/shard_map/ppermute | solution.py:567
  4.5 3.1 %collective-permute-start = (bf16[4,8,128]{2,1,0:T(8,128)(2,1)S(1)}, bf16[4,8,128]{2,1,0:T(8,128)(2,1)S(1)}, u32[]{:S(2)}, u32[]{:S(2)}) collective-permute-start(bf16[4,8,128]{2,1,0:T(8,128)(2,1)S(1)} %get-tuple-element.73), channel_id=1, source_target_pairs={{8,16},{16,8},{9,17},{17,9},{10,18},{18,10},{11,19},{19,11},{12,20... | collective-permute-start | bytes 24584 | tf_op jit(solution)/shard_map/ppermute | solution.py:566
  7.7 7.0 %collective-permute-start.3 = (bf16[12,4,128]{2,1,0:T(4,128)(2,1)S(1)}, bf16[12,4,128]{2,1,0:T(4,128)(2,1)S(1)}, u32[]{:S(2)}, u32[]{:S(2)}) collective-permute-start(bf16[12,4,128]{2,1,0:T(4,128)(2,1)S(1)} %get-tuple-element.68), channel_id=1, source_target_pairs={{0,1},{1,0},{2,3},{3,2},{4,5},{5,4},{6,7},{7,6},{8,9},{9,8},{10,11... | collective-permute-start | bytes 36872 | tf_op jit(solution)/shard_map/ppermute | solution.py:629
  7.8 6.9 %collective-permute-start.2 = (bf16[12,4,128]{2,1,0:T(4,128)(2,1)S(1)}, bf16[12,4,128]{2,1,0:T(4,128)(2,1)S(1)}, u32[]{:S(2)}, u32[]{:S(2)}) collective-permute-start(bf16[12,4,128]{2,1,0:T(4,128)(2,1)S(1)} %get-tuple-element.69), channel_id=1, source_target_pairs={{0,7},{1,2},{2,1},{3,4},{4,3},{5,6},{6,5},{7,0},{8,15},{9,10},{10,... | collective-permute-start | bytes 36872 | tf_op jit(solution)/shard_map/ppermute | solution.py:628
  20.0 1.9 %collective-permute-start.4 = (bf16[1024,128]{1,0:T(8,128)(2,1)S(1)}, bf16[1024,128]{1,0:T(8,128)(2,1)S(1)}, u32[]{:S(2)}, u32[]{:S(2)}) collective-permute-start(bf16[1024,128]{1,0:T(8,128)(2,1)S(1)} %slice_bitcast_fusion), channel_id=1, source_target_pairs={{0,1},{1,0},{2,3},{3,2},{4,5},{5,4},{6,7},{7,6},{8,9},{9,8},{10,11... | collective-permute-start | bytes 786440 | tf_op jit(solution)/shard_map/ppermute | solution.py:690
  53.1 1.8 %collective-permute-start.5 = (bf16[1024,128]{1,0:T(8,128)(2,1)S(1)}, bf16[1024,128]{1,0:T(8,128)(2,1)S(1)}, u32[]{:S(2)}, u32[]{:S(2)}) collective-permute-start(bf16[1024,128]{1,0:T(8,128)(2,1)S(1)} %bitcast.24), channel_id=1, source_target_pairs={{0,1},{1,0},{2,3},{3,2},{4,5},{5,4},{6,7},{7,6},{8,9},{9,8},{10,11... | collective-permute-start | bytes 786440 | tf_op jit(solution)/shard_map/ppermute | solution.py:705

commit v2 on v1

--- a/solution.py
+++ b/solution.py
@@ -14,7 +14,7 @@
 COL_HALO = 4
 SPAN = 16
 GRAD_ROWS = 80
-VMEM_BYTES = 36 * 1024 * 1024
+VMEM_BYTES = 24 * 1024 * 1024
 
 
 def split_two(value):
@@ -84,36 +84,46 @@
     return index, block[at + 1 : at + 2] + block[at + 2 : at + 3] + block[at + 3 : at + 4]
 
 
-def row_spots(place_ref, rsrc_ref, rfrac_ref, before_ref, after_ref, rows, band_rows, lat_count):
-    lat = place_ref[0]
-    line_of = lax.broadcasted_iota(jnp.int32, (1, LANES), 1)
-
-    def one_of(value, at):
-        return jnp.sum(jnp.where(line_of == at, value, 0.0))
-
+def joined_line(first, own, last, width):
+    lane_count = 2 * LANES
+    lane = lax.broadcasted_iota(jnp.int32, (1, lane_count), 1)
+    out = []
+    for part, shift in zip((first, own, last), (lane_count - width + 2, 2, width + 2)):
+        part = jnp.concatenate([part[:, :width], jnp.zeros((1, lane_count - width), F32)], axis=1)
+        out.append(pltpu.roll(jnp.broadcast_to(part, (8, lane_count)), shift, 1)[:1])
+    return jnp.where(lane < 2, out[0], jnp.where(lane < width + 2, out[1], out[2]))
+
+
+def row_blend(rsrc_ref, rfrac_ref, before_ref, after_ref, lat, lat_count, band_rows):
+    rows = rsrc_ref.shape[1]
+    cells = 2 * COL_HALO
     before_line = edge_line(before_ref[ROW_HALO].astype(F32), 0)
     after_line = edge_line(after_ref[ROW_HALO].astype(F32), 0)
-    spots = []
+    own_line = (rsrc_ref[...].astype(F32), rfrac_ref[...])
+    src, frac = (
+        joined_line(*lines, rows) for lines in zip(before_line, own_line, after_line)
+    )
+    spot = (src - (lat * band_rows - ROW_HALO).astype(F32)) * cells
+    shape = (cells, LANES)
+    at = lax.broadcasted_iota(jnp.int32, shape, 1) - lax.broadcasted_iota(jnp.int32, shape, 0)
+    at = at.astype(F32)
+    parts = []
     for q in range(rows + 4):
-        line_at = lat * rows + q - 2
-        inside = jnp.logical_and(line_at >= 0, line_at < lat_count * rows)
+        here = jnp.broadcast_to(spot[:, q : q + 1], shape)
+        f = jnp.broadcast_to(frac[:, q : q + 1], shape)
+        part = jnp.where(at == here, 1.0 - f, 0.0) + jnp.where(at == here + cells, f, 0.0)
         if q < 2:
-            index, f = (one_of(v, rows - 2 + q) for v in before_line)
-            index = index.astype(jnp.int32)
-        elif q < rows + 2:
-            index, f = rsrc_ref[0, q - 2], rfrac_ref[0, q - 2]
-        else:
-            index, f = (one_of(v, q - rows - 2) for v in after_line)
-            index = index.astype(jnp.int32)
-        j0 = jnp.clip(index - lat * band_rows + ROW_HALO, 0, band_rows + 2 * ROW_HALO - 2)
-        spots.append((j0, jnp.where(inside, 1.0 - f, 0.0), jnp.where(inside, f, 0.0)))
-    return spots
-
-
-def blend_rows(cells_ref, spots):
-    return jnp.concatenate(
-        [w0 * cells_ref[j0] + w1 * cells_ref[j0 + 1] for j0, w0, w1 in spots], axis=0
-    )
+            part = part * jnp.where(lat > 0, 1.0, 0.0)
+        elif q >= rows + 2:
+            part = part * jnp.where(lat < lat_count - 1, 1.0, 0.0)
+        parts.append(part)
+    return jnp.concatenate(list(split_two(jnp.concatenate(parts, axis=0))), axis=1)
+
+
+def blend_rows(matrix, cells):
+    fill = jnp.zeros((LANES - sum(c.shape[0] for c in cells), LANES), F32)
+    column = jnp.concatenate(list(cells) + [fill], axis=0).astype(BF16)
+    return jnp.dot(matrix, jnp.concatenate([column, column], axis=0), preferred_element_type=F32)
 
 
 def lift_rows(mixed, embed):
@@ -155,7 +165,6 @@
 
 
 def back_kernel(
-    place_ref,
     rsrc_ref,
     rfrac_ref,
     shift_ref,
@@ -173,7 +182,7 @@
     lifted_ref,
     tap_ref,
     cot_col_ref,
-    cells_ref,
+    blend_ref,
     *,
     lat_count,
     coarse_cols,
@@ -195,22 +204,19 @@
             for q in range(2):
                 bh_ref[2 * (first + m) + q] = out[m * wide : (m + 1) * wide, q * LANES : (q + 1) * LANES]
 
-    for j in range(cells_ref.shape[0]):
-        if j < ROW_HALO:
-            middle = before_ref[j]
-        elif j < ROW_HALO + band_rows:
-            middle = own_ref[j - ROW_HALO]
-        else:
-            middle = after_ref[j - ROW_HALO - band_rows]
-        cells_ref[j] = middle.astype(F32)
-    spots = row_spots(place_ref, rsrc_ref, rfrac_ref, before_ref, after_ref, rows, band_rows, lat_count)
-    mixed = blend_rows(cells_ref, spots)
+    lat = lax.axis_index("lat")
+    lon = lax.axis_index("ring") * 2 + lax.axis_index("core")
+    matrix = row_blend(rsrc_ref, rfrac_ref, before_ref, after_ref, lat, lat_count, band_rows)
+    blend_ref[...] = matrix
+    cells = [before_ref[j] for j in range(ROW_HALO)] + [own_ref[j] for j in range(band_rows)]
+    cells += [after_ref[j] for j in range(ROW_HALO)]
+    mixed = blend_rows(matrix, [c.astype(F32) for c in cells])
     rows_ref[0], rows_ref[1] = turned_rows(mixed, rows_ref.shape[2])
     lifted = lift_rows(mixed, embed_ref[...])
     lifted_ref[...] = lifted
     tap_ref[...] = tap_rows(lifted, w1_ref, band_cols)
 
-    blend = blend_cols(csrc_ref[...], cfrac_ref[...], place_ref[1], band_cols, coarse_cols)
+    blend = blend_cols(csrc_ref[...], cfrac_ref[...], lon, band_cols, coarse_cols)
     own_t = jnp.concatenate(list(split_two(blend)), axis=0)
     every = jnp.concatenate([cot_ref[r] for r in range(rows)], axis=1)
     back = jnp.dot(own_t, every, preferred_element_type=F32)
@@ -248,13 +254,8 @@
 
 
 def main_kernel(
-    place_ref,
-    rsrc_ref,
-    rfrac_ref,
-    before_ref,
-    after_ref,
-    west_ref,
-    east_ref,
+    far_ref,
+    near_ref,
     csrc_ref,
     cfrac_ref,
     embed_ref,
@@ -265,30 +266,29 @@
     lifted_ref,
     tap_ref,
     cot_col_ref,
+    blend_ref,
     hid_ref,
-    lift_ref,
+    own_ref,
+    lift_right_ref,
     msg_ref,
-    cells_ref,
     side_tap_ref,
     line_ref,
     right_ref,
-    lift_right_ref,
     delta_ref,
     back_ref,
     *,
     lat_count,
     coarse_cols,
-    band_rows,
     band_cols,
 ):
-    rows, cols, _ = lift_ref.shape
+    rows, cols = cot_col_ref.shape[0], own_ref.shape[0]
     wide = bh_ref.shape[1]
     pairs = bh_ref.shape[0] // 2
-    depth = cells_ref.shape[0]
+    depth = 2 * (far_ref.shape[0] - 1)
     half_rows = msg_ref.shape[1]
-    lat = place_ref[0]
-    lon = place_ref[1]
-    core = place_ref[2]
+    lat = lax.axis_index("lat")
+    core = lax.axis_index("core")
+    lon = lax.axis_index("ring") * 2 + core
     taps = 3 * SPAN
 
     def send(at, value):
@@ -296,27 +296,23 @@
         at = at % half_rows
         msg_ref[side, at : at + value.shape[0]] = value.astype(BF16)
 
+    sides = []
+    for j in range(depth // 2 + 1):
+        far, near = far_ref[j].astype(F32), near_ref[j].astype(F32)
+        sides.append((jnp.where(core == 1, near, far), jnp.where(core == 1, far, near)))
+    cells = []
     for j in range(depth):
-        cells_ref[j, :COL_HALO] = west_ref[j].astype(F32)
-        cells_ref[j, COL_HALO:] = east_ref[j].astype(F32)
-    spots = row_spots(place_ref, rsrc_ref, rfrac_ref, before_ref, after_ref, rows, band_rows, lat_count)
-    side_mixed = blend_rows(cells_ref, spots)
+        part = slice(j % 2 * COL_HALO, (j % 2 + 1) * COL_HALO)
+        cells += [v[part] for v in sides[j // 2]]
+    side_mixed = blend_rows(blend_ref[...], cells)
     side_lifted = lift_rows(side_mixed, embed_ref[...])
     side_tap_ref[...] = tap_rows(side_lifted, w1_ref, band_cols)
 
     lane_count = 2 * LANES
     lane = lax.broadcasted_iota(jnp.int32, (1, lane_count), 1)
-    west_line = edge_line(jnp.concatenate([west_ref[j] for j in (depth, depth + 1)], axis=0).astype(F32), 4)
-    east_line = edge_line(jnp.concatenate([east_ref[j] for j in (depth, depth + 1)], axis=0).astype(F32), 4)
+    west_line, east_line = (edge_line(v, 4) for v in sides[depth // 2])
     own_line = (csrc_ref[...].astype(F32), cfrac_ref[...])
-    blank = jnp.zeros((1, lane_count - cols), F32)
-    lines = []
-    for parts in zip(west_line, own_line, east_line):
-        out = []
-        for part, shift in zip(parts, (lane_count - cols + 2, 2, cols + 2)):
-            part = jnp.concatenate([part, blank], axis=1)
-            out.append(pltpu.roll(jnp.broadcast_to(part, (8, lane_count)), shift, 1)[:1])
-        lines.append(jnp.where(lane < 2, out[0], jnp.where(lane < cols + 2, out[1], out[2])))
+    lines = [joined_line(*v, cols) for v in zip(west_line, own_line, east_line)]
     known = lane < cols + 4
     src = jnp.where(known, lines[0], -1e6).astype(jnp.int32)
     blend = blend_cols(src, jnp.where(known, lines[1], 0.0), lon, band_cols, coarse_cols)
@@ -328,7 +324,7 @@
     col_lhs = jnp.concatenate([high_f.T, low_f.T, high_f.T], axis=1).astype(BF16)
     own_hi, own_lo = split_two(rolled[2][:, :cols])
     own_hi, own_lo = own_hi.astype(F32).T, own_lo.astype(F32).T
-    own_lhs = jnp.concatenate([own_hi, own_lo, own_hi], axis=1).astype(BF16)
+    own_ref[...] = jnp.concatenate([own_hi, own_lo, own_hi], axis=1).astype(BF16)
 
     def stacked(value):
         one, two = split_two(value)
@@ -346,9 +342,16 @@
         lift_right_ref[:, r * LANES : (r + 1) * LANES] = stacked(
             jnp.concatenate([lifted_ref[part], side_lifted[part]], axis=0)
         )
-    pre = jnp.dot(col_lhs, right_ref[...], preferred_element_type=F32)
-    for t in range(2 * pairs):
-        v = pre[:, t * LANES : (t + 1) * LANES]
+    half = rows // 2 + 2
+    spans = ((0, half), (half, 2 * pairs))
+    cells_half = rows // 4 * cols
+
+    def first_product(n):
+        span = slice(spans[n][0] * LANES, spans[n][1] * LANES)
+        return jnp.dot(col_lhs, right_ref[:, span], preferred_element_type=F32)
+
+    def activate(pre, first, t):
+        v = pre[:, (t - first) * LANES : (t - first + 1) * LANES]
         s = 0.5 + 0.5 * jnp.tanh(0.5 * v)
         if t == 0:
             s = s * jnp.where(lat > 0, 1.0, 0.0)
@@ -358,16 +361,39 @@
         slope = s + h * (1.0 - s)
         line_ref[t] = h
         delta_ref[:, t * LANES : (t + 1) * LANES] = (bh_ref[t] * slope).astype(BF16)
-    for t in range(2 * pairs):
+
+    def place_hidden(t):
+        at = (t // 2) * cols
         for b in range(3):
-            at = (t // 2) * cols
             hid_ref[b, t % 2, at : at + cols] = line_ref[t, b : b + cols].astype(BF16)
-    own = jnp.dot(own_lhs, lift_right_ref[...], preferred_element_type=F32)
-    for r in range(rows):
-        lift_ref[r] = own[:, r * LANES : (r + 1) * LANES]
-
+
+    def second_gradient(n, b):
+        right = []
+        for i in range(4):
+            start = (i // 2) * cols + n * cells_half
+            right.append(hid_ref[b, i % 2, start : start + cells_half])
+        left = turned_ref[:, n * cells_half : (n + 1) * cells_half]
+        return jnp.dot(left, jnp.concatenate(right, axis=1), preferred_element_type=F32)
+
+    pre = first_product(0)
+    for t in range(*spans[0]):
+        activate(pre, 0, t)
+    pre = first_product(1)
+    for t in range(*spans[0]):
+        place_hidden(t)
+    grads = []
+    rest = list(range(*spans[1]))
+    share = -(-len(rest) // 3)
+    for b in range(3):
+        grads.append(second_gradient(0, b))
+        for t in rest[b * share : (b + 1) * share]:
+            activate(pre, spans[1][0], t)
+            place_hidden(t)
     back = jnp.dot(col_t, delta_ref[...], preferred_element_type=F32)
     back = back[:taps] + back[taps:]
+    for b in range(3):
+        grads[b] = grads[b] + second_gradient(1, b)
+
     width = rows_ref.shape[2]
     used = 2 * pairs * band_cols
     blank = jnp.zeros((2, width - used, back_ref.shape[2]), BF16)
@@ -404,43 +430,54 @@
     if 2 * half_rows > tail:
         send(tail, jnp.zeros((2 * half_rows - tail, LANES), F32))
 
-    half = (rows // 2) * cols
-    left_t = turned_ref[...]
     for b in range(3):
-        right = jnp.concatenate(
-            [hid_ref[b, i % 2, (i // 2) * cols : (i // 2) * cols + half] for i in range(4)], axis=1
-        )
-        out = jnp.dot(left_t, right, preferred_element_type=F32)
         for a in range(3):
-            upper = out[:LANES, a * LANES : (a + 1) * LANES]
-            lower = out[LANES:, (a + 1) * LANES : (a + 2) * LANES]
-            tap = a * 3 + b
-            send(tap * LANES, (upper + lower).T)
-
-
-def features_kernel(weight_ref, hid_ref, lift_ref, *refs, first, last):
-    out_hbm, feat_ref, sems = refs[-3:]
-    cols = feat_ref.shape[1]
-    step = (last - first) // sems.shape[0]
-    copies = []
-    for n in range(sems.shape[0]):
-        top = first + n * step
+            upper = grads[b][:LANES, a * LANES : (a + 1) * LANES]
+            lower = grads[b][LANES:, (a + 1) * LANES : (a + 2) * LANES]
+            send((a * 3 + b) * LANES, (upper + lower).T)
+
+
+def join_kernel(own_ref, inner_ref, outer_ref, ready_ref, before_ref, after_ref, far_ref, near_ref):
+    band_rows, band_cols = own_ref.shape[0] - 1, own_ref.shape[1]
+    even = lax.rem(lax.axis_index("lat"), 2) == 0
+    first = lax.axis_index("core") == 0
+    outer = [outer_ref[j].astype(F32) for j in range(ROW_HALO + 1)]
+    inner = [inner_ref[j].astype(F32) for j in range(ROW_HALO + 1)]
+    before = [jnp.where(even, v, w) for v, w in zip(outer, inner)]
+    after = [jnp.where(even, w, v) for v, w in zip(outer, inner)]
+    own = [own_ref[j].astype(F32) for j in range(band_rows + 1)]
+    for j in range(ROW_HALO + 1):
+        before_ref[j] = before[j].astype(BF16)
+        after_ref[j] = after[j].astype(BF16)
+    tall = before[:ROW_HALO] + own[:band_rows] + after[:ROW_HALO]
+    for j in range(0, len(tall), 2):
+        to_last = jnp.concatenate([v[:COL_HALO] for v in tall[j : j + 2]], axis=0)
+        to_next = jnp.concatenate([v[band_cols - COL_HALO :] for v in tall[j : j + 2]], axis=0)
+        far_ref[j // 2] = jnp.where(first, to_last, to_next).astype(BF16)
+        near_ref[j // 2] = jnp.where(first, to_next, to_last).astype(BF16)
+    far_ref[len(tall) // 2] = own[band_rows].astype(BF16)
+    near_ref[len(tall) // 2] = own[band_rows].astype(BF16)
+
+
+def features_kernel(weight_ref, hid_ref, own_ref, lift_right_ref, *refs, first):
+    feat_ref = refs[-1]
+    rows, cols, _ = feat_ref.shape
+    step = 4
+    for n in range(0, rows // 2, step):
+        top = first + n
         blocks = []
         for b in range(3):
             for i in range(4):
                 start = (top + i // 2) * cols
                 blocks.append(hid_ref[b, i % 2, start : start + step * cols])
         out = jnp.dot(jnp.concatenate(blocks, axis=1), weight_ref[...], preferred_element_type=F32)
+        span = slice(2 * top * LANES, 2 * (top + step) * LANES)
+        lift = jnp.dot(own_ref[...], lift_right_ref[:, span], preferred_element_type=F32)
         for m in range(step):
             for q in range(2):
                 piece = out[m * cols : (m + 1) * cols, q * LANES : (q + 1) * LANES]
-                r = 2 * (top + m) + q
-                feat_ref[r - 2 * first] = (lift_ref[r] + piece).astype(BF16)
-        part = feat_ref.at[pl.ds(2 * n * step, 2 * step)]
-        copies.append(pltpu.make_async_copy(part, out_hbm.at[pl.ds(2 * top, 2 * step)], sems.at[n]))
-        copies[-1].start()
-    for copy in copies:
-        copy.wait()
+                own = lift[:, (2 * m + q) * LANES : (2 * m + q + 1) * LANES]
+                feat_ref[2 * (n + m) + q] = (own + piece).astype(BF16)
 
 
 def reduce_kernel(in_ref, out_ref):
@@ -460,22 +497,25 @@
 
 
 def last_kernel(
-    place_ref, mine_ref, other_ref, embed_ref, first_ref, ge_hbm, g1_hbm, g2_hbm,
+    mine_ref, other_ref, embed_ref, first_ref, upper_ref, lower_ref, feat_hbm, ge_hbm, g1_hbm, g2_hbm,
     sum_ref, ge_ref, g1_ref, g2_ref, sems, *, scale
 ):
-    core = place_ref[2]
+    core = lax.axis_index("core")
     half_rows = mine_ref.shape[0]
-    sum_ref[core] = mine_ref[...]
-    sum_ref[1 - core] = other_ref[...]
-
-    def read(at, count):
-        return sum_ref[at // half_rows, at % half_rows : at % half_rows + count]
-
     copies = []
 
     def leave(source, target):
         copies.append(pltpu.make_async_copy(source, target, sems.at[len(copies)]))
         copies[-1].start()
+
+    count = upper_ref.shape[0]
+    leave(upper_ref, feat_hbm.at[pl.ds(0, count)])
+    leave(lower_ref, feat_hbm.at[pl.ds(count, count)])
+    sum_ref[core] = mine_ref[...]
+    sum_ref[1 - core] = other_ref[...]
+
+    def read(at, count):
+        return sum_ref[at // half_rows, at % half_rows : at % half_rows + count]
 
     for a in range(3):
         for tap in range(3 * a, 3 * a + 3):
@@ -528,12 +568,10 @@
     depth = band_rows + 2 * ROW_HALO
     params = pltpu.CompilerParams(vmem_limit_bytes=VMEM_BYTES)
     vmem = pl.BlockSpec(memory_space=pltpu.VMEM)
-    smem = pl.BlockSpec(memory_space=pltpu.SMEM)
     far = pl.BlockSpec(memory_space=pltpu.HBM)
 
     w1 = conv1_weight.reshape(9, hidden, hidden)
     w2 = conv2_weight.reshape(9, hidden, hidden)
-    place = jnp.stack([lat_place, lon_place, core_place]).astype(jnp.int32)
     row_line = (row_src.reshape(1, rows), row_frac.reshape(1, rows))
     col_line = (col_src.reshape(1, cols), col_frac.reshape(1, cols))
 
@@ -565,7 +603,6 @@
     outer = outer + [(j, i) for i, j in outer]
     got_outer = lax.ppermute(jnp.where(even, to_last, to_next), "lat", outer)
     got_inner = lax.ppermute(jnp.where(even, to_next, to_last), "lat", inner)
-    before, after = got_outer, got_inner
 
     shift, back_weight, fore_weight, turned, first_weight, cot, near_w1, embed = pl.pallas_call(
         prepare_kernel,
@@ -589,46 +626,40 @@
         compiler_params=params,
         name="prepare",
     )(from_hbm(cotangent), from_hbm(w2), from_hbm(w1), from_hbm(embed_weight))
-    before, after, shift, back_weight = lax.optimization_barrier((before, after, shift, back_weight))
-    before, after = jnp.where(even, before, after), jnp.where(even, after, before)
+    before, after, far_message, near_message = pl.pallas_call(
+        join_kernel,
+        out_shape=[jax.ShapeDtypeStruct((ROW_HALO + 1, band_cols, LANES), BF16)] * 2
+        + [jax.ShapeDtypeStruct((depth // 2 + 1, band_cols, LANES), BF16)] * 2,
+        compiler_params=params,
+        name="join",
+    )(own, got_inner, got_outer, embed)
+    lon = ("ring", "core")
+    inner = [(i, i ^ 1) for i in range(lon_count)]
+    outer = [(i, (i + (1 if i % 2 else -1)) % lon_count) for i in range(lon_count)]
+    got_far = lax.ppermute(far_message, lon, outer)
+    got_near = lax.ppermute(near_message, lon, inner)
 
     def back_body(*refs):
         back_kernel(*refs, lat_count=lat_count, coarse_cols=band_cols * lon_count)
 
     reach = rows + 4
     width = -(-reach * band_cols // LANES) * LANES
-    bh, mixed, lifted, tap, cot_col = pl.pallas_call(
+    bh, mixed, lifted, tap, cot_col, blend = pl.pallas_call(
         back_body,
-        in_specs=[smem] * 3 + [vmem] * 10,
         out_shape=[
             jax.ShapeDtypeStruct((2 * pairs, wide, hidden), F32),
             jax.ShapeDtypeStruct((2, 3 * GRAD_ROWS, width), BF16),
             jax.ShapeDtypeStruct((reach * band_cols, hidden), F32),
             jax.ShapeDtypeStruct(((reach - 2) * band_cols, 3 * hidden), F32),
             jax.ShapeDtypeStruct((rows, SPAN, hidden), F32),
-        ],
-        scratch_shapes=[
-            pltpu.VMEM((depth, band_cols, LANES), F32),
+            jax.ShapeDtypeStruct((reach * band_cols, 2 * LANES), BF16),
         ],
         compiler_params=params,
         name="back_hidden",
     )(
-        place, *row_line, shift, back_weight, before, own, after, *col_line,
+        *row_line, shift, back_weight, before, own, after, *col_line,
         embed, near_w1, cot,
     )
-
-    tall = jnp.concatenate([before[:ROW_HALO], own[:band_rows], after[:ROW_HALO]])
-    lines = edge.reshape(band_cols // COL_HALO, COL_HALO, LANES)
-    lon = ("ring", "core")
-    to_next = jnp.concatenate([tall[:, band_cols - COL_HALO :], lines])
-    to_last = jnp.concatenate([tall[:, :COL_HALO], lines])
-    first = core_place == 0
-    inner = [(i, i ^ 1) for i in range(lon_count)]
-    outer = [(i, (i + (1 if i % 2 else -1)) % lon_count) for i in range(lon_count)]
-    got_outer = lax.ppermute(jnp.where(first, to_last, to_next), lon, outer)
-    got_inner = lax.ppermute(jnp.where(first, to_next, to_last), lon, inner)
-    west = jnp.where(first, got_outer, got_inner)
-    east = jnp.where(first, got_inner, got_outer)
 
     blocks = 9 * LANES + 10 * GRAD_ROWS
     chunk = -(-blocks // (core_count * group * 16)) * 16
@@ -639,49 +670,39 @@
             *refs,
             lat_count=lat_count,
             coarse_cols=band_cols * lon_count,
-            band_rows=band_rows,
             band_cols=band_cols,
         )
 
-    hid, lift, message = pl.pallas_call(
+    hid, own_blend, lift_right, message = pl.pallas_call(
         body,
-        in_specs=[smem] * 3 + [vmem] * 14,
-        out_specs=[vmem] * 3,
+        out_specs=[vmem] * 4,
         out_shape=[
             jax.ShapeDtypeStruct((3, 2, pairs * cols, hidden), BF16),
-            jax.ShapeDtypeStruct((rows, cols, hidden), F32),
+            jax.ShapeDtypeStruct((cols, 3 * SPAN), BF16),
+            jax.ShapeDtypeStruct((3 * SPAN, rows * hidden), BF16),
             jax.ShapeDtypeStruct((2, half_rows, LANES), BF16),
         ],
         scratch_shapes=[
-            pltpu.VMEM((depth, 2 * COL_HALO, LANES), F32),
             pltpu.VMEM(((reach - 2) * band_cols, 3 * hidden), F32),
             pltpu.VMEM((2 * pairs, wide, hidden), F32),
             pltpu.VMEM((9 * SPAN, 2 * pairs * hidden), BF16),
-            pltpu.VMEM((3 * SPAN, rows * hidden), BF16),
             pltpu.VMEM((wide, 2 * pairs * hidden), BF16),
             pltpu.VMEM((2, 2 * width, 4 * hidden), BF16),
         ],
         compiler_params=params,
         name="tile",
     )(
-        place, *row_line, before, after, west, east, *col_line,
-        embed, near_w1, turned, bh, mixed, lifted, tap, cot_col,
+        got_far, got_near, *col_line,
+        embed, near_w1, turned, bh, mixed, lifted, tap, cot_col, blend,
     )
 
-    def half_features(first, last, *arrays):
+    def half_features(first, *arrays):
         def body(*refs):
-            features_kernel(*refs, first=first, last=last)
+            features_kernel(*refs, first=first)
 
         return pl.pallas_call(
             body,
-            in_specs=[vmem] * 3 + [far] * (len(arrays) - 3),
-            out_specs=far,
-            out_shape=jax.ShapeDtypeStruct((rows, cols, hidden), BF16),
-            input_output_aliases={n: 0 for n in range(3, len(arrays))},
-            scratch_shapes=[
-                pltpu.VMEM((2 * (last - first), cols, hidden), BF16),
-                pltpu.SemaphoreType.DMA((2,)),
-            ],
+            out_shape=jax.ShapeDtypeStruct((rows // 2, cols, hidden), BF16),
             compiler_params=params,
             name=f"features_{first}",
         )(*arrays)
@@ -689,7 +710,7 @@
     swap = [(0, 1), (1, 0)]
     received = lax.ppermute(message[1], "core", swap)
     middle = rows // 4
-    part = half_features(0, middle, fore_weight, hid, lift)
+    part = half_features(0, fore_weight, hid, own_blend, lift_right)
     received, part = lax.optimization_barrier((received, part))
     pair = (message[0].astype(F32) + received.astype(F32)).astype(BF16)
     axes = ("lat", "ring")
@@ -703,18 +724,17 @@
     )(parts.reshape(group, chunk, LANES))
     mine = lax.all_to_all(copies.reshape(half_rows, LANES), axes, 0, 0, tiled=True)
     other = lax.ppermute(mine, "core", swap)
-    _, part = lax.optimization_barrier((mine, part))
-    features = half_features(middle, rows // 2, fore_weight, hid, lift, part)
+    last_part = half_features(middle, fore_weight, hid, own_blend, lift_right, mine)
     scale = 1.0 / math.sqrt(rows * lat_count * cols * lon_count)
 
     def finish(*refs):
         last_kernel(*refs, scale=scale)
 
-    grad_embed, grad_first, grad_second = pl.pallas_call(
+    features, grad_embed, grad_first, grad_second = pl.pallas_call(
         finish,
-        in_specs=[smem] + [vmem] * 4,
-        out_specs=[far] * 3,
+        out_specs=[far] * 4,
         out_shape=[
+            jax.ShapeDtypeStruct((rows, cols, hidden), BF16),
             jax.ShapeDtypeStruct((fields, hidden), F32),
             jax.ShapeDtypeStruct((9, hidden, hidden), F32),
             jax.ShapeDtypeStruct((9, hidden, hidden), F32),
@@ -724,11 +744,11 @@
             pltpu.VMEM((fields, hidden), F32),
             pltpu.VMEM((9, hidden, hidden), F32),
             pltpu.VMEM((9, hidden, hidden), F32),
-            pltpu.SemaphoreType.DMA((7,)),
+            pltpu.SemaphoreType.DMA((9,)),
         ],
         compiler_params=params,
         name="finish",
-    )(place, mine, other, embed, first_weight)
+    )(mine, other, embed, first_weight, part, last_part)
     shape = (3, 3, hidden, hidden)
     return (features, grad_embed, grad_first.reshape(shape), grad_second.reshape(shape))
 

time: 57 us -> 53.3 us (0.935)
  Pallas kernels: 17 us -> 13.9 us
  blocking collectives: 31 us -> 28.3 us
  starting transfers between devices: 7.5 us -> 9.52 us
    pallas_call x5 -> x6, Pallas kernels: 13.7 us -> 10.7 us  [the longest x1 4.31 us: on_device(): pl.pallas_call(body, out_specs=[vmem] * 4, out_shape=[jax.ShapeDtypeStruc...]
    all_to_all x1, blocking collectives: 18.2 us -> 15.3 us  [on_device(): parts = lax.all_to_all(pair, axes, 0, 0, tiled=True)]
    ppermute x1, starting transfers between devices: 3 us -> 5.74 us  [on_device(): got_inner = lax.ppermute(jnp.where(even, to_next, to_last), 'lat', inner)]
    ppermute x2, starting transfers between devices: 3.77 us -> 2.55 us  [the longest x1 2.55 us: on_device(): got_far = lax.ppermute(far_message, lon, outer)]
  transfers between devices with their start and end apart: 6 -> 6, of which waited for: 0 -> 1; matrix products, arithmetic and copies ran while one was open for 0% -> 0% of each run, Pallas kernels for 16% -> 14%
where the time goes in v2:
time: 53.3 us; the launch traced here: 53.1 us
  blocking collectives  28.3 us (53%)
  Pallas kernels  13.9 us (26%)
  starting transfers between devices  9.52 us (18%)
  between operations  0.77 us (1%)
    all_to_all x1, blocking collectives, on_device(): parts = lax.all_to_all(pair, axes, 0, 0, tiled=True)  15.3 us
    all_to_all x1, blocking collectives, on_device(): lax.all_to_all(copies.reshape(half_rows, LANES), axes, 0, 0, tiled=True)  13 us
    ppermute x1, starting transfers between devices, on_device(): got_inner = lax.ppermute(jnp.where(even, to_next, to_last), 'lat', inner)  5.74 us
    pallas_call x1, Pallas kernels, on_device(): pl.pallas_call(body, out_specs=[vmem] * 4, out_shape=[jax.ShapeDtypeStruc...  4.31 us
    pallas_call x1, Pallas kernels, on_device(): pl.pallas_call(back_body, out_shape=[jax.ShapeDtypeStruct((2 * pairs, wid...  2.68 us
    ppermute x1, starting transfers between devices, on_device(): got_far = lax.ppermute(far_message, lon, outer)  2.55 us
    pallas_call x1, Pallas kernels, on_device(): pl.pallas_call(prepare_kernel, out_shape=[jax.ShapeDtypeStruct((3, 2, (pa...  2.42 us
    pallas_call x2, Pallas kernels, half_features(): pl.pallas_call(body, out_shape=jax.ShapeDtypeStruct((rows // 2, cols, hid...  2.22 us
  transfers between devices with their start and end apart: 6, of which 1 were waited for; matrix products, arithmetic and copies ran while one was open for 0% of the time, Pallas kernels for 14%

profile of v2, /device:TPU:0, one launch (start us, length us, event | category | flops | bytes accessed | tf_op | source)
XLA Modules:
  0.0 53.1 jit_solution(14976606260475182102)
XLA Ops:
  0.6 0.8 %pack.1 = (f32[5,8,128]{2,1,0:T(8,128)S(1)}, s32[1,32]{1,0:T(1,128)S(1)}, f32[1,32]{1,0:T(1,128)S(1)}, s32[1,128]{1,0:T(1,128)S(1)}, f32[1,128]{1,0:T(1,128)S(1)}) custom-call(bf16[4,8,73]{2,1,0:T(8,128)(2,1)} %bitcast.22, s32[1,32]{1,0:T(1,128)} %bitcast.23, f32[1,32]{1,0:T(1,128)} %bitcast.24, s32[1,128]{1,0:T(1,128)} %bitcast.25, f32[1,128]{1,0:T(1,128)} %bitcast.26), custom_call_target="tpu_custom_call" | custom-call | tf_op jit(solution)/shard_map/pack/pallas_call | solution.py:583
  1.5 0.7 %collective-permute-start.1 = (bf16[4,8,128]{2,1,0:T(8,128)(2,1)S(1)}, bf16[4,8,128]{2,1,0:T(8,128)(2,1)S(1)}, u32[]{:S(2)}, u32[]{:S(2)}) collective-permute-start(bf16[4,8,128]{2,1,0:T(8,128)(2,1)S(1)} %get-tuple-element.70), channel_id=1, source_target_pairs={{8,16},{16,8},{9,17},{17,9},{10,18},{18,10},{11,19},{19,11},{12,20... | collective-permute-start | bytes 24584 | tf_op jit(solution)/shard_map/ppermute | solution.py:604
  2.2 5.7 %collective-permute-start = (bf16[4,8,128]{2,1,0:T(8,128)(2,1)S(1)}, bf16[4,8,128]{2,1,0:T(8,128)(2,1)S(1)}, u32[]{:S(2)}, u32[]{:S(2)}) collective-permute-start(bf16[4,8,128]{2,1,0:T(8,128)(2,1)S(1)} %get-tuple-element.71), channel_id=1, source_target_pairs={{0,8},{8,0},{16,24},{24,16},{1,9},{9,1},{17,25},{25,17},{2,10},{10... | collective-permute-start | bytes 24584 | tf_op jit(solution)/shard_map/ppermute | solution.py:605
  7.9 2.4 %prepare.1 = (bf16[3,2,2592,128]{3,2,1,0:T(8,128)(2,1)S(1)}, bf16[1536,256]{1,0:T(8,128)(2,1)S(1)}, bf16[1536,256]{1,0:T(8,128)(2,1)S(1)}, bf16[256,2048]{1,0:T(...) custom-call(bf16[32,128,128]{2,1,0:T(8,128)(2,1)} %cot_hbm.1, ...), custom_call_target="tpu_custom_call" | custom-call | tf_op jit(solution)/shard_map/prepare/pallas_call | solution.py:607
  10.3 0.0 collective-permute-done.1.outer_ref
  10.3 0.0 collective-permute-done.inner_ref
  10.4 2.5 %collective-permute-start.2 = (bf16[6,8,128]{2,1,0:T(8,128)(2,1)S(1)}, bf16[6,8,128]{2,1,0:T(8,128)(2,1)S(1)}, u32[]{:S(2)}, u32[]{:S(2)}) collective-permute-start(bf16[6,8,128]{2,1,0:T(8,128)(2,1)S(1)} %get-tuple-element.39), channel_id=1, source_target_pairs={{0,7},{1,2},{2,1},{3,4},{4,3},{5,6},{6,5},{7,0},{8,15},{9,10},{10,... | collective-permute-start | bytes 36872 | tf_op jit(solution)/shard_map/ppermute | solution.py:639
  12.9 0.0 collective-permute-start.3
  12.9 2.7 %back_hidden.1 = (f32[34,144,128]{2,1,0:T(8,128)S(1)}, bf16[2,240,384]{2,1,0:T(8,128)(2,1)S(1)}, f32[288,128]{1,0:T(8,128)S(1)}, f32[272,384]{1,0:T(8,128)S(1)},...) custom-call(s32[1,32]{1,0:T(1,128)S(1)} %get-tuple-element.45.refs_0_, f32[1,32]{1,0:T(1,128)S(1)} %get-tuple-element.46.refs_1_, ...), custom_call_target="tpu_custom_call" | custom-call | tf_op jit(solution)/shard_map/back_hidden/pallas_call | solution.py:647
  15.6 0.0 collective-permute-done.2.refs_0_
  15.6 0.0 collective-permute-done.3.refs_1_
  15.6 4.3 %tile.1 = (bf16[3,2,2176,128]{3,2,1,0:T(8,128)(2,1)S(1)}, bf16[128,48]{1,0:T(8,128)(2,1)S(1)}, bf16[48,4096]{1,0:T(8,128)(2,1)S(1)}, bf16[2,1024,128]{2,1,0:T(8,128)(2,1)S(1)}) custom-call(bf16[6,8,128]{2,1,0:T(8,128)(2,1)S(1)} %collective-permute-done.2.refs_0_, bf16[6,8,128]{2,1,0:T(8,128)(2,1)S(1)} %collective-permute-done.3.refs_1_, ...), custom_call_target="tpu_custom_call" | custom-call | tf_op jit(solution)/shard_map/tile/pallas_call | solution.py:676
  19.9 0.6 %collective-permute-start.4 = (bf16[1024,128]{1,0:T(8,128)(2,1)S(1)}, bf16[1024,128]{1,0:T(8,128)(2,1)S(1)}, u32[]{:S(2)}, u32[]{:S(2)}) collective-permute-start(bf16[1024,128]{1,0:T(8,128)(2,1)S(1)} %slice_bitcast_fusion), channel_id=1, source_target_pairs={{0,1},{1,0},{2,3},{3,2},{4,5},{5,4},{6,7},{7,6},{8,9},{9,8},{10,11... | collective-permute-start | bytes 786440 | tf_op jit(solution)/shard_map/ppermute | solution.py:711
  20.5 1.1 %features_0.1.refs_4_ = bf16[16,128,128]{2,1,0:T(8,128)(2,1)S(1)} custom-call(bf16[1536,256]{1,0:T(8,128)(2,1)S(1)} %get-tuple-element.59.refs_0_, bf16[3,2,2176,128]{3,2,1,0:T(8,128)(2,1)S(1)} %get-tuple-element.60.refs_1_, bf16[128,48]{1,0:T(8,128)(2,1)S(1)} %get-tuple-element.61.refs_2_, bf16[48,4096]{1,0:T(8,128)(2,1)S(1)} %get-tuple-element.62.refs_3_), custom_call_target="tpu_custom_call" | custom-call | tf_op jit(solution)/shard_map/features_0/pallas_call | solution.py:703
  21.6 0.0 collective-permute-done.4
  21.7 0.1 fusion
  21.8 15.3 %all_to_all.17.in_ref = bf16[16,64,128]{2,1,0:T(8,128)(2,1)S(1)} all-to-all(bf16[16,64,128]{2,1,0:T(8,128)(2,1)S(1)} %bitcast.19), channel_id=1, replica_groups=mesh['lat'=4,'ring'=4,'core'=2] {'lat','ring'}, dimensions={0} | all-to-all | bytes 524288 | tf_op jit(solution)/shard_map/all_to_all | solution.py:718
  37.1 13.0 %all_to_all.18 = bf16[16,64,128]{2,1,0:T(8,128)(2,1)S(1)} all-to-all(bf16[16,64,128]{2,1,0:T(8,128)(2,1)S(1)} %sum_chunks.1), channel_id=1, replica_groups=mesh['lat'=4,'ring'=4,'core'=2] {'lat','ring'}, dimensions={0} | all-to-all | bytes 524288 | tf_op jit(solution)/shard_map/all_to_all | solution.py:725
  50.1 0.0 collective-permute-start.5
  50.1 1.1 %features_8.1.refs_5_ = bf16[16,128,128]{2,1,0:T(8,128)(2,1)S(1)} custom-call(bf16[1536,256]{1,0:T(8,128)(2,1)S(1)} %get-tuple-element.59.refs_0_, bf16[3,2,2176,128]{3,2,1,0:T(8,128)(2,1)S(1)} %get-tuple-element.60.refs_1_, bf16[128,48]{1,0:T(8,128)(2,1)S(1)} %get-tuple-element.61.refs_2_, bf16[48,4096]{1,0:T(8,128)(2,1)S(1)} %get-tuple-element.62.refs_3_, ...), custom_call_target="tpu_custom_call" | custom-call | tf_op jit(solution)/shard_map/features_8/pallas_call | solution.py:703
  51.2 0.4 collective-permute-done.5.refs_1_
  51.6 1.4 %finish.1 = (bf16[32,128,128]{2,1,0:T(8,128)(2,1)}, f32[73,128]{1,0:T(8,128)}, f32[9,128,128]{2,1,0:T(8,128)}, f32[9,128,128]{2,1,0:T(8,128)}) custom-call(bf16[1024,128]{1,0:T(8,128)(2,1)S(1)} %bitcast.18, bf16[1024,128]{1,0:T(8,128)(2,1)S(1)} %collective-permute-done.5.refs_1_, bf16[128,128]{1,0:T(8,128)(2,1)S(1)} %get-tuple-element.38.ready_ref.refs_9_.refs_4_.refs_2_, ...), custom_call_target="tpu_custom_call" | custom-call | tf_op jit(solution)/shard_map/finish/pallas_call | solution.py:733
  (7 shorter events, 0.1 us)
Async XLA Ops:
  1.5 8.8 %collective-permute-start.1 = (bf16[4,8,128]{2,1,0:T(8,128)(2,1)S(1)}, bf16[4,8,128]{2,1,0:T(8,128)(2,1)S(1)}, u32[]{:S(2)}, u32[]{:S(2)}) collective-permute-start(bf16[4,8,128]{2,1,0:T(8,128)(2,1)S(1)} %get-tuple-element.70), channel_id=1, source_target_pairs={{8,16},{16,8},{9,17},{17,9},{10,18},{18,10},{11,19},{19,11},{12,20... | collective-permute-start | bytes 24584 | tf_op jit(solution)/shard_map/ppermute | solution.py:604
  2.2 8.2 %collective-permute-start = (bf16[4,8,128]{2,1,0:T(8,128)(2,1)S(1)}, bf16[4,8,128]{2,1,0:T(8,128)(2,1)S(1)}, u32[]{:S(2)}, u32[]{:S(2)}) collective-permute-start(bf16[4,8,128]{2,1,0:T(8,128)(2,1)S(1)} %get-tuple-element.71), channel_id=1, source_target_pairs={{0,8},{8,0},{16,24},{24,16},{1,9},{9,1},{17,25},{25,17},{2,10},{10... | collective-permute-start | bytes 24584 | tf_op jit(solution)/shard_map/ppermute | solution.py:605
  10.4 5.2 %collective-permute-start.2 = (bf16[6,8,128]{2,1,0:T(8,128)(2,1)S(1)}, bf16[6,8,128]{2,1,0:T(8,128)(2,1)S(1)}, u32[]{:S(2)}, u32[]{:S(2)}) collective-permute-start(bf16[6,8,128]{2,1,0:T(8,128)(2,1)S(1)} %get-tuple-element.39), channel_id=1, source_target_pairs={{0,7},{1,2},{2,1},{3,4},{4,3},{5,6},{6,5},{7,0},{8,15},{9,10},{10,... | collective-permute-start | bytes 36872 | tf_op jit(solution)/shard_map/ppermute | solution.py:639
  12.9 2.7 %collective-permute-start.3 = (bf16[6,8,128]{2,1,0:T(8,128)(2,1)S(1)}, bf16[6,8,128]{2,1,0:T(8,128)(2,1)S(1)}, u32[]{:S(2)}, u32[]{:S(2)}) collective-permute-start(bf16[6,8,128]{2,1,0:T(8,128)(2,1)S(1)} %get-tuple-element.40), channel_id=1, source_target_pairs={{0,1},{1,0},{2,3},{3,2},{4,5},{5,4},{6,7},{7,6},{8,9},{9,8},{10,11... | collective-permute-start | bytes 36872 | tf_op jit(solution)/shard_map/ppermute | solution.py:640
  19.9 1.7 %collective-permute-start.4 = (bf16[1024,128]{1,0:T(8,128)(2,1)S(1)}, bf16[1024,128]{1,0:T(8,128)(2,1)S(1)}, u32[]{:S(2)}, u32[]{:S(2)}) collective-permute-start(bf16[1024,128]{1,0:T(8,128)(2,1)S(1)} %slice_bitcast_fusion), channel_id=1, source_target_pairs={{0,1},{1,0},{2,3},{3,2},{4,5},{5,4},{6,7},{7,6},{8,9},{9,8},{10,11... | collective-permute-start | bytes 786440 | tf_op jit(solution)/shard_map/ppermute | solution.py:711
  50.1 1.5 %collective-permute-start.5 = (bf16[1024,128]{1,0:T(8,128)(2,1)S(1)}, bf16[1024,128]{1,0:T(8,128)(2,1)S(1)}, u32[]{:S(2)}, u32[]{:S(2)}) collective-permute-start(bf16[1024,128]{1,0:T(8,128)(2,1)S(1)} %bitcast.16), channel_id=1, source_target_pairs={{0,1},{1,0},{2,3},{3,2},{4,5},{5,4},{6,7},{7,6},{8,9},{9,8},{10,11... | collective-permute-start | bytes 786440 | tf_op jit(solution)/shard_map/ppermute | solution.py:726

commit v3 on v2

--- a/solution.py
+++ b/solution.py
@@ -126,6 +126,11 @@
     return jnp.dot(matrix, jnp.concatenate([column, column], axis=0), preferred_element_type=F32)
 
 
+def stacked(value):
+    one, two = split_two(value)
+    return jnp.concatenate([one, one, two], axis=0)
+
+
 def lift_rows(mixed, embed):
     pair = jnp.concatenate(list(split_two(mixed)), axis=1)
     return jnp.dot(pair, jnp.concatenate([embed, embed], axis=0), preferred_element_type=F32)
@@ -225,9 +230,9 @@
         cot_col_ref[r] = back[:, r * LANES : (r + 1) * LANES]
 
 
-def pack_kernel(cells_hbm, rsrc_hbm, rfrac_hbm, csrc_hbm, cfrac_hbm, out_ref, *space):
+def pack_kernel(cells_hbm, rsrc_hbm, rfrac_hbm, csrc_hbm, cfrac_hbm, *space):
     sources = (cells_hbm, rsrc_hbm, rfrac_hbm, csrc_hbm, cfrac_hbm)
-    *lines, cells_ref, sems = space
+    own_ref, early_ref, outer_ref, late_ref, *lines, cells_ref, out_ref, sems = space
     targets = (cells_ref, *lines)
     copies = [
         pltpu.make_async_copy(source, target, sems.at[n])
@@ -251,6 +256,18 @@
         for value in (index_ref[...].astype(F32), one, two, fraction - one - two):
             out_ref[depth, at : at + 1, :width] = value
             at += 1
+    lat = lax.axis_index("lat")
+    even = lax.rem(lat, 2) == 0
+    own = [out_ref[j] for j in range(depth + 1)]
+    to_next = own[depth - ROW_HALO :]
+    to_last = own[:ROW_HALO] + own[depth:]
+    for j in range(depth + 1):
+        own_ref[j] = own[j].astype(BF16)
+    for j in range(ROW_HALO + 1):
+        inner = jnp.where(even, to_next[j], to_last[j]).astype(BF16)
+        early_ref[j] = inner
+        outer_ref[j] = jnp.where(even, to_last[j], to_next[j]).astype(BF16)
+        late_ref[j] = inner
 
 
 def main_kernel(
@@ -263,13 +280,12 @@
     turned_ref,
     bh_ref,
     rows_ref,
-    lifted_ref,
     tap_ref,
     cot_col_ref,
     blend_ref,
     hid_ref,
     own_ref,
-    lift_right_ref,
+    side_lifted_ref,
     msg_ref,
     side_tap_ref,
     line_ref,
@@ -306,6 +322,7 @@
         cells += [v[part] for v in sides[j // 2]]
     side_mixed = blend_rows(blend_ref[...], cells)
     side_lifted = lift_rows(side_mixed, embed_ref[...])
+    side_lifted_ref[...] = side_lifted
     side_tap_ref[...] = tap_rows(side_lifted, w1_ref, band_cols)
 
     lane_count = 2 * LANES
@@ -326,10 +343,6 @@
     own_hi, own_lo = own_hi.astype(F32).T, own_lo.astype(F32).T
     own_ref[...] = jnp.concatenate([own_hi, own_lo, own_hi], axis=1).astype(BF16)
 
-    def stacked(value):
-        one, two = split_two(value)
-        return jnp.concatenate([one, one, two], axis=0)
-
     for t in range(2 * pairs):
         part = slice(t * band_cols, (t + 1) * band_cols)
         blocks = []
@@ -337,11 +350,6 @@
             column = slice(b * LANES, (b + 1) * LANES)
             blocks += [tap_ref[part, column], side_tap_ref[part, column]]
         right_ref[:, t * LANES : (t + 1) * LANES] = stacked(jnp.concatenate(blocks, axis=0))
-    for r in range(rows):
-        part = slice((r + 2) * band_cols, (r + 3) * band_cols)
-        lift_right_ref[:, r * LANES : (r + 1) * LANES] = stacked(
-            jnp.concatenate([lifted_ref[part], side_lifted[part]], axis=0)
-        )
     half = rows // 2 + 2
     spans = ((0, half), (half, 2 * pairs))
     cells_half = rows // 4 * cols
@@ -437,12 +445,17 @@
             send((a * 3 + b) * LANES, (upper + lower).T)
 
 
-def join_kernel(own_ref, inner_ref, outer_ref, ready_ref, before_ref, after_ref, far_ref, near_ref):
+def join_kernel(own_ref, early_ref, outer_ref, late_ref, ready_ref, before_ref, after_ref, far_ref, near_ref):
     band_rows, band_cols = own_ref.shape[0] - 1, own_ref.shape[1]
-    even = lax.rem(lax.axis_index("lat"), 2) == 0
+    lat = lax.axis_index("lat")
+    even = lax.rem(lat, 2) == 0
+    sent_late = lax.rem(lat + lat // 2, 2) == 0
     first = lax.axis_index("core") == 0
     outer = [outer_ref[j].astype(F32) for j in range(ROW_HALO + 1)]
-    inner = [inner_ref[j].astype(F32) for j in range(ROW_HALO + 1)]
+    inner = [
+        jnp.where(sent_late, late_ref[j].astype(F32), early_ref[j].astype(F32))
+        for j in range(ROW_HALO + 1)
+    ]
     before = [jnp.where(even, v, w) for v, w in zip(outer, inner)]
     after = [jnp.where(even, w, v) for v, w in zip(outer, inner)]
     own = [own_ref[j].astype(F32) for j in range(band_rows + 1)]
@@ -459,9 +472,10 @@
     near_ref[len(tall) // 2] = own[band_rows].astype(BF16)
 
 
-def features_kernel(weight_ref, hid_ref, own_ref, lift_right_ref, *refs, first):
+def features_kernel(weight_ref, hid_ref, own_ref, lifted_ref, side_lifted_ref, *refs, first):
     feat_ref = refs[-1]
     rows, cols, _ = feat_ref.shape
+    cells = own_ref.shape[1] // 6
     step = 4
     for n in range(0, rows // 2, step):
         top = first + n
@@ -471,8 +485,11 @@
                 start = (top + i // 2) * cols
                 blocks.append(hid_ref[b, i % 2, start : start + step * cols])
         out = jnp.dot(jnp.concatenate(blocks, axis=1), weight_ref[...], preferred_element_type=F32)
-        span = slice(2 * top * LANES, 2 * (top + step) * LANES)
-        lift = jnp.dot(own_ref[...], lift_right_ref[:, span], preferred_element_type=F32)
+        right = []
+        for r in range(2 * top, 2 * (top + step)):
+            part = slice((r + 2) * cells, (r + 3) * cells)
+            right.append(stacked(jnp.concatenate([lifted_ref[part], side_lifted_ref[part]], axis=0)))
+        lift = jnp.dot(own_ref[...], jnp.concatenate(right, axis=1), preferred_element_type=F32)
         for m in range(step):
             for q in range(2):
                 piece = out[m * cols : (m + 1) * cols, q * LANES : (q + 1) * LANES]
@@ -557,9 +574,6 @@
     ring_count = lax.axis_size("ring")
     core_count = lax.axis_size("core")
     lon_count = ring_count * core_count
-    lat_place = lax.axis_index("lat")
-    core_place = lax.axis_index("core")
-    lon_place = lax.axis_index("ring") * core_count + core_place
     fields, band_rows, band_cols = coarse.shape
     rows, cols, hidden = cotangent.shape
     group = lat_count * ring_count
@@ -580,29 +594,28 @@
         *row_line,
         *col_line,
     )
-    own, *lines = pl.pallas_call(
+    own, to_early, to_outer, to_late, *lines = pl.pallas_call(
         pack_kernel,
         in_specs=[far] * 5,
-        out_shape=[jax.ShapeDtypeStruct((band_rows + 1, band_cols, LANES), F32)]
+        out_shape=[jax.ShapeDtypeStruct((band_rows + 1, band_cols, LANES), BF16)]
+        + [jax.ShapeDtypeStruct((ROW_HALO + 1, band_cols, LANES), BF16)] * 3
         + [jax.ShapeDtypeStruct(x.shape, x.dtype) for x in pack_inputs[1:]],
         scratch_shapes=[
             pltpu.VMEM(pack_inputs[0].shape, BF16),
+            pltpu.VMEM((band_rows + 1, band_cols, LANES), F32),
             pltpu.SemaphoreType.DMA((5,)),
         ],
         compiler_params=params,
         name="pack",
     )(*(from_hbm(x) for x in pack_inputs))
-    own = own.astype(BF16)
     row_line, col_line = lines[:2], lines[2:]
-    edge = own[band_rows:]
-    to_next = own[band_rows - ROW_HALO :]
-    to_last = jnp.concatenate([own[:ROW_HALO], edge])
-    even = lat_place % 2 == 0
-    inner = [(i, i ^ 1) for i in range(lat_count)]
+    early = [(i, i ^ 1) for i in range(lat_count) if (i + i // 2) % 2 == 0]
+    late = [(j, i) for i, j in early]
     outer = [(i, i + 1) for i in range(1, lat_count - 1, 2)]
     outer = outer + [(j, i) for i, j in outer]
-    got_outer = lax.ppermute(jnp.where(even, to_last, to_next), "lat", outer)
-    got_inner = lax.ppermute(jnp.where(even, to_next, to_last), "lat", inner)
+    got_early = lax.ppermute(to_early, "lat", early)
+    got_outer = lax.ppermute(to_outer, "lat", outer)
+    got_late = lax.ppermute(to_late, "lat", late)
 
     shift, back_weight, fore_weight, turned, first_weight, cot, near_w1, embed = pl.pallas_call(
         prepare_kernel,
@@ -632,7 +645,7 @@
         + [jax.ShapeDtypeStruct((depth // 2 + 1, band_cols, LANES), BF16)] * 2,
         compiler_params=params,
         name="join",
-    )(own, got_inner, got_outer, embed)
+    )(own, got_early, got_outer, got_late, embed)
     lon = ("ring", "core")
     inner = [(i, i ^ 1) for i in range(lon_count)]
     outer = [(i, (i + (1 if i % 2 else -1)) % lon_count) for i in range(lon_count)]
@@ -673,13 +686,13 @@
             band_cols=band_cols,
         )
 
-    hid, own_blend, lift_right, message = pl.pallas_call(
+    hid, own_blend, side_lifted, message = pl.pallas_call(
         body,
         out_specs=[vmem] * 4,
         out_shape=[
             jax.ShapeDtypeStruct((3, 2, pairs * cols, hidden), BF16),
             jax.ShapeDtypeStruct((cols, 3 * SPAN), BF16),
-            jax.ShapeDtypeStruct((3 * SPAN, rows * hidden), BF16),
+            jax.ShapeDtypeStruct((reach * band_cols, hidden), F32),
             jax.ShapeDtypeStruct((2, half_rows, LANES), BF16),
         ],
         scratch_shapes=[
@@ -693,7 +706,7 @@
         name="tile",
     )(
         got_far, got_near, *col_line,
-        embed, near_w1, turned, bh, mixed, lifted, tap, cot_col, blend,
+        embed, near_w1, turned, bh, mixed, tap, cot_col, blend,
     )
 
     def half_features(first, *arrays):
@@ -710,7 +723,7 @@
     swap = [(0, 1), (1, 0)]
     received = lax.ppermute(message[1], "core", swap)
     middle = rows // 4
-    part = half_features(0, fore_weight, hid, own_blend, lift_right)
+    part = half_features(0, fore_weight, hid, own_blend, lifted, side_lifted)
     received, part = lax.optimization_barrier((received, part))
     pair = (message[0].astype(F32) + received.astype(F32)).astype(BF16)
     axes = ("lat", "ring")
@@ -724,7 +737,7 @@
     )(parts.reshape(group, chunk, LANES))
     mine = lax.all_to_all(copies.reshape(half_rows, LANES), axes, 0, 0, tiled=True)
     other = lax.ppermute(mine, "core", swap)
-    last_part = half_features(middle, fore_weight, hid, own_blend, lift_right, mine)
+    last_part = half_features(middle, fore_weight, hid, own_blend, lifted, side_lifted, mine)
     scale = 1.0 / math.sqrt(rows * lat_count * cols * lon_count)
 
     def finish(*refs):

time: 53.3 us -> 54.9 us (1.030)
  waiting for transfers between devices: 0.47 us -> 3.17 us
  starting transfers between devices: 9.52 us -> 8.63 us
    ppermute x2 -> x3, waiting for transfers between devices: 0.01 us -> 1.79 us  [the longest x1 1.79 us: on_device(): got_late = lax.ppermute(to_late, 'lat', late)]
    ppermute x1, starting transfers between devices: 2.55 us -> 1.68 us  [on_device(): got_far = lax.ppermute(far_message, lon, outer)]
    ppermute x1, waiting for transfers between devices: 0.01 us -> 0.56 us  [on_device(): got_far = lax.ppermute(far_message, lon, outer)]
    ppermute x2 -> x3, starting transfers between devices: 6.4 us -> 6.8 us  [the longest x1 4.84 us: on_device(): got_early = lax.ppermute(to_early, 'lat', early)]
  transfers between devices with their start and end apart: 6 -> 7, of which waited for: 1 -> 4; matrix products, arithmetic and copies ran while one was open for 0% -> 0% of each run, Pallas kernels for 14% -> 13%
where the time goes in v3:
time: 54.9 us; the launch traced here: 54.6 us
  blocking collectives  28 us (51%)
  Pallas kernels  13.9 us (25%)
  starting transfers between devices  8.63 us (16%)
  waiting for transfers between devices  3.17 us (6%)
  between operations  0.75 us (1%)
    all_to_all x1, blocking collectives, on_device(): parts = lax.all_to_all(pair, axes, 0, 0, tiled=True)  15.1 us
    all_to_all x1, blocking collectives, on_device(): lax.all_to_all(copies.reshape(half_rows, LANES), axes, 0, 0, tiled=True)  12.9 us
    ppermute x1, starting transfers between devices, on_device(): got_early = lax.ppermute(to_early, 'lat', early)  4.84 us
    pallas_call x1, Pallas kernels, on_device(): pl.pallas_call(body, out_specs=[vmem] * 4, out_shape=[jax.ShapeDtypeStruc...  4.31 us
    pallas_call x1, Pallas kernels, on_device(): pl.pallas_call(back_body, out_shape=[jax.ShapeDtypeStruct((2 * pairs, wid...  2.67 us
    pallas_call x1, Pallas kernels, on_device(): pl.pallas_call(prepare_kernel, out_shape=[jax.ShapeDtypeStruct((3, 2, (pa...  2.43 us
    pallas_call x2, Pallas kernels, half_features(): pl.pallas_call(body, out_shape=jax.ShapeDtypeStruct((rows // 2, cols, hid...  2.23 us
    ppermute x1, waiting for transfers between devices, on_device(): got_late = lax.ppermute(to_late, 'lat', late)  1.79 us
  transfers between devices with their start and end apart: 7, of which 4 were waited for; matrix products, arithmetic and copies ran while one was open for 0% of the time, Pallas kernels for 13%

profile of v3, /device:TPU:0, one launch (start us, length us, event | category | flops | bytes accessed | tf_op | source)
XLA Modules:
  0.0 54.6 jit_solution(9137378357629833112)
XLA Ops:
  0.6 0.8 %pack.1 = (bf16[5,8,128]{2,1,0:T(8,128)(2,1)S(1)}, bf16[4,8,128]{2,1,0:T(8,128)(2,1)S(1)}, bf16[4,8,128]{2,1,0:T(8,128)(2,1)S(1)}, bf16[4,8,128]{2,1,0:T(8,128)(...) custom-call(bf16[4,8,73]{2,1,0:T(8,128)(2,1)} %bitcast.22, ...), custom_call_target="tpu_custom_call" | custom-call | tf_op jit(solution)/shard_map/pack/pallas_call | solution.py:597
  1.4 4.8 %collective-permute-start = (bf16[4,8,128]{2,1,0:T(8,128)(2,1)S(1)}, bf16[4,8,128]{2,1,0:T(8,128)(2,1)S(1)}, u32[]{:S(2)}, u32[]{:S(2)}) collective-permute-start(bf16[4,8,128]{2,1,0:T(8,128)(2,1)S(1)} %get-tuple-element.41), channel_id=1, source_target_pairs={{0,8},{24,16},{1,9},{25,17},{2,10},{26,18},{3,11},{27,19},{4,12},{... | collective-permute-start | bytes 24584 | tf_op jit(solution)/shard_map/ppermute | solution.py:616
  6.3 0.7 %collective-permute-start.1 = (bf16[4,8,128]{2,1,0:T(8,128)(2,1)S(1)}, bf16[4,8,128]{2,1,0:T(8,128)(2,1)S(1)}, u32[]{:S(2)}, u32[]{:S(2)}) collective-permute-start(bf16[4,8,128]{2,1,0:T(8,128)(2,1)S(1)} %get-tuple-element.42), channel_id=1, source_target_pairs={{8,16},{16,8},{9,17},{17,9},{10,18},{18,10},{11,19},{19,11},{12,20... | collective-permute-start | bytes 24584 | tf_op jit(solution)/shard_map/ppermute | solution.py:617
  6.9 1.3 %collective-permute-start.2 = (bf16[4,8,128]{2,1,0:T(8,128)(2,1)S(1)}, bf16[4,8,128]{2,1,0:T(8,128)(2,1)S(1)}, u32[]{:S(2)}, u32[]{:S(2)}) collective-permute-start(bf16[4,8,128]{2,1,0:T(8,128)(2,1)S(1)} %get-tuple-element.43), channel_id=1, source_target_pairs={{8,0},{16,24},{9,1},{17,25},{10,2},{18,26},{11,3},{19,27},{12,4},{... | collective-permute-start | bytes 24584 | tf_op jit(solution)/shard_map/ppermute | solution.py:618
  8.2 2.4 %prepare.1 = (bf16[3,2,2592,128]{3,2,1,0:T(8,128)(2,1)S(1)}, bf16[1536,256]{1,0:T(8,128)(2,1)S(1)}, bf16[1536,256]{1,0:T(8,128)(2,1)S(1)}, bf16[256,2048]{1,0:T(...) custom-call(bf16[32,128,128]{2,1,0:T(8,128)(2,1)} %cot_hbm.1, ...), custom_call_target="tpu_custom_call" | custom-call | tf_op jit(solution)/shard_map/prepare/pallas_call | solution.py:620
  10.7 0.0 collective-permute-done.early_ref
  10.7 0.0 collective-permute-done.1.outer_ref
  10.7 1.8 %collective-permute-done.2.late_ref = bf16[4,8,128]{2,1,0:T(8,128)(2,1)S(1)} collective-permute-done((bf16[4,8,128]{2,1,0:T(8,128)(2,1)S(1)}, bf16[4,8,128]{2,1,0:T(8,128)(2,1)S(1)}, u32[]{:S(2)}, u32[]{:S(2)}) %collective-permute-start.2) | collective-permute-done | bytes 8224 | tf_op jit(solution)/shard_map/ppermute | solution.py:618
  12.5 1.7 %collective-permute-start.3 = (bf16[6,8,128]{2,1,0:T(8,128)(2,1)S(1)}, bf16[6,8,128]{2,1,0:T(8,128)(2,1)S(1)}, u32[]{:S(2)}, u32[]{:S(2)}) collective-permute-start(bf16[6,8,128]{2,1,0:T(8,128)(2,1)S(1)} %get-tuple-element.45), channel_id=1, source_target_pairs={{0,7},{1,2},{2,1},{3,4},{4,3},{5,6},{6,5},{7,0},{8,15},{9,10},{10,... | collective-permute-start | bytes 36872 | tf_op jit(solution)/shard_map/ppermute | solution.py:652
  14.2 0.1 collective-permute-start.4
  14.3 2.7 %back_hidden.1 = (f32[34,144,128]{2,1,0:T(8,128)S(1)}, bf16[2,240,384]{2,1,0:T(8,128)(2,1)S(1)}, f32[288,128]{1,0:T(8,128)S(1)}, f32[272,384]{1,0:T(8,128)S(1)},...) custom-call(s32[1,32]{1,0:T(1,128)S(1)} %get-tuple-element.51.refs_0_, f32[1,32]{1,0:T(1,128)S(1)} %get-tuple-element.52.refs_1_, ...), custom_call_target="tpu_custom_call" | custom-call | tf_op jit(solution)/shard_map/back_hidden/pallas_call | solution.py:660
  16.9 0.6 %collective-permute-done.3.refs_0_ = bf16[6,8,128]{2,1,0:T(8,128)(2,1)S(1)} collective-permute-done((bf16[6,8,128]{2,1,0:T(8,128)(2,1)S(1)}, bf16[6,8,128]{2,1,0:T(8,128)(2,1)S(1)}, u32[]{:S(2)}, u32[]{:S(2)}) %collective-permute-start.3) | collective-permute-done | bytes 12320 | tf_op jit(solution)/shard_map/ppermute | solution.py:652
  17.5 0.0 collective-permute-done.4.refs_1_
  17.5 4.3 %tile.1 = (bf16[3,2,2176,128]{3,2,1,0:T(8,128)(2,1)S(1)}, bf16[128,48]{1,0:T(8,128)(2,1)S(1)}, f32[288,128]{1,0:T(8,128)S(1)}, bf16[2,1024,128]{2,1,0:T(8,128)(2,1)S(1)}) custom-call(bf16[6,8,128]{2,1,0:T(8,128)(2,1)S(1)} %collective-permute-done.3.refs_0_, bf16[6,8,128]{2,1,0:T(8,128)(2,1)S(1)} %collective-permute-done.4.refs_1_, ...), custom_call_target="tpu_custom_call" | custom-call | tf_op jit(solution)/shard_map/tile/pallas_call | solution.py:689
  21.8 0.1 collective-permute-start.5
  21.9 1.1 %features_0.1.refs_4_ = bf16[16,128,128]{2,1,0:T(8,128)(2,1)S(1)} custom-call(bf16[1536,256]{1,0:T(8,128)(2,1)S(1)} %get-tuple-element.64.refs_0_, bf16[3,2,2176,128]{3,2,1,0:T(8,128)(2,1)S(1)} %get-tuple-element.65.refs_1_, bf16[128,48]{1,0:T(8,128)(2,1)S(1)} %get-tuple-element.66.refs_2_, f32[288,128]{1,0:T(8,128)S(1)} %get-tuple-element.67.refs_3_, ...), custom_call_target="tpu_custom_call" | custom-call | tf_op jit(solution)/shard_map/features_0/pallas_call | solution.py:716
  23.0 0.4 collective-permute-done.5
  23.4 0.1 fusion
  23.5 15.1 %all_to_all.17.in_ref = bf16[16,64,128]{2,1,0:T(8,128)(2,1)S(1)} all-to-all(bf16[16,64,128]{2,1,0:T(8,128)(2,1)S(1)} %bitcast.19), channel_id=1, replica_groups=mesh['lat'=4,'ring'=4,'core'=2] {'lat','ring'}, dimensions={0} | all-to-all | bytes 524288 | tf_op jit(solution)/shard_map/all_to_all | solution.py:731
  38.7 12.9 %all_to_all.18 = bf16[16,64,128]{2,1,0:T(8,128)(2,1)S(1)} all-to-all(bf16[16,64,128]{2,1,0:T(8,128)(2,1)S(1)} %sum_chunks.1), channel_id=1, replica_groups=mesh['lat'=4,'ring'=4,'core'=2] {'lat','ring'}, dimensions={0} | all-to-all | bytes 524288 | tf_op jit(solution)/shard_map/all_to_all | solution.py:738
  51.6 0.0 collective-permute-start.6
  51.6 1.1 %features_8.1.refs_5_ = bf16[16,128,128]{2,1,0:T(8,128)(2,1)S(1)} custom-call(bf16[1536,256]{1,0:T(8,128)(2,1)S(1)} %get-tuple-element.64.refs_0_, bf16[3,2,2176,128]{3,2,1,0:T(8,128)(2,1)S(1)} %get-tuple-element.65.refs_1_, bf16[128,48]{1,0:T(8,128)(2,1)S(1)} %get-tuple-element.66.refs_2_, f32[288,128]{1,0:T(8,128)S(1)} %get-tuple-element.67.refs_3_, ...), custom_call_target="tpu_custom_call" | custom-call | tf_op jit(solution)/shard_map/features_8/pallas_call | solution.py:716
  52.7 0.4 collective-permute-done.6.refs_1_
  53.1 1.4 %finish.1 = (bf16[32,128,128]{2,1,0:T(8,128)(2,1)}, f32[73,128]{1,0:T(8,128)}, f32[9,128,128]{2,1,0:T(8,128)}, f32[9,128,128]{2,1,0:T(8,128)}) custom-call(bf16[1024,128]{1,0:T(8,128)(2,1)S(1)} %bitcast.18, bf16[1024,128]{1,0:T(8,128)(2,1)S(1)} %collective-permute-done.6.refs_1_, bf16[128,128]{1,0:T(8,128)(2,1)S(1)} %get-tuple-element.44.ready_ref.refs_9_.refs_4_.refs_2_, ...), custom_call_target="tpu_custom_call" | custom-call | tf_op jit(solution)/shard_map/finish/pallas_call | solution.py:746
  (3 shorter events, 0.1 us)
Async XLA Ops:
  1.4 9.3 %collective-permute-start = (bf16[4,8,128]{2,1,0:T(8,128)(2,1)S(1)}, bf16[4,8,128]{2,1,0:T(8,128)(2,1)S(1)}, u32[]{:S(2)}, u32[]{:S(2)}) collective-permute-start(bf16[4,8,128]{2,1,0:T(8,128)(2,1)S(1)} %get-tuple-element.41), channel_id=1, source_target_pairs={{0,8},{24,16},{1,9},{25,17},{2,10},{26,18},{3,11},{27,19},{4,12},{... | collective-permute-start | bytes 24584 | tf_op jit(solution)/shard_map/ppermute | solution.py:616
  6.3 4.4 %collective-permute-start.1 = (bf16[4,8,128]{2,1,0:T(8,128)(2,1)S(1)}, bf16[4,8,128]{2,1,0:T(8,128)(2,1)S(1)}, u32[]{:S(2)}, u32[]{:S(2)}) collective-permute-start(bf16[4,8,128]{2,1,0:T(8,128)(2,1)S(1)} %get-tuple-element.42), channel_id=1, source_target_pairs={{8,16},{16,8},{9,17},{17,9},{10,18},{18,10},{11,19},{19,11},{12,20... | collective-permute-start | bytes 24584 | tf_op jit(solution)/shard_map/ppermute | solution.py:617
  6.9 5.5 %collective-permute-start.2 = (bf16[4,8,128]{2,1,0:T(8,128)(2,1)S(1)}, bf16[4,8,128]{2,1,0:T(8,128)(2,1)S(1)}, u32[]{:S(2)}, u32[]{:S(2)}) collective-permute-start(bf16[4,8,128]{2,1,0:T(8,128)(2,1)S(1)} %get-tuple-element.43), channel_id=1, source_target_pairs={{8,0},{16,24},{9,1},{17,25},{10,2},{18,26},{11,3},{19,27},{12,4},{... | collective-permute-start | bytes 24584 | tf_op jit(solution)/shard_map/ppermute | solution.py:618
  12.5 5.0 %collective-permute-start.3 = (bf16[6,8,128]{2,1,0:T(8,128)(2,1)S(1)}, bf16[6,8,128]{2,1,0:T(8,128)(2,1)S(1)}, u32[]{:S(2)}, u32[]{:S(2)}) collective-permute-start(bf16[6,8,128]{2,1,0:T(8,128)(2,1)S(1)} %get-tuple-element.45), channel_id=1, source_target_pairs={{0,7},{1,2},{2,1},{3,4},{4,3},{5,6},{6,5},{7,0},{8,15},{9,10},{10,... | collective-permute-start | bytes 36872 | tf_op jit(solution)/shard_map/ppermute | solution.py:652
  14.2 3.3 %collective-permute-start.4 = (bf16[6,8,128]{2,1,0:T(8,128)(2,1)S(1)}, bf16[6,8,128]{2,1,0:T(8,128)(2,1)S(1)}, u32[]{:S(2)}, u32[]{:S(2)}) collective-permute-start(bf16[6,8,128]{2,1,0:T(8,128)(2,1)S(1)} %get-tuple-element.46), channel_id=1, source_target_pairs={{0,1},{1,0},{2,3},{3,2},{4,5},{5,4},{6,7},{7,6},{8,9},{9,8},{10,11... | collective-permute-start | bytes 36872 | tf_op jit(solution)/shard_map/ppermute | solution.py:653
  21.8 1.6 %collective-permute-start.5 = (bf16[1024,128]{1,0:T(8,128)(2,1)S(1)}, bf16[1024,128]{1,0:T(8,128)(2,1)S(1)}, u32[]{:S(2)}, u32[]{:S(2)}) collective-permute-start(bf16[1024,128]{1,0:T(8,128)(2,1)S(1)} %slice_bitcast_fusion), channel_id=1, source_target_pairs={{0,1},{1,0},{2,3},{3,2},{4,5},{5,4},{6,7},{7,6},{8,9},{9,8},{10,11... | collective-permute-start | bytes 786440 | tf_op jit(solution)/shard_map/ppermute | solution.py:724
  51.6 1.5 %collective-permute-start.6 = (bf16[1024,128]{1,0:T(8,128)(2,1)S(1)}, bf16[1024,128]{1,0:T(8,128)(2,1)S(1)}, u32[]{:S(2)}, u32[]{:S(2)}) collective-permute-start(bf16[1024,128]{1,0:T(8,128)(2,1)S(1)} %bitcast.16), channel_id=1, source_target_pairs={{0,1},{1,0},{2,3},{3,2},{4,5},{5,4},{6,7},{7,6},{8,9},{9,8},{10,11... | collective-permute-start | bytes 786440 | tf_op jit(solution)/shard_map/ppermute | solution.py:739

commit v4 on v3

--- a/solution.py
+++ b/solution.py
@@ -232,7 +232,7 @@
 
 def pack_kernel(cells_hbm, rsrc_hbm, rfrac_hbm, csrc_hbm, cfrac_hbm, *space):
     sources = (cells_hbm, rsrc_hbm, rfrac_hbm, csrc_hbm, cfrac_hbm)
-    own_ref, early_ref, outer_ref, late_ref, *lines, cells_ref, out_ref, sems = space
+    own_ref, outer_ref, inner_ref, *lines, cells_ref, out_ref, sems = space
     targets = (cells_ref, *lines)
     copies = [
         pltpu.make_async_copy(source, target, sems.at[n])
@@ -264,10 +264,8 @@
     for j in range(depth + 1):
         own_ref[j] = own[j].astype(BF16)
     for j in range(ROW_HALO + 1):
-        inner = jnp.where(even, to_next[j], to_last[j]).astype(BF16)
-        early_ref[j] = inner
         outer_ref[j] = jnp.where(even, to_last[j], to_next[j]).astype(BF16)
-        late_ref[j] = inner
+        inner_ref[j] = jnp.where(even, to_next[j], to_last[j]).astype(BF16)
 
 
 def main_kernel(
@@ -399,16 +397,14 @@
             place_hidden(t)
     back = jnp.dot(col_t, delta_ref[...], preferred_element_type=F32)
     back = back[:taps] + back[taps:]
-    for b in range(3):
-        grads[b] = grads[b] + second_gradient(1, b)
-
     width = rows_ref.shape[2]
     used = 2 * pairs * band_cols
     blank = jnp.zeros((2, width - used, back_ref.shape[2]), BF16)
     back_ref[:, used:width] = blank
     back_ref[:, width + used :] = blank
     nothing = jnp.zeros((SPAN, LANES), F32)
-    for p in range(pairs):
+
+    def place_back(p):
         for b in range(4):
             lines = []
             for t in (2 * p, 2 * p + 1):
@@ -423,12 +419,27 @@
                 at = side * width + p * SPAN
                 back_ref[0, at : at + SPAN, column] = one
                 back_ref[1, at : at + SPAN, column] = two
+
+    def send_second(b):
+        for a in range(3):
+            upper = grads[b][:LANES, a * LANES : (a + 1) * LANES]
+            lower = grads[b][LANES:, (a + 1) * LANES : (a + 2) * LANES]
+            send((a * 3 + b) * LANES, (upper + lower).T)
+
+    share = -(-pairs // 3)
     side_hi, side_lo = turned_rows(side_mixed, width)
+    for b in range(3):
+        grads[b] = grads[b] + second_gradient(1, b)
+        for p in range(b * share, min((b + 1) * share, pairs)):
+            place_back(p)
     upper = jnp.concatenate([rows_ref[0], side_hi], axis=1)
     lower = jnp.concatenate([rows_ref[1], side_lo], axis=1)
     g = jnp.dot(jnp.concatenate([upper, lower], axis=0), back_ref[0], preferred_element_type=F32)
+    send_second(0)
+    send_second(1)
     g = g[: 3 * GRAD_ROWS] + g[3 * GRAD_ROWS :]
     g = g + jnp.dot(upper, back_ref[1], preferred_element_type=F32)
+    send_second(2)
     for a in range(3):
         line = g[a * GRAD_ROWS : (a + 1) * GRAD_ROWS]
         for b in range(3):
@@ -438,24 +449,14 @@
     if 2 * half_rows > tail:
         send(tail, jnp.zeros((2 * half_rows - tail, LANES), F32))
 
-    for b in range(3):
-        for a in range(3):
-            upper = grads[b][:LANES, a * LANES : (a + 1) * LANES]
-            lower = grads[b][LANES:, (a + 1) * LANES : (a + 2) * LANES]
-            send((a * 3 + b) * LANES, (upper + lower).T)
-
-
-def join_kernel(own_ref, early_ref, outer_ref, late_ref, ready_ref, before_ref, after_ref, far_ref, near_ref):
+
+def join_kernel(own_ref, outer_ref, inner_ref, ready_ref, before_ref, after_ref, far_ref, near_ref):
     band_rows, band_cols = own_ref.shape[0] - 1, own_ref.shape[1]
     lat = lax.axis_index("lat")
     even = lax.rem(lat, 2) == 0
-    sent_late = lax.rem(lat + lat // 2, 2) == 0
     first = lax.axis_index("core") == 0
     outer = [outer_ref[j].astype(F32) for j in range(ROW_HALO + 1)]
-    inner = [
-        jnp.where(sent_late, late_ref[j].astype(F32), early_ref[j].astype(F32))
-        for j in range(ROW_HALO + 1)
-    ]
+    inner = [inner_ref[j].astype(F32) for j in range(ROW_HALO + 1)]
     before = [jnp.where(even, v, w) for v, w in zip(outer, inner)]
     after = [jnp.where(even, w, v) for v, w in zip(outer, inner)]
     own = [own_ref[j].astype(F32) for j in range(band_rows + 1)]
@@ -594,11 +595,11 @@
         *row_line,
         *col_line,
     )
-    own, to_early, to_outer, to_late, *lines = pl.pallas_call(
+    own, to_outer, to_inner, *lines = pl.pallas_call(
         pack_kernel,
         in_specs=[far] * 5,
         out_shape=[jax.ShapeDtypeStruct((band_rows + 1, band_cols, LANES), BF16)]
-        + [jax.ShapeDtypeStruct((ROW_HALO + 1, band_cols, LANES), BF16)] * 3
+        + [jax.ShapeDtypeStruct((ROW_HALO + 1, band_cols, LANES), BF16)] * 2
         + [jax.ShapeDtypeStruct(x.shape, x.dtype) for x in pack_inputs[1:]],
         scratch_shapes=[
             pltpu.VMEM(pack_inputs[0].shape, BF16),
@@ -609,13 +610,11 @@
         name="pack",
     )(*(from_hbm(x) for x in pack_inputs))
     row_line, col_line = lines[:2], lines[2:]
-    early = [(i, i ^ 1) for i in range(lat_count) if (i + i // 2) % 2 == 0]
-    late = [(j, i) for i, j in early]
+    inner = [(i, i ^ 1) for i in range(lat_count)]
     outer = [(i, i + 1) for i in range(1, lat_count - 1, 2)]
     outer = outer + [(j, i) for i, j in outer]
-    got_early = lax.ppermute(to_early, "lat", early)
     got_outer = lax.ppermute(to_outer, "lat", outer)
-    got_late = lax.ppermute(to_late, "lat", late)
+    got_inner = lax.ppermute(to_inner, "lat", inner)
 
     shift, back_weight, fore_weight, turned, first_weight, cot, near_w1, embed = pl.pallas_call(
         prepare_kernel,
@@ -645,7 +644,7 @@
         + [jax.ShapeDtypeStruct((depth // 2 + 1, band_cols, LANES), BF16)] * 2,
         compiler_params=params,
         name="join",
-    )(own, got_early, got_outer, got_late, embed)
+    )(own, got_outer, got_inner, embed)
     lon = ("ring", "core")
     inner = [(i, i ^ 1) for i in range(lon_count)]
     outer = [(i, (i + (1 if i % 2 else -1)) % lon_count) for i in range(lon_count)]

time: 54.9 us -> 53.3 us (0.971)
  waiting for transfers between devices: 3.17 us -> 0.47 us
  starting transfers between devices: 8.63 us -> 9.53 us
    ppermute x2 -> x1, waiting for transfers between devices: 1.79 us -> 0.01 us  [on_device(): got_inner = lax.ppermute(to_inner, 'lat', inner)]
    ppermute x1, starting transfers between devices: 1.68 us -> 2.55 us  [on_device(): got_far = lax.ppermute(far_message, lon, outer)]
    ppermute x1, waiting for transfers between devices: 0.56 us -> 0.01 us  [on_device(): got_far = lax.ppermute(far_message, lon, outer)]
    ppermute x2 -> x1, starting transfers between devices: 6.13 us -> 5.74 us  [on_device(): got_inner = lax.ppermute(to_inner, 'lat', inner)]
  transfers between devices with their start and end apart: 7 -> 6, of which waited for: 4 -> 1; matrix products, arithmetic and copies ran while one was open for 0% -> 0% of each run, Pallas kernels for 13% -> 14%
where the time goes in v4:
time: 53.3 us; the launch traced here: 53 us
  blocking collectives  28.3 us (53%)
  Pallas kernels  13.9 us (26%)
  starting transfers between devices  9.53 us (18%)
  between operations  0.72 us (1%)
    all_to_all x1, blocking collectives, on_device(): parts = lax.all_to_all(pair, axes, 0, 0, tiled=True)  15.3 us
    all_to_all x1, blocking collectives, on_device(): lax.all_to_all(copies.reshape(half_rows, LANES), axes, 0, 0, tiled=True)  13 us
    ppermute x1, starting transfers between devices, on_device(): got_inner = lax.ppermute(to_inner, 'lat', inner)  5.74 us
    pallas_call x1, Pallas kernels, on_device(): pl.pallas_call(body, out_specs=[vmem] * 4, out_shape=[jax.ShapeDtypeStruc...  4.32 us
    pallas_call x1, Pallas kernels, on_device(): pl.pallas_call(back_body, out_shape=[jax.ShapeDtypeStruct((2 * pairs, wid...  2.67 us
    ppermute x1, starting transfers between devices, on_device(): got_far = lax.ppermute(far_message, lon, outer)  2.55 us
    pallas_call x1, Pallas kernels, on_device(): pl.pallas_call(prepare_kernel, out_shape=[jax.ShapeDtypeStruct((3, 2, (pa...  2.42 us
    pallas_call x2, Pallas kernels, half_features(): pl.pallas_call(body, out_shape=jax.ShapeDtypeStruct((rows // 2, cols, hid...  2.22 us
  transfers between devices with their start and end apart: 6, of which 1 were waited for; matrix products, arithmetic and copies ran while one was open for 0% of the time, Pallas kernels for 14%

profile of v4, /device:TPU:0, one launch (start us, length us, event | category | flops | bytes accessed | tf_op | source)
XLA Modules:
  0.0 53.0 jit_solution(12846726758555074033)
XLA Ops:
  0.6 0.8 %pack.1 = (bf16[5,8,128]{2,1,0:T(8,128)(2,1)S(1)}, bf16[4,8,128]{2,1,0:T(8,128)(2,1)S(1)}, bf16[4,8,128]{2,1,0:T(8,128)(2,1)S(1)}, s32[1,32]{1,0:T(1,128)S(1)}, ...) custom-call(bf16[4,8,73]{2,1,0:T(8,128)(2,1)} %bitcast.22, s32[1,32]{1,0:T(1,128)} %bitcast.23, ...), custom_call_target="tpu_custom_call" | custom-call | tf_op jit(solution)/shard_map/pack/pallas_call | solution.py:598
  1.4 0.7 %collective-permute-start = (bf16[4,8,128]{2,1,0:T(8,128)(2,1)S(1)}, bf16[4,8,128]{2,1,0:T(8,128)(2,1)S(1)}, u32[]{:S(2)}, u32[]{:S(2)}) collective-permute-start(bf16[4,8,128]{2,1,0:T(8,128)(2,1)S(1)} %get-tuple-element.40), channel_id=1, source_target_pairs={{8,16},{16,8},{9,17},{17,9},{10,18},{18,10},{11,19},{19,11},{12,20... | collective-permute-start | bytes 24584 | tf_op jit(solution)/shard_map/ppermute | solution.py:616
  2.1 5.7 %collective-permute-start.1 = (bf16[4,8,128]{2,1,0:T(8,128)(2,1)S(1)}, bf16[4,8,128]{2,1,0:T(8,128)(2,1)S(1)}, u32[]{:S(2)}, u32[]{:S(2)}) collective-permute-start(bf16[4,8,128]{2,1,0:T(8,128)(2,1)S(1)} %get-tuple-element.41), channel_id=1, source_target_pairs={{0,8},{8,0},{16,24},{24,16},{1,9},{9,1},{17,25},{25,17},{2,10},{10... | collective-permute-start | bytes 24584 | tf_op jit(solution)/shard_map/ppermute | solution.py:617
  7.8 2.4 %prepare.1 = (bf16[3,2,2592,128]{3,2,1,0:T(8,128)(2,1)S(1)}, bf16[1536,256]{1,0:T(8,128)(2,1)S(1)}, bf16[1536,256]{1,0:T(8,128)(2,1)S(1)}, bf16[256,2048]{1,0:T(...) custom-call(bf16[32,128,128]{2,1,0:T(8,128)(2,1)} %cot_hbm.1, ...), custom_call_target="tpu_custom_call" | custom-call | tf_op jit(solution)/shard_map/prepare/pallas_call | solution.py:619
  10.3 0.0 collective-permute-done.outer_ref
  10.3 0.0 collective-permute-done.1.inner_ref
  10.3 2.5 %collective-permute-start.2 = (bf16[6,8,128]{2,1,0:T(8,128)(2,1)S(1)}, bf16[6,8,128]{2,1,0:T(8,128)(2,1)S(1)}, u32[]{:S(2)}, u32[]{:S(2)}) collective-permute-start(bf16[6,8,128]{2,1,0:T(8,128)(2,1)S(1)} %get-tuple-element.43), channel_id=1, source_target_pairs={{0,7},{1,2},{2,1},{3,4},{4,3},{5,6},{6,5},{7,0},{8,15},{9,10},{10,... | collective-permute-start | bytes 36872 | tf_op jit(solution)/shard_map/ppermute | solution.py:651
  12.9 0.0 collective-permute-start.3
  12.9 2.7 %back_hidden.1 = (f32[34,144,128]{2,1,0:T(8,128)S(1)}, bf16[2,240,384]{2,1,0:T(8,128)(2,1)S(1)}, f32[288,128]{1,0:T(8,128)S(1)}, f32[272,384]{1,0:T(8,128)S(1)},...) custom-call(s32[1,32]{1,0:T(1,128)S(1)} %get-tuple-element.49.refs_0_, f32[1,32]{1,0:T(1,128)S(1)} %get-tuple-element.50.refs_1_, ...), custom_call_target="tpu_custom_call" | custom-call | tf_op jit(solution)/shard_map/back_hidden/pallas_call | solution.py:659
  15.5 0.0 collective-permute-done.2.refs_0_
  15.5 0.0 collective-permute-done.3.refs_1_
  15.5 4.3 %tile.1 = (bf16[3,2,2176,128]{3,2,1,0:T(8,128)(2,1)S(1)}, bf16[128,48]{1,0:T(8,128)(2,1)S(1)}, f32[288,128]{1,0:T(8,128)S(1)}, bf16[2,1024,128]{2,1,0:T(8,128)(2,1)S(1)}) custom-call(bf16[6,8,128]{2,1,0:T(8,128)(2,1)S(1)} %collective-permute-done.2.refs_0_, bf16[6,8,128]{2,1,0:T(8,128)(2,1)S(1)} %collective-permute-done.3.refs_1_, ...), custom_call_target="tpu_custom_call" | custom-call | tf_op jit(solution)/shard_map/tile/pallas_call | solution.py:688
  19.9 0.6 %collective-permute-start.4 = (bf16[1024,128]{1,0:T(8,128)(2,1)S(1)}, bf16[1024,128]{1,0:T(8,128)(2,1)S(1)}, u32[]{:S(2)}, u32[]{:S(2)}) collective-permute-start(bf16[1024,128]{1,0:T(8,128)(2,1)S(1)} %slice_bitcast_fusion), channel_id=1, source_target_pairs={{0,1},{1,0},{2,3},{3,2},{4,5},{5,4},{6,7},{7,6},{8,9},{9,8},{10,11... | collective-permute-start | bytes 786440 | tf_op jit(solution)/shard_map/ppermute | solution.py:723
  20.5 1.1 %features_0.1.refs_4_ = bf16[16,128,128]{2,1,0:T(8,128)(2,1)S(1)} custom-call(bf16[1536,256]{1,0:T(8,128)(2,1)S(1)} %get-tuple-element.62.refs_0_, bf16[3,2,2176,128]{3,2,1,0:T(8,128)(2,1)S(1)} %get-tuple-element.63.refs_1_, bf16[128,48]{1,0:T(8,128)(2,1)S(1)} %get-tuple-element.64.refs_2_, f32[288,128]{1,0:T(8,128)S(1)} %get-tuple-element.65.refs_3_, ...), custom_call_target="tpu_custom_call" | custom-call | tf_op jit(solution)/shard_map/features_0/pallas_call | solution.py:715
  21.6 0.0 collective-permute-done.4
  21.6 0.1 fusion
  21.7 15.3 %all_to_all.17.in_ref = bf16[16,64,128]{2,1,0:T(8,128)(2,1)S(1)} all-to-all(bf16[16,64,128]{2,1,0:T(8,128)(2,1)S(1)} %bitcast.19), channel_id=1, replica_groups=mesh['lat'=4,'ring'=4,'core'=2] {'lat','ring'}, dimensions={0} | all-to-all | bytes 524288 | tf_op jit(solution)/shard_map/all_to_all | solution.py:730
  37.1 13.0 %all_to_all.18 = bf16[16,64,128]{2,1,0:T(8,128)(2,1)S(1)} all-to-all(bf16[16,64,128]{2,1,0:T(8,128)(2,1)S(1)} %sum_chunks.1), channel_id=1, replica_groups=mesh['lat'=4,'ring'=4,'core'=2] {'lat','ring'}, dimensions={0} | all-to-all | bytes 524288 | tf_op jit(solution)/shard_map/all_to_all | solution.py:737
  50.1 0.0 collective-permute-start.5
  50.1 1.1 %features_8.1.refs_5_ = bf16[16,128,128]{2,1,0:T(8,128)(2,1)S(1)} custom-call(bf16[1536,256]{1,0:T(8,128)(2,1)S(1)} %get-tuple-element.62.refs_0_, bf16[3,2,2176,128]{3,2,1,0:T(8,128)(2,1)S(1)} %get-tuple-element.63.refs_1_, bf16[128,48]{1,0:T(8,128)(2,1)S(1)} %get-tuple-element.64.refs_2_, f32[288,128]{1,0:T(8,128)S(1)} %get-tuple-element.65.refs_3_, ...), custom_call_target="tpu_custom_call" | custom-call | tf_op jit(solution)/shard_map/features_8/pallas_call | solution.py:715
  51.2 0.4 collective-permute-done.5.refs_1_
  51.6 1.4 %finish.1 = (bf16[32,128,128]{2,1,0:T(8,128)(2,1)}, f32[73,128]{1,0:T(8,128)}, f32[9,128,128]{2,1,0:T(8,128)}, f32[9,128,128]{2,1,0:T(8,128)}) custom-call(bf16[1024,128]{1,0:T(8,128)(2,1)S(1)} %bitcast.18, bf16[1024,128]{1,0:T(8,128)(2,1)S(1)} %collective-permute-done.5.refs_1_, bf16[128,128]{1,0:T(8,128)(2,1)S(1)} %get-tuple-element.42.ready_ref.refs_9_.refs_4_.refs_2_, ...), custom_call_target="tpu_custom_call" | custom-call | tf_op jit(solution)/shard_map/finish/pallas_call | solution.py:745
  (3 shorter events, 0.1 us)
Async XLA Ops:
  1.4 8.8 %collective-permute-start = (bf16[4,8,128]{2,1,0:T(8,128)(2,1)S(1)}, bf16[4,8,128]{2,1,0:T(8,128)(2,1)S(1)}, u32[]{:S(2)}, u32[]{:S(2)}) collective-permute-start(bf16[4,8,128]{2,1,0:T(8,128)(2,1)S(1)} %get-tuple-element.40), channel_id=1, source_target_pairs={{8,16},{16,8},{9,17},{17,9},{10,18},{18,10},{11,19},{19,11},{12,20... | collective-permute-start | bytes 24584 | tf_op jit(solution)/shard_map/ppermute | solution.py:616
  2.1 8.2 %collective-permute-start.1 = (bf16[4,8,128]{2,1,0:T(8,128)(2,1)S(1)}, bf16[4,8,128]{2,1,0:T(8,128)(2,1)S(1)}, u32[]{:S(2)}, u32[]{:S(2)}) collective-permute-start(bf16[4,8,128]{2,1,0:T(8,128)(2,1)S(1)} %get-tuple-element.41), channel_id=1, source_target_pairs={{0,8},{8,0},{16,24},{24,16},{1,9},{9,1},{17,25},{25,17},{2,10},{10... | collective-permute-start | bytes 24584 | tf_op jit(solution)/shard_map/ppermute | solution.py:617
  10.3 5.2 %collective-permute-start.2 = (bf16[6,8,128]{2,1,0:T(8,128)(2,1)S(1)}, bf16[6,8,128]{2,1,0:T(8,128)(2,1)S(1)}, u32[]{:S(2)}, u32[]{:S(2)}) collective-permute-start(bf16[6,8,128]{2,1,0:T(8,128)(2,1)S(1)} %get-tuple-element.43), channel_id=1, source_target_pairs={{0,7},{1,2},{2,1},{3,4},{4,3},{5,6},{6,5},{7,0},{8,15},{9,10},{10,... | collective-permute-start | bytes 36872 | tf_op jit(solution)/shard_map/ppermute | solution.py:651
  12.9 2.7 %collective-permute-start.3 = (bf16[6,8,128]{2,1,0:T(8,128)(2,1)S(1)}, bf16[6,8,128]{2,1,0:T(8,128)(2,1)S(1)}, u32[]{:S(2)}, u32[]{:S(2)}) collective-permute-start(bf16[6,8,128]{2,1,0:T(8,128)(2,1)S(1)} %get-tuple-element.44), channel_id=1, source_target_pairs={{0,1},{1,0},{2,3},{3,2},{4,5},{5,4},{6,7},{7,6},{8,9},{9,8},{10,11... | collective-permute-start | bytes 36872 | tf_op jit(solution)/shard_map/ppermute | solution.py:652
  19.9 1.7 %collective-permute-start.4 = (bf16[1024,128]{1,0:T(8,128)(2,1)S(1)}, bf16[1024,128]{1,0:T(8,128)(2,1)S(1)}, u32[]{:S(2)}, u32[]{:S(2)}) collective-permute-start(bf16[1024,128]{1,0:T(8,128)(2,1)S(1)} %slice_bitcast_fusion), channel_id=1, source_target_pairs={{0,1},{1,0},{2,3},{3,2},{4,5},{5,4},{6,7},{7,6},{8,9},{9,8},{10,11... | collective-permute-start | bytes 786440 | tf_op jit(solution)/shard_map/ppermute | solution.py:723
  50.1 1.5 %collective-permute-start.5 = (bf16[1024,128]{1,0:T(8,128)(2,1)S(1)}, bf16[1024,128]{1,0:T(8,128)(2,1)S(1)}, u32[]{:S(2)}, u32[]{:S(2)}) collective-permute-start(bf16[1024,128]{1,0:T(8,128)(2,1)S(1)} %bitcast.16), channel_id=1, source_target_pairs={{0,1},{1,0},{2,3},{3,2},{4,5},{5,4},{6,7},{7,6},{8,9},{9,8},{10,11... | collective-permute-start | bytes 786440 | tf_op jit(solution)/shard_map/ppermute | solution.py:738

commit v5 on v4

--- a/solution.py
+++ b/solution.py
@@ -473,8 +473,27 @@
     near_ref[len(tall) // 2] = own[band_rows].astype(BF16)
 
 
+def leave_parts(source, target, sems, at):
+    count = sems.shape[0]
+    share = source.shape[0] // count
+    copies = [
+        pltpu.make_async_copy(
+            source.at[pl.ds(n * share, share)], target.at[pl.ds(at + n * share, share)], sems.at[n]
+        )
+        for n in range(count)
+    ]
+    for copy in copies:
+        copy.start()
+    return copies
+
+
 def features_kernel(weight_ref, hid_ref, own_ref, lifted_ref, side_lifted_ref, *refs, first):
-    feat_ref = refs[-1]
+    copies = []
+    if first:
+        _, earlier_ref, feat_ref, out_hbm, sems = refs
+        copies = leave_parts(earlier_ref, out_hbm, sems, 0)
+    else:
+        (feat_ref,) = refs
     rows, cols, _ = feat_ref.shape
     cells = own_ref.shape[1] // 6
     step = 4
@@ -496,6 +515,8 @@
                 piece = out[m * cols : (m + 1) * cols, q * LANES : (q + 1) * LANES]
                 own = lift[:, (2 * m + q) * LANES : (2 * m + q + 1) * LANES]
                 feat_ref[2 * (n + m) + q] = (own + piece).astype(BF16)
+    for copy in copies:
+        copy.wait()
 
 
 def reduce_kernel(in_ref, out_ref):
@@ -515,43 +536,36 @@
 
 
 def last_kernel(
-    mine_ref, other_ref, embed_ref, first_ref, upper_ref, lower_ref, feat_hbm, ge_hbm, g1_hbm, g2_hbm,
-    sum_ref, ge_ref, g1_ref, g2_ref, sems, *, scale
+    mine_ref, other_ref, embed_ref, first_ref, part_ref, begun_hbm, feat_hbm, ge_hbm, g1_hbm, g2_hbm,
+    sum_ref, ge_ref, g1_ref, g2_ref, feat_sems, g1_sems, g2_sems, ge_sem, *, scale
 ):
     core = lax.axis_index("core")
     half_rows = mine_ref.shape[0]
-    copies = []
-
-    def leave(source, target):
-        copies.append(pltpu.make_async_copy(source, target, sems.at[len(copies)]))
-        copies[-1].start()
-
-    count = upper_ref.shape[0]
-    leave(upper_ref, feat_hbm.at[pl.ds(0, count)])
-    leave(lower_ref, feat_hbm.at[pl.ds(count, count)])
+    copies = leave_parts(part_ref, feat_hbm, feat_sems, part_ref.shape[0])
     sum_ref[core] = mine_ref[...]
     sum_ref[1 - core] = other_ref[...]
 
     def read(at, count):
         return sum_ref[at // half_rows, at % half_rows : at % half_rows + count]
 
-    for a in range(3):
-        for tap in range(3 * a, 3 * a + 3):
-            g2_ref[tap] = read(tap * LANES, LANES).astype(F32) * scale
-        leave(g2_ref.at[pl.ds(3 * a, 3)], g2_hbm.at[pl.ds(3 * a, 3)])
+    def leave(source, target, sem):
+        copies.append(pltpu.make_async_copy(source, target, sem))
+        copies[-1].start()
+
+    for tap in range(9):
+        g2_ref[tap] = read(tap * LANES, LANES).astype(F32) * scale
+        leave(g2_ref.at[tap], g2_hbm.at[tap], g2_sems.at[tap])
     embed_t = embed_ref[...].astype(F32).T.astype(BF16)[:, :GRAD_ROWS]
     base = 9 * LANES
     g = jnp.concatenate([read(base + tap * GRAD_ROWS, GRAD_ROWS) for tap in range(9)], axis=1)
-    for a in range(3):
-        part = g[:, 3 * a * LANES : (3 * a + 3) * LANES]
-        out = jnp.dot(embed_t, part, preferred_element_type=F32) * scale
-        for b in range(3):
-            g1_ref[3 * a + b] = out[:, b * LANES : (b + 1) * LANES]
-        leave(g1_ref.at[pl.ds(3 * a, 3)], g1_hbm.at[pl.ds(3 * a, 3)])
     lift = read(base + 9 * GRAD_ROWS, GRAD_ROWS).astype(F32)
     lift = lift + jnp.dot(g, first_ref[...], preferred_element_type=F32)
     ge_ref[...] = lift[: ge_ref.shape[0]] * scale
-    leave(ge_ref, ge_hbm)
+    leave(ge_ref, ge_hbm, ge_sem)
+    out = jnp.dot(embed_t, g, preferred_element_type=F32) * scale
+    for tap in range(9):
+        g1_ref[tap] = out[:, tap * LANES : (tap + 1) * LANES]
+        leave(g1_ref.at[tap], g1_hbm.at[tap], g1_sems.at[tap])
     for copy in copies:
         copy.wait()
 
@@ -712,9 +726,13 @@
         def body(*refs):
             features_kernel(*refs, first=first)
 
+        half = jax.ShapeDtypeStruct((rows // 2, cols, hidden), BF16)
+        whole = jax.ShapeDtypeStruct((rows, cols, hidden), BF16)
         return pl.pallas_call(
             body,
-            out_shape=jax.ShapeDtypeStruct((rows // 2, cols, hidden), BF16),
+            out_specs=[vmem, far] if first else vmem,
+            out_shape=[half, whole] if first else half,
+            scratch_shapes=[pltpu.SemaphoreType.DMA((4,))] if first else [],
             compiler_params=params,
             name=f"features_{first}",
         )(*arrays)
@@ -736,7 +754,9 @@
     )(parts.reshape(group, chunk, LANES))
     mine = lax.all_to_all(copies.reshape(half_rows, LANES), axes, 0, 0, tiled=True)
     other = lax.ppermute(mine, "core", swap)
-    last_part = half_features(middle, fore_weight, hid, own_blend, lifted, side_lifted, mine)
+    last_part, features = half_features(
+        middle, fore_weight, hid, own_blend, lifted, side_lifted, mine, part
+    )
     scale = 1.0 / math.sqrt(rows * lat_count * cols * lon_count)
 
     def finish(*refs):
@@ -744,7 +764,9 @@
 
     features, grad_embed, grad_first, grad_second = pl.pallas_call(
         finish,
+        in_specs=[vmem] * 5 + [far],
         out_specs=[far] * 4,
+        input_output_aliases={5: 0},
         out_shape=[
             jax.ShapeDtypeStruct((rows, cols, hidden), BF16),
             jax.ShapeDtypeStruct((fields, hidden), F32),
@@ -756,11 +778,14 @@
             pltpu.VMEM((fields, hidden), F32),
             pltpu.VMEM((9, hidden, hidden), F32),
             pltpu.VMEM((9, hidden, hidden), F32),
+            pltpu.SemaphoreType.DMA((4,)),
             pltpu.SemaphoreType.DMA((9,)),
+            pltpu.SemaphoreType.DMA((9,)),
+            pltpu.SemaphoreType.DMA,
         ],
         compiler_params=params,
         name="finish",
-    )(mine, other, embed, first_weight, part, last_part)
+    )(mine, other, embed, first_weight, last_part, features)
     shape = (3, 3, hidden, hidden)
     return (features, grad_embed, grad_first.reshape(shape), grad_second.reshape(shape))
 

time: 53.3 us -> 53.8 us (level)
  Pallas kernels: 13.9 us -> 14.7 us
    pallas_call x3, Pallas kernels: 3.66 us -> 4.45 us  [the longest x2 2.8 us: half_features(): pl.pallas_call(body, out_specs=[vmem, far] if first else vmem, out_shape=...]
  transfers between devices with their start and end apart: 6 -> 6, of which waited for: 1 -> 0; matrix products, arithmetic and copies ran while one was open for 0% -> 0% of each run, Pallas kernels for 14% -> 15%
where the time goes in v5:
time: 53.8 us; the launch traced here: 53.4 us
  blocking collectives  28.3 us (53%)
  Pallas kernels  14.7 us (27%)
  starting transfers between devices  9.53 us (18%)
  between operations  0.73 us (1%)
    all_to_all x1, blocking collectives, on_device(): parts = lax.all_to_all(pair, axes, 0, 0, tiled=True)  15.3 us
    all_to_all x1, blocking collectives, on_device(): lax.all_to_all(copies.reshape(half_rows, LANES), axes, 0, 0, tiled=True)  13 us
    ppermute x1, starting transfers between devices, on_device(): got_inner = lax.ppermute(to_inner, 'lat', inner)  5.74 us
    pallas_call x1, Pallas kernels, on_device(): pl.pallas_call(body, out_specs=[vmem] * 4, out_shape=[jax.ShapeDtypeStruc...  4.32 us
    pallas_call x2, Pallas kernels, half_features(): pl.pallas_call(body, out_specs=[vmem, far] if first else vmem, out_shape=...  2.8 us
    pallas_call x1, Pallas kernels, on_device(): pl.pallas_call(back_body, out_shape=[jax.ShapeDtypeStruct((2 * pairs, wid...  2.67 us
    ppermute x1, starting transfers between devices, on_device(): got_far = lax.ppermute(far_message, lon, outer)  2.55 us
    pallas_call x1, Pallas kernels, on_device(): pl.pallas_call(prepare_kernel, out_shape=[jax.ShapeDtypeStruct((3, 2, (pa...  2.42 us
  transfers between devices with their start and end apart: 6, of which 0 were waited for; matrix products, arithmetic and copies ran while one was open for 0% of the time, Pallas kernels for 15%

profile of v5, /device:TPU:0, one launch (start us, length us, event | category | flops | bytes accessed | tf_op | source)
XLA Modules:
  0.0 53.4 jit_solution(8061805624978937488)
XLA Ops:
  0.6 0.8 %pack.1 = (bf16[5,8,128]{2,1,0:T(8,128)(2,1)S(1)}, bf16[4,8,128]{2,1,0:T(8,128)(2,1)S(1)}, bf16[4,8,128]{2,1,0:T(8,128)(2,1)S(1)}, s32[1,32]{1,0:T(1,128)S(1)}, ...) custom-call(bf16[4,8,73]{2,1,0:T(8,128)(2,1)} %bitcast.22, s32[1,32]{1,0:T(1,128)} %bitcast.23, ...), custom_call_target="tpu_custom_call" | custom-call | tf_op jit(solution)/shard_map/pack/pallas_call | solution.py:612
  1.4 0.7 %collective-permute-start = (bf16[4,8,128]{2,1,0:T(8,128)(2,1)S(1)}, bf16[4,8,128]{2,1,0:T(8,128)(2,1)S(1)}, u32[]{:S(2)}, u32[]{:S(2)}) collective-permute-start(bf16[4,8,128]{2,1,0:T(8,128)(2,1)S(1)} %get-tuple-element.42), channel_id=1, source_target_pairs={{8,16},{16,8},{9,17},{17,9},{10,18},{18,10},{11,19},{19,11},{12,20... | collective-permute-start | bytes 24584 | tf_op jit(solution)/shard_map/ppermute | solution.py:630
  2.1 5.7 %collective-permute-start.1 = (bf16[4,8,128]{2,1,0:T(8,128)(2,1)S(1)}, bf16[4,8,128]{2,1,0:T(8,128)(2,1)S(1)}, u32[]{:S(2)}, u32[]{:S(2)}) collective-permute-start(bf16[4,8,128]{2,1,0:T(8,128)(2,1)S(1)} %get-tuple-element.43), channel_id=1, source_target_pairs={{0,8},{8,0},{16,24},{24,16},{1,9},{9,1},{17,25},{25,17},{2,10},{10... | collective-permute-start | bytes 24584 | tf_op jit(solution)/shard_map/ppermute | solution.py:631
  7.8 2.4 %prepare.1 = (bf16[3,2,2592,128]{3,2,1,0:T(8,128)(2,1)S(1)}, bf16[1536,256]{1,0:T(8,128)(2,1)S(1)}, bf16[1536,256]{1,0:T(8,128)(2,1)S(1)}, bf16[256,2048]{1,0:T(...) custom-call(bf16[32,128,128]{2,1,0:T(8,128)(2,1)} %cot_hbm.1, ...), custom_call_target="tpu_custom_call" | custom-call | tf_op jit(solution)/shard_map/prepare/pallas_call | solution.py:633
  10.3 0.0 collective-permute-done.outer_ref
  10.3 0.0 collective-permute-done.1.inner_ref
  10.3 2.5 %collective-permute-start.2 = (bf16[6,8,128]{2,1,0:T(8,128)(2,1)S(1)}, bf16[6,8,128]{2,1,0:T(8,128)(2,1)S(1)}, u32[]{:S(2)}, u32[]{:S(2)}) collective-permute-start(bf16[6,8,128]{2,1,0:T(8,128)(2,1)S(1)} %get-tuple-element.45), channel_id=1, source_target_pairs={{0,7},{1,2},{2,1},{3,4},{4,3},{5,6},{6,5},{7,0},{8,15},{9,10},{10,... | collective-permute-start | bytes 36872 | tf_op jit(solution)/shard_map/ppermute | solution.py:665
  12.9 0.0 collective-permute-start.3
  12.9 2.7 %back_hidden.1 = (f32[34,144,128]{2,1,0:T(8,128)S(1)}, bf16[2,240,384]{2,1,0:T(8,128)(2,1)S(1)}, f32[288,128]{1,0:T(8,128)S(1)}, f32[272,384]{1,0:T(8,128)S(1)},...) custom-call(s32[1,32]{1,0:T(1,128)S(1)} %get-tuple-element.51.refs_0_, f32[1,32]{1,0:T(1,128)S(1)} %get-tuple-element.52.refs_1_, ...), custom_call_target="tpu_custom_call" | custom-call | tf_op jit(solution)/shard_map/back_hidden/pallas_call | solution.py:673
  15.5 0.0 collective-permute-done.2.refs_0_
  15.5 0.0 collective-permute-done.3.refs_1_
  15.5 4.3 %tile.1 = (bf16[3,2,2176,128]{3,2,1,0:T(8,128)(2,1)S(1)}, bf16[128,48]{1,0:T(8,128)(2,1)S(1)}, f32[288,128]{1,0:T(8,128)S(1)}, bf16[2,1024,128]{2,1,0:T(8,128)(2,1)S(1)}) custom-call(bf16[6,8,128]{2,1,0:T(8,128)(2,1)S(1)} %collective-permute-done.2.refs_0_, bf16[6,8,128]{2,1,0:T(8,128)(2,1)S(1)} %collective-permute-done.3.refs_1_, ...), custom_call_target="tpu_custom_call" | custom-call | tf_op jit(solution)/shard_map/tile/pallas_call | solution.py:702
  19.9 0.6 %collective-permute-start.4 = (bf16[1024,128]{1,0:T(8,128)(2,1)S(1)}, bf16[1024,128]{1,0:T(8,128)(2,1)S(1)}, u32[]{:S(2)}, u32[]{:S(2)}) collective-permute-start(bf16[1024,128]{1,0:T(8,128)(2,1)S(1)} %slice_bitcast_fusion), channel_id=1, source_target_pairs={{0,1},{1,0},{2,3},{3,2},{4,5},{5,4},{6,7},{7,6},{8,9},{9,8},{10,11... | collective-permute-start | bytes 786440 | tf_op jit(solution)/shard_map/ppermute | solution.py:741
  20.5 1.1 %features_0.1.refs_6_ = bf16[16,128,128]{2,1,0:T(8,128)(2,1)S(1)} custom-call(bf16[1536,256]{1,0:T(8,128)(2,1)S(1)} %get-tuple-element.64.refs_0_, bf16[3,2,2176,128]{3,2,1,0:T(8,128)(2,1)S(1)} %get-tuple-element.65.refs_1_, bf16[128,48]{1,0:T(8,128)(2,1)S(1)} %get-tuple-element.66.refs_2_, f32[288,128]{1,0:T(8,128)S(1)} %get-tuple-element.67.refs_3_, ...), custom_call_target="tpu_custom_call" | custom-call | tf_op jit(solution)/shard_map/features_0/pallas_call | solution.py:731
  21.6 0.0 collective-permute-done.4
  21.6 0.1 fusion
  21.7 15.3 %all_to_all.17.in_ref = bf16[16,64,128]{2,1,0:T(8,128)(2,1)S(1)} all-to-all(bf16[16,64,128]{2,1,0:T(8,128)(2,1)S(1)} %bitcast.19), channel_id=1, replica_groups=mesh['lat'=4,'ring'=4,'core'=2] {'lat','ring'}, dimensions={0} | all-to-all | bytes 524288 | tf_op jit(solution)/shard_map/all_to_all | solution.py:748
  37.1 13.0 %all_to_all.18 = bf16[16,64,128]{2,1,0:T(8,128)(2,1)S(1)} all-to-all(bf16[16,64,128]{2,1,0:T(8,128)(2,1)S(1)} %sum_chunks.1), channel_id=1, replica_groups=mesh['lat'=4,'ring'=4,'core'=2] {'lat','ring'}, dimensions={0} | all-to-all | bytes 524288 | tf_op jit(solution)/shard_map/all_to_all | solution.py:755
  50.1 0.0 collective-permute-start.5
  50.1 1.7 %features_8.1 = (bf16[16,128,128]{2,1,0:T(8,128)(2,1)S(1)}, bf16[32,128,128]{2,1,0:T(8,128)(2,1)}) custom-call(bf16[1536,256]{1,0:T(8,128)(2,1)S(1)} %get-tuple-element.64.refs_0_, bf16[3,2,2176,128]{3,2,1,0:T(8,128)(2,1)S(1)} %get-tuple-element.65.refs_1_, bf16[128,48]{1,0:T(8,128)(2,1)S(1)} %get-tuple-element.66.refs_2_, ...), custom_call_target="tpu_custom_call" | custom-call | tf_op jit(solution)/shard_map/features_8/pallas_call | solution.py:731
  51.8 0.0 collective-permute-done.5.refs_1_
  51.8 1.6 %finish.1 = (bf16[32,128,128]{2,1,0:T(8,128)(2,1)}, f32[73,128]{1,0:T(8,128)}, f32[9,128,128]{2,1,0:T(8,128)}, f32[9,128,128]{2,1,0:T(8,128)}) custom-call(bf16[1024,128]{1,0:T(8,128)(2,1)S(1)} %bitcast.18, bf16[1024,128]{1,0:T(8,128)(2,1)S(1)} %collective-permute-done.5.refs_1_, ...), custom_call_target="tpu_custom_call", output_to_operand_aliasing={{0}: (5, {})} | custom-call | tf_op jit(solution)/shard_map/finish/pallas_call | solution.py:765
  (3 shorter events, 0.1 us)
Async XLA Ops:
  1.4 8.8 %collective-permute-start = (bf16[4,8,128]{2,1,0:T(8,128)(2,1)S(1)}, bf16[4,8,128]{2,1,0:T(8,128)(2,1)S(1)}, u32[]{:S(2)}, u32[]{:S(2)}) collective-permute-start(bf16[4,8,128]{2,1,0:T(8,128)(2,1)S(1)} %get-tuple-element.42), channel_id=1, source_target_pairs={{8,16},{16,8},{9,17},{17,9},{10,18},{18,10},{11,19},{19,11},{12,20... | collective-permute-start | bytes 24584 | tf_op jit(solution)/shard_map/ppermute | solution.py:630
  2.1 8.2 %collective-permute-start.1 = (bf16[4,8,128]{2,1,0:T(8,128)(2,1)S(1)}, bf16[4,8,128]{2,1,0:T(8,128)(2,1)S(1)}, u32[]{:S(2)}, u32[]{:S(2)}) collective-permute-start(bf16[4,8,128]{2,1,0:T(8,128)(2,1)S(1)} %get-tuple-element.43), channel_id=1, source_target_pairs={{0,8},{8,0},{16,24},{24,16},{1,9},{9,1},{17,25},{25,17},{2,10},{10... | collective-permute-start | bytes 24584 | tf_op jit(solution)/shard_map/ppermute | solution.py:631
  10.3 5.2 %collective-permute-start.2 = (bf16[6,8,128]{2,1,0:T(8,128)(2,1)S(1)}, bf16[6,8,128]{2,1,0:T(8,128)(2,1)S(1)}, u32[]{:S(2)}, u32[]{:S(2)}) collective-permute-start(bf16[6,8,128]{2,1,0:T(8,128)(2,1)S(1)} %get-tuple-element.45), channel_id=1, source_target_pairs={{0,7},{1,2},{2,1},{3,4},{4,3},{5,6},{6,5},{7,0},{8,15},{9,10},{10,... | collective-permute-start | bytes 36872 | tf_op jit(solution)/shard_map/ppermute | solution.py:665
  12.9 2.7 %collective-permute-start.3 = (bf16[6,8,128]{2,1,0:T(8,128)(2,1)S(1)}, bf16[6,8,128]{2,1,0:T(8,128)(2,1)S(1)}, u32[]{:S(2)}, u32[]{:S(2)}) collective-permute-start(bf16[6,8,128]{2,1,0:T(8,128)(2,1)S(1)} %get-tuple-element.46), channel_id=1, source_target_pairs={{0,1},{1,0},{2,3},{3,2},{4,5},{5,4},{6,7},{7,6},{8,9},{9,8},{10,11... | collective-permute-start | bytes 36872 | tf_op jit(solution)/shard_map/ppermute | solution.py:666
  19.9 1.7 %collective-permute-start.4 = (bf16[1024,128]{1,0:T(8,128)(2,1)S(1)}, bf16[1024,128]{1,0:T(8,128)(2,1)S(1)}, u32[]{:S(2)}, u32[]{:S(2)}) collective-permute-start(bf16[1024,128]{1,0:T(8,128)(2,1)S(1)} %slice_bitcast_fusion), channel_id=1, source_target_pairs={{0,1},{1,0},{2,3},{3,2},{4,5},{5,4},{6,7},{7,6},{8,9},{9,8},{10,11... | collective-permute-start | bytes 786440 | tf_op jit(solution)/shard_map/ppermute | solution.py:741
  50.1 1.7 %collective-permute-start.5 = (bf16[1024,128]{1,0:T(8,128)(2,1)S(1)}, bf16[1024,128]{1,0:T(8,128)(2,1)S(1)}, u32[]{:S(2)}, u32[]{:S(2)}) collective-permute-start(bf16[1024,128]{1,0:T(8,128)(2,1)S(1)} %bitcast.16), channel_id=1, source_target_pairs={{0,1},{1,0},{2,3},{3,2},{4,5},{5,4},{6,7},{7,6},{8,9},{9,8},{10,11... | collective-permute-start | bytes 786440 | tf_op jit(solution)/shard_map/ppermute | solution.py:756

commit v6 on v4

--- a/solution.py
+++ b/solution.py
@@ -515,7 +515,7 @@
 
 
 def last_kernel(
-    mine_ref, other_ref, embed_ref, first_ref, upper_ref, lower_ref, feat_hbm, ge_hbm, g1_hbm, g2_hbm,
+    mine_ref, near_ref, next_ref, embed_ref, first_ref, upper_ref, lower_ref, feat_hbm, ge_hbm, g1_hbm, g2_hbm,
     sum_ref, ge_ref, g1_ref, g2_ref, sems, *, scale
 ):
     core = lax.axis_index("core")
@@ -530,7 +530,9 @@
     leave(upper_ref, feat_hbm.at[pl.ds(0, count)])
     leave(lower_ref, feat_hbm.at[pl.ds(count, count)])
     sum_ref[core] = mine_ref[...]
-    sum_ref[1 - core] = other_ref[...]
+    quarter = near_ref.shape[0]
+    sum_ref[1 - core, :quarter] = near_ref[...]
+    sum_ref[1 - core, quarter:] = next_ref[...]
 
     def read(at, count):
         return sum_ref[at // half_rows, at % half_rows : at % half_rows + count]
@@ -720,10 +722,16 @@
         )(*arrays)
 
     swap = [(0, 1), (1, 0)]
-    received = lax.ppermute(message[1], "core", swap)
+    quarter = half_rows // 2
+
+    def swapped(value):
+        return [lax.ppermute(v, "core", swap) for v in (value[:quarter], value[quarter:])]
+
+    received = swapped(message[1])
     middle = rows // 4
     part = half_features(0, fore_weight, hid, own_blend, lifted, side_lifted)
-    received, part = lax.optimization_barrier((received, part))
+    *received, part = lax.optimization_barrier((*received, part))
+    received = jnp.concatenate(received)
     pair = (message[0].astype(F32) + received.astype(F32)).astype(BF16)
     axes = ("lat", "ring")
     chunk = half_rows // group
@@ -735,7 +743,7 @@
         name="sum_chunks",
     )(parts.reshape(group, chunk, LANES))
     mine = lax.all_to_all(copies.reshape(half_rows, LANES), axes, 0, 0, tiled=True)
-    other = lax.ppermute(mine, "core", swap)
+    other = swapped(mine)
     last_part = half_features(middle, fore_weight, hid, own_blend, lifted, side_lifted, mine)
     scale = 1.0 / math.sqrt(rows * lat_count * cols * lon_count)
 
@@ -760,7 +768,7 @@
         ],
         compiler_params=params,
         name="finish",
-    )(mine, other, embed, first_weight, part, last_part)
+    )(mine, *other, embed, first_weight, part, last_part)
     shape = (3, 3, hidden, hidden)
     return (features, grad_embed, grad_first.reshape(shape), grad_second.reshape(shape))
 

time: 53.3 us -> 53.7 us (level)
  starting transfers between devices: 9.53 us -> 10.2 us
    ppermute x2 -> x4, starting transfers between devices: 0.58 us -> 1.22 us  [swapped(): lax.ppermute(v, 'core', swap)]
  transfers between devices with their start and end apart: 6 -> 8, of which waited for: 1 -> 1; matrix products, arithmetic and copies ran while one was open for 0% -> 0% of each run, Pallas kernels for 14% -> 14%
where the time goes in v6:
time: 53.7 us; the launch traced here: 53.4 us
  blocking collectives  28.2 us (53%)
  Pallas kernels  13.9 us (26%)
  starting transfers between devices  10.2 us (19%)
  between operations  0.77 us (1%)
    all_to_all x1, blocking collectives, on_device(): parts = lax.all_to_all(pair, axes, 0, 0, tiled=True)  15.2 us
    all_to_all x1, blocking collectives, on_device(): lax.all_to_all(copies.reshape(half_rows, LANES), axes, 0, 0, tiled=True)  13 us
    ppermute x1, starting transfers between devices, on_device(): got_inner = lax.ppermute(to_inner, 'lat', inner)  5.74 us
    pallas_call x1, Pallas kernels, on_device(): pl.pallas_call(body, out_specs=[vmem] * 4, out_shape=[jax.ShapeDtypeStruc...  4.32 us
    pallas_call x1, Pallas kernels, on_device(): pl.pallas_call(back_body, out_shape=[jax.ShapeDtypeStruct((2 * pairs, wid...  2.67 us
    ppermute x1, starting transfers between devices, on_device(): got_far = lax.ppermute(far_message, lon, outer)  2.55 us
    pallas_call x1, Pallas kernels, on_device(): pl.pallas_call(prepare_kernel, out_shape=[jax.ShapeDtypeStruct((3, 2, (pa...  2.42 us
    pallas_call x2, Pallas kernels, half_features(): pl.pallas_call(body, out_shape=jax.ShapeDtypeStruct((rows // 2, cols, hid...  2.23 us
  transfers between devices with their start and end apart: 8, of which 1 were waited for; matrix products, arithmetic and copies ran while one was open for 0% of the time, Pallas kernels for 14%

profile of v6, /device:TPU:0, one launch (start us, length us, event | category | flops | bytes accessed | tf_op | source)
XLA Modules:
  0.0 53.4 jit_solution(12260873653088244685)
XLA Ops:
  0.6 0.8 %pack.1 = (bf16[5,8,128]{2,1,0:T(8,128)(2,1)S(1)}, bf16[4,8,128]{2,1,0:T(8,128)(2,1)S(1)}, bf16[4,8,128]{2,1,0:T(8,128)(2,1)S(1)}, s32[1,32]{1,0:T(1,128)S(1)}, ...) custom-call(bf16[4,8,73]{2,1,0:T(8,128)(2,1)} %bitcast.28, s32[1,32]{1,0:T(1,128)} %bitcast.29, ...), custom_call_target="tpu_custom_call" | custom-call | tf_op jit(solution)/shard_map/pack/pallas_call | solution.py:600
  1.4 0.7 %collective-permute-start = (bf16[4,8,128]{2,1,0:T(8,128)(2,1)S(1)}, bf16[4,8,128]{2,1,0:T(8,128)(2,1)S(1)}, u32[]{:S(2)}, u32[]{:S(2)}) collective-permute-start(bf16[4,8,128]{2,1,0:T(8,128)(2,1)S(1)} %get-tuple-element.41), channel_id=1, source_target_pairs={{8,16},{16,8},{9,17},{17,9},{10,18},{18,10},{11,19},{19,11},{12,20... | collective-permute-start | bytes 24584 | tf_op jit(solution)/shard_map/ppermute | solution.py:618
  2.1 5.7 %collective-permute-start.1 = (bf16[4,8,128]{2,1,0:T(8,128)(2,1)S(1)}, bf16[4,8,128]{2,1,0:T(8,128)(2,1)S(1)}, u32[]{:S(2)}, u32[]{:S(2)}) collective-permute-start(bf16[4,8,128]{2,1,0:T(8,128)(2,1)S(1)} %get-tuple-element.42), channel_id=1, source_target_pairs={{0,8},{8,0},{16,24},{24,16},{1,9},{9,1},{17,25},{25,17},{2,10},{10... | collective-permute-start | bytes 24584 | tf_op jit(solution)/shard_map/ppermute | solution.py:619
  7.8 2.4 %prepare.1 = (bf16[3,2,2592,128]{3,2,1,0:T(8,128)(2,1)S(1)}, bf16[1536,256]{1,0:T(8,128)(2,1)S(1)}, bf16[1536,256]{1,0:T(8,128)(2,1)S(1)}, bf16[256,2048]{1,0:T(...) custom-call(bf16[32,128,128]{2,1,0:T(8,128)(2,1)} %cot_hbm.1, ...), custom_call_target="tpu_custom_call" | custom-call | tf_op jit(solution)/shard_map/prepare/pallas_call | solution.py:621
  10.3 0.0 collective-permute-done.outer_ref
  10.3 0.0 collective-permute-done.1.inner_ref
  10.3 2.5 %collective-permute-start.2 = (bf16[6,8,128]{2,1,0:T(8,128)(2,1)S(1)}, bf16[6,8,128]{2,1,0:T(8,128)(2,1)S(1)}, u32[]{:S(2)}, u32[]{:S(2)}) collective-permute-start(bf16[6,8,128]{2,1,0:T(8,128)(2,1)S(1)} %get-tuple-element.44), channel_id=1, source_target_pairs={{0,7},{1,2},{2,1},{3,4},{4,3},{5,6},{6,5},{7,0},{8,15},{9,10},{10,... | collective-permute-start | bytes 36872 | tf_op jit(solution)/shard_map/ppermute | solution.py:653
  12.9 0.0 collective-permute-start.3
  12.9 2.7 %back_hidden.1 = (f32[34,144,128]{2,1,0:T(8,128)S(1)}, bf16[2,240,384]{2,1,0:T(8,128)(2,1)S(1)}, f32[288,128]{1,0:T(8,128)S(1)}, f32[272,384]{1,0:T(8,128)S(1)},...) custom-call(s32[1,32]{1,0:T(1,128)S(1)} %get-tuple-element.50.refs_0_, f32[1,32]{1,0:T(1,128)S(1)} %get-tuple-element.51.refs_1_, ...), custom_call_target="tpu_custom_call" | custom-call | tf_op jit(solution)/shard_map/back_hidden/pallas_call | solution.py:661
  15.5 0.0 collective-permute-done.2.refs_0_
  15.5 0.0 collective-permute-done.3.refs_1_
  15.5 4.3 %tile.1 = (bf16[3,2,2176,128]{3,2,1,0:T(8,128)(2,1)S(1)}, bf16[128,48]{1,0:T(8,128)(2,1)S(1)}, f32[288,128]{1,0:T(8,128)S(1)}, bf16[2,1024,128]{2,1,0:T(8,128)(2,1)S(1)}) custom-call(bf16[6,8,128]{2,1,0:T(8,128)(2,1)S(1)} %collective-permute-done.2.refs_0_, bf16[6,8,128]{2,1,0:T(8,128)(2,1)S(1)} %collective-permute-done.3.refs_1_, ...), custom_call_target="tpu_custom_call" | custom-call | tf_op jit(solution)/shard_map/tile/pallas_call | solution.py:690
  19.9 0.6 %collective-permute-start.5 = (bf16[512,128]{1,0:T(8,128)(2,1)S(1)}, bf16[512,128]{1,0:T(8,128)(2,1)S(1)}, u32[]{:S(2)}, u32[]{:S(2)}) collective-permute-start(bf16[512,128]{1,0:T(8,128)(2,1)S(1)} %get-tuple-element.76), channel_id=1, source_target_pairs={{0,1},{1,0},{2,3},{3,2},{4,5},{5,4},{6,7},{7,6},{8,9},{9,8},{10,11... | collective-permute-start | bytes 393224 | tf_op jit(solution)/shard_map/ppermute | solution.py:728
  20.5 0.1 collective-permute-start.4
  20.6 1.1 %features_0.1.refs_5_ = bf16[16,128,128]{2,1,0:T(8,128)(2,1)S(1)} custom-call(bf16[1536,256]{1,0:T(8,128)(2,1)S(1)} %get-tuple-element.63.refs_0_, bf16[3,2,2176,128]{3,2,1,0:T(8,128)(2,1)S(1)} %get-tuple-element.64.refs_1_, bf16[128,48]{1,0:T(8,128)(2,1)S(1)} %get-tuple-element.65.refs_2_, f32[288,128]{1,0:T(8,128)S(1)} %get-tuple-element.66.refs_3_, ...), custom_call_target="tpu_custom_call" | custom-call | tf_op jit(solution)/shard_map/features_0/pallas_call | solution.py:717
  21.7 0.0 collective-permute-done.5
  21.7 0.1 collective-permute-done.4
  21.8 0.1 fusion
  21.9 15.2 %all_to_all.14.in_ref = bf16[16,64,128]{2,1,0:T(8,128)(2,1)S(1)} all-to-all(bf16[16,64,128]{2,1,0:T(8,128)(2,1)S(1)} %fusion), channel_id=1, replica_groups=mesh['lat'=4,'ring'=4,'core'=2] {'lat','ring'}, dimensions={0} | all-to-all | bytes 524288 | tf_op jit(solution)/shard_map/all_to_all | solution.py:738
  37.2 13.0 %all_to_all.15 = bf16[16,64,128]{2,1,0:T(8,128)(2,1)S(1)} all-to-all(bf16[16,64,128]{2,1,0:T(8,128)(2,1)S(1)} %sum_chunks.1), channel_id=1, replica_groups=mesh['lat'=4,'ring'=4,'core'=2] {'lat','ring'}, dimensions={0} | all-to-all | bytes 524288 | tf_op jit(solution)/shard_map/all_to_all | solution.py:745
  50.2 0.1 collective-permute-start.6
  50.3 0.5 collective-permute-start.7
  50.8 1.1 %features_8.1.refs_6_ = bf16[16,128,128]{2,1,0:T(8,128)(2,1)S(1)} custom-call(bf16[1536,256]{1,0:T(8,128)(2,1)S(1)} %get-tuple-element.63.refs_0_, bf16[3,2,2176,128]{3,2,1,0:T(8,128)(2,1)S(1)} %get-tuple-element.64.refs_1_, bf16[128,48]{1,0:T(8,128)(2,1)S(1)} %get-tuple-element.65.refs_2_, f32[288,128]{1,0:T(8,128)S(1)} %get-tuple-element.66.refs_3_, ...), custom_call_target="tpu_custom_call" | custom-call | tf_op jit(solution)/shard_map/features_8/pallas_call | solution.py:717
  51.9 0.0 collective-permute-done.6.refs_1_
  51.9 0.0 collective-permute-done.7.refs_2_
  52.0 1.4 %finish.1 = (bf16[32,128,128]{2,1,0:T(8,128)(2,1)}, f32[73,128]{1,0:T(8,128)}, f32[9,128,128]{2,1,0:T(8,128)}, f32[9,128,128]{2,1,0:T(8,128)}) custom-call(bf16[1024,128]{1,0:T(8,128)(2,1)S(1)} %bitcast.21, bf16[512,128]{1,0:T(8,128)(2,1)S(1)} %collective-permute-done.6.refs_1_, bf16[512,128]{1,0:T(8,128)(2,1)S(1)} %collective-permute-done.7.refs_2_, ...), custom_call_target="tpu_custom_call" | custom-call | tf_op jit(solution)/shard_map/finish/pallas_call | solution.py:753
  (6 shorter events, 0.1 us)
Async XLA Ops:
  1.4 8.8 %collective-permute-start = (bf16[4,8,128]{2,1,0:T(8,128)(2,1)S(1)}, bf16[4,8,128]{2,1,0:T(8,128)(2,1)S(1)}, u32[]{:S(2)}, u32[]{:S(2)}) collective-permute-start(bf16[4,8,128]{2,1,0:T(8,128)(2,1)S(1)} %get-tuple-element.41), channel_id=1, source_target_pairs={{8,16},{16,8},{9,17},{17,9},{10,18},{18,10},{11,19},{19,11},{12,20... | collective-permute-start | bytes 24584 | tf_op jit(solution)/shard_map/ppermute | solution.py:618
  2.1 8.2 %collective-permute-start.1 = (bf16[4,8,128]{2,1,0:T(8,128)(2,1)S(1)}, bf16[4,8,128]{2,1,0:T(8,128)(2,1)S(1)}, u32[]{:S(2)}, u32[]{:S(2)}) collective-permute-start(bf16[4,8,128]{2,1,0:T(8,128)(2,1)S(1)} %get-tuple-element.42), channel_id=1, source_target_pairs={{0,8},{8,0},{16,24},{24,16},{1,9},{9,1},{17,25},{25,17},{2,10},{10... | collective-permute-start | bytes 24584 | tf_op jit(solution)/shard_map/ppermute | solution.py:619
  10.3 5.2 %collective-permute-start.2 = (bf16[6,8,128]{2,1,0:T(8,128)(2,1)S(1)}, bf16[6,8,128]{2,1,0:T(8,128)(2,1)S(1)}, u32[]{:S(2)}, u32[]{:S(2)}) collective-permute-start(bf16[6,8,128]{2,1,0:T(8,128)(2,1)S(1)} %get-tuple-element.44), channel_id=1, source_target_pairs={{0,7},{1,2},{2,1},{3,4},{4,3},{5,6},{6,5},{7,0},{8,15},{9,10},{10,... | collective-permute-start | bytes 36872 | tf_op jit(solution)/shard_map/ppermute | solution.py:653
  12.9 2.7 %collective-permute-start.3 = (bf16[6,8,128]{2,1,0:T(8,128)(2,1)S(1)}, bf16[6,8,128]{2,1,0:T(8,128)(2,1)S(1)}, u32[]{:S(2)}, u32[]{:S(2)}) collective-permute-start(bf16[6,8,128]{2,1,0:T(8,128)(2,1)S(1)} %get-tuple-element.45), channel_id=1, source_target_pairs={{0,1},{1,0},{2,3},{3,2},{4,5},{5,4},{6,7},{7,6},{8,9},{9,8},{10,11... | collective-permute-start | bytes 36872 | tf_op jit(solution)/shard_map/ppermute | solution.py:654
  19.9 1.8 %collective-permute-start.5 = (bf16[512,128]{1,0:T(8,128)(2,1)S(1)}, bf16[512,128]{1,0:T(8,128)(2,1)S(1)}, u32[]{:S(2)}, u32[]{:S(2)}) collective-permute-start(bf16[512,128]{1,0:T(8,128)(2,1)S(1)} %get-tuple-element.76), channel_id=1, source_target_pairs={{0,1},{1,0},{2,3},{3,2},{4,5},{5,4},{6,7},{7,6},{8,9},{9,8},{10,11... | collective-permute-start | bytes 393224 | tf_op jit(solution)/shard_map/ppermute | solution.py:728
  20.5 1.3 %collective-permute-start.4 = (bf16[512,128]{1,0:T(8,128)(2,1)S(1)}, bf16[512,128]{1,0:T(8,128)(2,1)S(1)}, u32[]{:S(2)}, u32[]{:S(2)}) collective-permute-start(bf16[512,128]{1,0:T(8,128)(2,1)S(1)} %get-tuple-element.77), channel_id=1, source_target_pairs={{0,1},{1,0},{2,3},{3,2},{4,5},{5,4},{6,7},{7,6},{8,9},{9,8},{10,11... | collective-permute-start | bytes 393224 | tf_op jit(solution)/shard_map/ppermute | solution.py:728
  50.2 1.7 %collective-permute-start.6 = (bf16[512,128]{1,0:T(8,128)(2,1)S(1)}, bf16[512,128]{1,0:T(8,128)(2,1)S(1)}, u32[]{:S(2)}, u32[]{:S(2)}) collective-permute-start(bf16[512,128]{1,0:T(8,128)(2,1)S(1)} %bitcast.27), channel_id=1, source_target_pairs={{0,1},{1,0},{2,3},{3,2},{4,5},{5,4},{6,7},{7,6},{8,9},{9,8},{10,11... | collective-permute-start | bytes 393224 | tf_op jit(solution)/shard_map/ppermute | solution.py:728
  50.3 1.6 %collective-permute-start.7 = (bf16[512,128]{1,0:T(8,128)(2,1)S(1)}, bf16[512,128]{1,0:T(8,128)(2,1)S(1)}, u32[]{:S(2)}, u32[]{:S(2)}) collective-permute-start(bf16[512,128]{1,0:T(8,128)(2,1)S(1)} %bitcast.26), channel_id=1, source_target_pairs={{0,1},{1,0},{2,3},{3,2},{4,5},{5,4},{6,7},{7,6},{8,9},{9,8},{10,11... | collective-permute-start | bytes 393224 | tf_op jit(solution)/shard_map/ppermute | solution.py:728

commit v7 on v4

--- a/solution.py
+++ b/solution.py
@@ -350,7 +350,6 @@
         right_ref[:, t * LANES : (t + 1) * LANES] = stacked(jnp.concatenate(blocks, axis=0))
     half = rows // 2 + 2
     spans = ((0, half), (half, 2 * pairs))
-    cells_half = rows // 4 * cols
 
     def first_product(n):
         span = slice(spans[n][0] * LANES, spans[n][1] * LANES)
@@ -373,13 +372,12 @@
         for b in range(3):
             hid_ref[b, t % 2, at : at + cols] = line_ref[t, b : b + cols].astype(BF16)
 
-    def second_gradient(n, b):
+    def second_gradient(b):
         right = []
         for i in range(4):
-            start = (i // 2) * cols + n * cells_half
-            right.append(hid_ref[b, i % 2, start : start + cells_half])
-        left = turned_ref[:, n * cells_half : (n + 1) * cells_half]
-        return jnp.dot(left, jnp.concatenate(right, axis=1), preferred_element_type=F32)
+            start = (i // 2) * cols
+            right.append(hid_ref[b, i % 2, start : start + rows // 2 * cols])
+        return jnp.dot(turned_ref[...], jnp.concatenate(right, axis=1), preferred_element_type=F32)
 
     pre = first_product(0)
     for t in range(*spans[0]):
@@ -387,16 +385,13 @@
     pre = first_product(1)
     for t in range(*spans[0]):
         place_hidden(t)
-    grads = []
-    rest = list(range(*spans[1]))
-    share = -(-len(rest) // 3)
-    for b in range(3):
-        grads.append(second_gradient(0, b))
-        for t in rest[b * share : (b + 1) * share]:
-            activate(pre, spans[1][0], t)
-            place_hidden(t)
+    for t in range(*spans[1]):
+        activate(pre, spans[1][0], t)
+        place_hidden(t)
     back = jnp.dot(col_t, delta_ref[...], preferred_element_type=F32)
     back = back[:taps] + back[taps:]
+    grads = []
+
     width = rows_ref.shape[2]
     used = 2 * pairs * band_cols
     blank = jnp.zeros((2, width - used, back_ref.shape[2]), BF16)
@@ -429,7 +424,7 @@
     share = -(-pairs // 3)
     side_hi, side_lo = turned_rows(side_mixed, width)
     for b in range(3):
-        grads[b] = grads[b] + second_gradient(1, b)
+        grads.append(second_gradient(b))
         for p in range(b * share, min((b + 1) * share, pairs)):
             place_back(p)
     upper = jnp.concatenate([rows_ref[0], side_hi], axis=1)

time: 53.3 us -> 53.3 us (level)
  no operation moved by 1% of the time
where the time goes in v7:
time: 53.3 us; the launch traced here: 53.1 us
  blocking collectives  28.3 us (53%)
  Pallas kernels  13.9 us (26%)
  starting transfers between devices  9.53 us (18%)
  between operations  0.72 us (1%)
    all_to_all x1, blocking collectives, on_device(): parts = lax.all_to_all(pair, axes, 0, 0, tiled=True)  15.3 us
    all_to_all x1, blocking collectives, on_device(): lax.all_to_all(copies.reshape(half_rows, LANES), axes, 0, 0, tiled=True)  13 us
    ppermute x1, starting transfers between devices, on_device(): got_inner = lax.ppermute(to_inner, 'lat', inner)  5.74 us
    pallas_call x1, Pallas kernels, on_device(): pl.pallas_call(body, out_specs=[vmem] * 4, out_shape=[jax.ShapeDtypeStruc...  4.34 us
    pallas_call x1, Pallas kernels, on_device(): pl.pallas_call(back_body, out_shape=[jax.ShapeDtypeStruct((2 * pairs, wid...  2.67 us
    ppermute x1, starting transfers between devices, on_device(): got_far = lax.ppermute(far_message, lon, outer)  2.55 us
    pallas_call x1, Pallas kernels, on_device(): pl.pallas_call(prepare_kernel, out_shape=[jax.ShapeDtypeStruct((3, 2, (pa...  2.42 us
    pallas_call x2, Pallas kernels, half_features(): pl.pallas_call(body, out_shape=jax.ShapeDtypeStruct((rows // 2, cols, hid...  2.22 us
  transfers between devices with their start and end apart: 6, of which 1 were waited for; matrix products, arithmetic and copies ran while one was open for 0% of the time, Pallas kernels for 14%

profile of v7, /device:TPU:0, one launch (start us, length us, event | category | flops | bytes accessed | tf_op | source)
XLA Modules:
  0.0 53.1 jit_solution(15834727932952512058)
XLA Ops:
  0.6 0.8 %pack.1 = (bf16[5,8,128]{2,1,0:T(8,128)(2,1)S(1)}, bf16[4,8,128]{2,1,0:T(8,128)(2,1)S(1)}, bf16[4,8,128]{2,1,0:T(8,128)(2,1)S(1)}, s32[1,32]{1,0:T(1,128)S(1)}, ...) custom-call(bf16[4,8,73]{2,1,0:T(8,128)(2,1)} %bitcast.22, s32[1,32]{1,0:T(1,128)} %bitcast.23, ...), custom_call_target="tpu_custom_call" | custom-call | tf_op jit(solution)/shard_map/pack/pallas_call | solution.py:593
  1.4 0.7 %collective-permute-start = (bf16[4,8,128]{2,1,0:T(8,128)(2,1)S(1)}, bf16[4,8,128]{2,1,0:T(8,128)(2,1)S(1)}, u32[]{:S(2)}, u32[]{:S(2)}) collective-permute-start(bf16[4,8,128]{2,1,0:T(8,128)(2,1)S(1)} %get-tuple-element.40), channel_id=1, source_target_pairs={{8,16},{16,8},{9,17},{17,9},{10,18},{18,10},{11,19},{19,11},{12,20... | collective-permute-start | bytes 24584 | tf_op jit(solution)/shard_map/ppermute | solution.py:611
  2.1 5.7 %collective-permute-start.1 = (bf16[4,8,128]{2,1,0:T(8,128)(2,1)S(1)}, bf16[4,8,128]{2,1,0:T(8,128)(2,1)S(1)}, u32[]{:S(2)}, u32[]{:S(2)}) collective-permute-start(bf16[4,8,128]{2,1,0:T(8,128)(2,1)S(1)} %get-tuple-element.41), channel_id=1, source_target_pairs={{0,8},{8,0},{16,24},{24,16},{1,9},{9,1},{17,25},{25,17},{2,10},{10... | collective-permute-start | bytes 24584 | tf_op jit(solution)/shard_map/ppermute | solution.py:612
  7.8 2.4 %prepare.1 = (bf16[3,2,2592,128]{3,2,1,0:T(8,128)(2,1)S(1)}, bf16[1536,256]{1,0:T(8,128)(2,1)S(1)}, bf16[1536,256]{1,0:T(8,128)(2,1)S(1)}, bf16[256,2048]{1,0:T(...) custom-call(bf16[32,128,128]{2,1,0:T(8,128)(2,1)} %cot_hbm.1, ...), custom_call_target="tpu_custom_call" | custom-call | tf_op jit(solution)/shard_map/prepare/pallas_call | solution.py:614
  10.3 0.0 collective-permute-done.outer_ref
  10.3 0.0 collective-permute-done.1.inner_ref
  10.3 2.5 %collective-permute-start.2 = (bf16[6,8,128]{2,1,0:T(8,128)(2,1)S(1)}, bf16[6,8,128]{2,1,0:T(8,128)(2,1)S(1)}, u32[]{:S(2)}, u32[]{:S(2)}) collective-permute-start(bf16[6,8,128]{2,1,0:T(8,128)(2,1)S(1)} %get-tuple-element.43), channel_id=1, source_target_pairs={{0,7},{1,2},{2,1},{3,4},{4,3},{5,6},{6,5},{7,0},{8,15},{9,10},{10,... | collective-permute-start | bytes 36872 | tf_op jit(solution)/shard_map/ppermute | solution.py:646
  12.9 0.0 collective-permute-start.3
  12.9 2.7 %back_hidden.1 = (f32[34,144,128]{2,1,0:T(8,128)S(1)}, bf16[2,240,384]{2,1,0:T(8,128)(2,1)S(1)}, f32[288,128]{1,0:T(8,128)S(1)}, f32[272,384]{1,0:T(8,128)S(1)},...) custom-call(s32[1,32]{1,0:T(1,128)S(1)} %get-tuple-element.49.refs_0_, f32[1,32]{1,0:T(1,128)S(1)} %get-tuple-element.50.refs_1_, ...), custom_call_target="tpu_custom_call" | custom-call | tf_op jit(solution)/shard_map/back_hidden/pallas_call | solution.py:654
  15.5 0.0 collective-permute-done.2.refs_0_
  15.5 0.0 collective-permute-done.3.refs_1_
  15.5 4.3 %tile.1 = (bf16[3,2,2176,128]{3,2,1,0:T(8,128)(2,1)S(1)}, bf16[128,48]{1,0:T(8,128)(2,1)S(1)}, f32[288,128]{1,0:T(8,128)S(1)}, bf16[2,1024,128]{2,1,0:T(8,128)(2,1)S(1)}) custom-call(bf16[6,8,128]{2,1,0:T(8,128)(2,1)S(1)} %collective-permute-done.2.refs_0_, bf16[6,8,128]{2,1,0:T(8,128)(2,1)S(1)} %collective-permute-done.3.refs_1_, ...), custom_call_target="tpu_custom_call" | custom-call | tf_op jit(solution)/shard_map/tile/pallas_call | solution.py:683
  19.9 0.6 %collective-permute-start.4 = (bf16[1024,128]{1,0:T(8,128)(2,1)S(1)}, bf16[1024,128]{1,0:T(8,128)(2,1)S(1)}, u32[]{:S(2)}, u32[]{:S(2)}) collective-permute-start(bf16[1024,128]{1,0:T(8,128)(2,1)S(1)} %slice_bitcast_fusion), channel_id=1, source_target_pairs={{0,1},{1,0},{2,3},{3,2},{4,5},{5,4},{6,7},{7,6},{8,9},{9,8},{10,11... | collective-permute-start | bytes 786440 | tf_op jit(solution)/shard_map/ppermute | solution.py:718
  20.5 1.1 %features_0.1.refs_4_ = bf16[16,128,128]{2,1,0:T(8,128)(2,1)S(1)} custom-call(bf16[1536,256]{1,0:T(8,128)(2,1)S(1)} %get-tuple-element.62.refs_0_, bf16[3,2,2176,128]{3,2,1,0:T(8,128)(2,1)S(1)} %get-tuple-element.63.refs_1_, bf16[128,48]{1,0:T(8,128)(2,1)S(1)} %get-tuple-element.64.refs_2_, f32[288,128]{1,0:T(8,128)S(1)} %get-tuple-element.65.refs_3_, ...), custom_call_target="tpu_custom_call" | custom-call | tf_op jit(solution)/shard_map/features_0/pallas_call | solution.py:710
  21.6 0.0 collective-permute-done.4
  21.7 0.1 fusion
  21.7 15.3 %all_to_all.17.in_ref = bf16[16,64,128]{2,1,0:T(8,128)(2,1)S(1)} all-to-all(bf16[16,64,128]{2,1,0:T(8,128)(2,1)S(1)} %bitcast.19), channel_id=1, replica_groups=mesh['lat'=4,'ring'=4,'core'=2] {'lat','ring'}, dimensions={0} | all-to-all | bytes 524288 | tf_op jit(solution)/shard_map/all_to_all | solution.py:725
  37.1 13.0 %all_to_all.18 = bf16[16,64,128]{2,1,0:T(8,128)(2,1)S(1)} all-to-all(bf16[16,64,128]{2,1,0:T(8,128)(2,1)S(1)} %sum_chunks.1), channel_id=1, replica_groups=mesh['lat'=4,'ring'=4,'core'=2] {'lat','ring'}, dimensions={0} | all-to-all | bytes 524288 | tf_op jit(solution)/shard_map/all_to_all | solution.py:732
  50.1 0.0 collective-permute-start.5
  50.1 1.1 %features_8.1.refs_5_ = bf16[16,128,128]{2,1,0:T(8,128)(2,1)S(1)} custom-call(bf16[1536,256]{1,0:T(8,128)(2,1)S(1)} %get-tuple-element.62.refs_0_, bf16[3,2,2176,128]{3,2,1,0:T(8,128)(2,1)S(1)} %get-tuple-element.63.refs_1_, bf16[128,48]{1,0:T(8,128)(2,1)S(1)} %get-tuple-element.64.refs_2_, f32[288,128]{1,0:T(8,128)S(1)} %get-tuple-element.65.refs_3_, ...), custom_call_target="tpu_custom_call" | custom-call | tf_op jit(solution)/shard_map/features_8/pallas_call | solution.py:710
  51.2 0.4 collective-permute-done.5.refs_1_
  51.6 1.4 %finish.1 = (bf16[32,128,128]{2,1,0:T(8,128)(2,1)}, f32[73,128]{1,0:T(8,128)}, f32[9,128,128]{2,1,0:T(8,128)}, f32[9,128,128]{2,1,0:T(8,128)}) custom-call(bf16[1024,128]{1,0:T(8,128)(2,1)S(1)} %bitcast.18, bf16[1024,128]{1,0:T(8,128)(2,1)S(1)} %collective-permute-done.5.refs_1_, bf16[128,128]{1,0:T(8,128)(2,1)S(1)} %get-tuple-element.42.ready_ref.refs_9_.refs_4_.refs_2_, ...), custom_call_target="tpu_custom_call" | custom-call | tf_op jit(solution)/shard_map/finish/pallas_call | solution.py:740
  (3 shorter events, 0.1 us)
Async XLA Ops:
  1.4 8.8 %collective-permute-start = (bf16[4,8,128]{2,1,0:T(8,128)(2,1)S(1)}, bf16[4,8,128]{2,1,0:T(8,128)(2,1)S(1)}, u32[]{:S(2)}, u32[]{:S(2)}) collective-permute-start(bf16[4,8,128]{2,1,0:T(8,128)(2,1)S(1)} %get-tuple-element.40), channel_id=1, source_target_pairs={{8,16},{16,8},{9,17},{17,9},{10,18},{18,10},{11,19},{19,11},{12,20... | collective-permute-start | bytes 24584 | tf_op jit(solution)/shard_map/ppermute | solution.py:611
  2.1 8.2 %collective-permute-start.1 = (bf16[4,8,128]{2,1,0:T(8,128)(2,1)S(1)}, bf16[4,8,128]{2,1,0:T(8,128)(2,1)S(1)}, u32[]{:S(2)}, u32[]{:S(2)}) collective-permute-start(bf16[4,8,128]{2,1,0:T(8,128)(2,1)S(1)} %get-tuple-element.41), channel_id=1, source_target_pairs={{0,8},{8,0},{16,24},{24,16},{1,9},{9,1},{17,25},{25,17},{2,10},{10... | collective-permute-start | bytes 24584 | tf_op jit(solution)/shard_map/ppermute | solution.py:612
  10.3 5.2 %collective-permute-start.2 = (bf16[6,8,128]{2,1,0:T(8,128)(2,1)S(1)}, bf16[6,8,128]{2,1,0:T(8,128)(2,1)S(1)}, u32[]{:S(2)}, u32[]{:S(2)}) collective-permute-start(bf16[6,8,128]{2,1,0:T(8,128)(2,1)S(1)} %get-tuple-element.43), channel_id=1, source_target_pairs={{0,7},{1,2},{2,1},{3,4},{4,3},{5,6},{6,5},{7,0},{8,15},{9,10},{10,... | collective-permute-start | bytes 36872 | tf_op jit(solution)/shard_map/ppermute | solution.py:646
  12.9 2.7 %collective-permute-start.3 = (bf16[6,8,128]{2,1,0:T(8,128)(2,1)S(1)}, bf16[6,8,128]{2,1,0:T(8,128)(2,1)S(1)}, u32[]{:S(2)}, u32[]{:S(2)}) collective-permute-start(bf16[6,8,128]{2,1,0:T(8,128)(2,1)S(1)} %get-tuple-element.44), channel_id=1, source_target_pairs={{0,1},{1,0},{2,3},{3,2},{4,5},{5,4},{6,7},{7,6},{8,9},{9,8},{10,11... | collective-permute-start | bytes 36872 | tf_op jit(solution)/shard_map/ppermute | solution.py:647
  19.9 1.7 %collective-permute-start.4 = (bf16[1024,128]{1,0:T(8,128)(2,1)S(1)}, bf16[1024,128]{1,0:T(8,128)(2,1)S(1)}, u32[]{:S(2)}, u32[]{:S(2)}) collective-permute-start(bf16[1024,128]{1,0:T(8,128)(2,1)S(1)} %slice_bitcast_fusion), channel_id=1, source_target_pairs={{0,1},{1,0},{2,3},{3,2},{4,5},{5,4},{6,7},{7,6},{8,9},{9,8},{10,11... | collective-permute-start | bytes 786440 | tf_op jit(solution)/shard_map/ppermute | solution.py:718
  50.1 1.5 %collective-permute-start.5 = (bf16[1024,128]{1,0:T(8,128)(2,1)S(1)}, bf16[1024,128]{1,0:T(8,128)(2,1)S(1)}, u32[]{:S(2)}, u32[]{:S(2)}) collective-permute-start(bf16[1024,128]{1,0:T(8,128)(2,1)S(1)} %bitcast.16), channel_id=1, source_target_pairs={{0,1},{1,0},{2,3},{3,2},{4,5},{5,4},{6,7},{7,6},{8,9},{9,8},{10,11... | collective-permute-start | bytes 786440 | tf_op jit(solution)/shard_map/ppermute | solution.py:733

commit v8 on v7

--- a/solution.py
+++ b/solution.py
@@ -22,10 +22,27 @@
     return high, (value - high.astype(F32)).astype(BF16)
 
 
+def back_rows(shift_ref, weight_ref, out_ref, start_pair):
+    wide = out_ref.shape[1]
+    pairs = out_ref.shape[0] // 2
+    step = 7
+    for first in range(0, pairs, step):
+        count = min(step, pairs - first)
+        blocks = []
+        for b in range(3):
+            for i in range(4):
+                start = (start_pair + first + i // 2) * wide
+                blocks.append(shift_ref[b, i % 2, start : start + count * wide])
+        out = jnp.dot(jnp.concatenate(blocks, axis=1), weight_ref[...], preferred_element_type=F32)
+        for m in range(count):
+            for q in range(2):
+                out_ref[2 * (first + m) + q] = out[m * wide : (m + 1) * wide, q * LANES : (q + 1) * LANES]
+
+
 def prepare_kernel(
     cot_hbm, w2_hbm, w1_hbm, embed_hbm,
-    shift_ref, back_ref, fore_ref, turned_ref, first_ref, cot_ref, w1_ref, padded_ref,
-    w2_ref, embed_ref, line_ref, sems
+    shift_ref, back_ref, turned_ref, cot_ref, w1_ref, w2_ref, padded_ref, begun_ref,
+    embed_ref, line_ref, sems
 ):
     rows, cols, _ = cot_ref.shape
     wide = cols + 16
@@ -45,7 +62,6 @@
     embed_copy.start()
     line_ref[...] = jnp.zeros_like(line_ref)
     back_ref[...] = jnp.zeros_like(back_ref)
-    fore_ref[...] = jnp.zeros_like(fore_ref)
     blank = jnp.zeros((wide, LANES), BF16)
     for b in range(3):
         for parity in range(2):
@@ -54,14 +70,10 @@
     weight_copy.wait()
     for a in range(3):
         for b in range(3):
-            straight = w2_ref[a * 3 + b]
-            turned = straight.astype(F32).T.astype(BF16)
+            turned = w2_ref[a * 3 + b].astype(F32).T.astype(BF16)
             for q in range(2):
-                column = slice(q * LANES, (q + 1) * LANES)
                 at = (b * 4 + 2 + q - a) * LANES
-                back_ref[at : at + LANES, column] = turned
-                at = (b * 4 + a + q) * LANES
-                fore_ref[at : at + LANES, column] = straight
+                back_ref[at : at + LANES, q * LANES : (q + 1) * LANES] = turned
     for r in range(rows):
         slot = r % 4
         if r % share == 0:
@@ -75,8 +87,7 @@
     embed_copy.wait()
     padded_ref[...] = padded_embed(embed_ref, line_ref)
     other_copy.wait()
-    for tap in range(9):
-        first_ref[tap * LANES : (tap + 1) * LANES] = w1_ref[tap].astype(F32).T.astype(BF16)
+    back_rows(shift_ref, back_ref, begun_ref, 0)
 
 
 def edge_line(block, at):
@@ -193,21 +204,8 @@
     coarse_cols,
 ):
     rows, cols, _ = cot_ref.shape
-    wide = bh_ref.shape[1]
-    pairs = bh_ref.shape[0] // 2
     band_rows, band_cols = own_ref.shape[0] - 1, own_ref.shape[1]
-    step = 6
-    for first in range(0, pairs, step):
-        count = min(step, pairs - first)
-        blocks = []
-        for b in range(3):
-            for i in range(4):
-                start = (first + i // 2) * wide
-                blocks.append(shift_ref[b, i % 2, start : start + count * wide])
-        out = jnp.dot(jnp.concatenate(blocks, axis=1), weight_ref[...], preferred_element_type=F32)
-        for m in range(count):
-            for q in range(2):
-                bh_ref[2 * (first + m) + q] = out[m * wide : (m + 1) * wide, q * LANES : (q + 1) * LANES]
+    back_rows(shift_ref, weight_ref, bh_ref, rows // 2 + 1 - bh_ref.shape[0] // 2)
 
     lat = lax.axis_index("lat")
     lon = lax.axis_index("ring") * 2 + lax.axis_index("core")
@@ -276,6 +274,7 @@
     embed_ref,
     w1_ref,
     turned_ref,
+    begun_ref,
     bh_ref,
     rows_ref,
     tap_ref,
@@ -297,7 +296,8 @@
 ):
     rows, cols = cot_col_ref.shape[0], own_ref.shape[0]
     wide = bh_ref.shape[1]
-    pairs = bh_ref.shape[0] // 2
+    begun = begun_ref.shape[0]
+    pairs = (begun + bh_ref.shape[0]) // 2
     depth = 2 * (far_ref.shape[0] - 1)
     half_rows = msg_ref.shape[1]
     lat = lax.axis_index("lat")
@@ -365,7 +365,8 @@
         h = v * s
         slope = s + h * (1.0 - s)
         line_ref[t] = h
-        delta_ref[:, t * LANES : (t + 1) * LANES] = (bh_ref[t] * slope).astype(BF16)
+        arrived = begun_ref[t] if t < begun else bh_ref[t - begun]
+        delta_ref[:, t * LANES : (t + 1) * LANES] = (arrived * slope).astype(BF16)
 
     def place_hidden(t):
         at = (t // 2) * cols
@@ -468,8 +469,20 @@
     near_ref[len(tall) // 2] = own[band_rows].astype(BF16)
 
 
-def features_kernel(weight_ref, hid_ref, own_ref, lifted_ref, side_lifted_ref, *refs, first):
-    feat_ref = refs[-1]
+def features_kernel(given_ref, hid_ref, own_ref, lifted_ref, side_lifted_ref, *refs, first):
+    if first:
+        weight_ref = given_ref
+        _, w1_ref, feat_ref, first_ref = refs
+        for tap in range(9):
+            first_ref[tap * LANES : (tap + 1) * LANES] = w1_ref[tap].astype(F32).T.astype(BF16)
+    else:
+        feat_ref, weight_ref = refs
+        weight_ref[...] = jnp.zeros_like(weight_ref)
+        for a in range(3):
+            for b in range(3):
+                for q in range(2):
+                    at = (b * 4 + a + q) * LANES
+                    weight_ref[at : at + LANES, q * LANES : (q + 1) * LANES] = given_ref[a * 3 + b]
     rows, cols, _ = feat_ref.shape
     cells = own_ref.shape[1] // 6
     step = 4
@@ -575,6 +588,7 @@
     group = lat_count * ring_count
     wide = cols + 16
     pairs = rows // 2 + 1
+    early_pairs = pairs // 4
     depth = band_rows + 2 * ROW_HALO
     params = pltpu.CompilerParams(vmem_limit_bytes=VMEM_BYTES)
     vmem = pl.BlockSpec(memory_space=pltpu.VMEM)
@@ -611,21 +625,20 @@
     got_outer = lax.ppermute(to_outer, "lat", outer)
     got_inner = lax.ppermute(to_inner, "lat", inner)
 
-    shift, back_weight, fore_weight, turned, first_weight, cot, near_w1, embed = pl.pallas_call(
+    shift, back_weight, turned, cot, near_w1, near_w2, embed, begun = pl.pallas_call(
         prepare_kernel,
         out_shape=[
             jax.ShapeDtypeStruct((3, 2, (pairs + 1) * wide, hidden), BF16),
             jax.ShapeDtypeStruct((12 * hidden, 2 * hidden), BF16),
-            jax.ShapeDtypeStruct((12 * hidden, 2 * hidden), BF16),
             jax.ShapeDtypeStruct((2 * hidden, rows // 2 * cols), BF16),
-            jax.ShapeDtypeStruct((9 * hidden, hidden), BF16),
             jax.ShapeDtypeStruct((rows, cols, hidden), BF16),
             jax.ShapeDtypeStruct((9, hidden, hidden), BF16),
+            jax.ShapeDtypeStruct((9, hidden, hidden), BF16),
             jax.ShapeDtypeStruct((LANES, hidden), BF16),
+            jax.ShapeDtypeStruct((2 * early_pairs, wide, hidden), F32),
         ],
         in_specs=[far] * 4,
         scratch_shapes=[
-            pltpu.VMEM((9, hidden, hidden), BF16),
             pltpu.VMEM((fields, hidden), BF16),
             pltpu.VMEM((4, wide + 16, hidden), F32),
             pltpu.SemaphoreType.DMA((11,)),
@@ -654,7 +667,7 @@
     bh, mixed, lifted, tap, cot_col, blend = pl.pallas_call(
         back_body,
         out_shape=[
-            jax.ShapeDtypeStruct((2 * pairs, wide, hidden), F32),
+            jax.ShapeDtypeStruct((2 * (pairs - early_pairs), wide, hidden), F32),
             jax.ShapeDtypeStruct((2, 3 * GRAD_ROWS, width), BF16),
             jax.ShapeDtypeStruct((reach * band_cols, hidden), F32),
             jax.ShapeDtypeStruct(((reach - 2) * band_cols, 3 * hidden), F32),
@@ -700,7 +713,7 @@
         name="tile",
     )(
         got_far, got_near, *col_line,
-        embed, near_w1, turned, bh, mixed, tap, cot_col, blend,
+        embed, near_w1, turned, begun, bh, mixed, tap, cot_col, blend,
     )
 
     def half_features(first, *arrays):
@@ -709,7 +722,12 @@
 
         return pl.pallas_call(
             body,
-            out_shape=jax.ShapeDtypeStruct((rows // 2, cols, hidden), BF16),
+            out_shape=[
+                jax.ShapeDtypeStruct((rows // 2, cols, hidden), BF16),
+                jax.ShapeDtypeStruct((9 * hidden, hidden), BF16)
+                if first
+                else jax.ShapeDtypeStruct((12 * hidden, 2 * hidden), BF16),
+            ],
             compiler_params=params,
             name=f"features_{first}",
         )(*arrays)
@@ -717,7 +735,7 @@
     swap = [(0, 1), (1, 0)]
     received = lax.ppermute(message[1], "core", swap)
     middle = rows // 4
-    part = half_features(0, fore_weight, hid, own_blend, lifted, side_lifted)
+    part, fore_weight = half_features(0, near_w2, hid, own_blend, lifted, side_lifted)
     received, part = lax.optimization_barrier((received, part))
     pair = (message[0].astype(F32) + received.astype(F32)).astype(BF16)
     axes = ("lat", "ring")
@@ -731,7 +749,9 @@
     )(parts.reshape(group, chunk, LANES))
     mine = lax.all_to_all(copies.reshape(half_rows, LANES), axes, 0, 0, tiled=True)
     other = lax.ppermute(mine, "core", swap)
-    last_part = half_features(middle, fore_weight, hid, own_blend, lifted, side_lifted, mine)
+    last_part, first_weight = half_features(
+        middle, fore_weight, hid, own_blend, lifted, side_lifted, mine, near_w1
+    )
     scale = 1.0 / math.sqrt(rows * lat_count * cols * lon_count)
 
     def finish(*refs):

time: 53.3 us -> 53.7 us (level)
  transfers between devices with their start and end apart: 6 -> 6, of which waited for: 1 -> 3; matrix products, arithmetic and copies ran while one was open for 0% -> 0% of each run, Pallas kernels for 14% -> 14%
where the time goes in v8:
time: 53.7 us; the launch traced here: 53.4 us
  blocking collectives  28.6 us (53%)
  Pallas kernels  13.9 us (26%)
  starting transfers between devices  9.31 us (17%)
  between operations  0.72 us (1%)
  waiting for transfers between devices  0.69 us (1%)
    all_to_all x1, blocking collectives, on_device(): parts = lax.all_to_all(pair, axes, 0, 0, tiled=True)  15.7 us
    all_to_all x1, blocking collectives, on_device(): lax.all_to_all(copies.reshape(half_rows, LANES), axes, 0, 0, tiled=True)  13 us
    ppermute x1, starting transfers between devices, on_device(): got_inner = lax.ppermute(to_inner, 'lat', inner)  5.74 us
    pallas_call x1, Pallas kernels, on_device(): pl.pallas_call(body, out_specs=[vmem] * 4, out_shape=[jax.ShapeDtypeStruc...  4.31 us
    pallas_call x1, Pallas kernels, on_device(): pl.pallas_call(prepare_kernel, out_shape=[jax.ShapeDtypeStruct((3, 2, (pa...  2.83 us
    ppermute x1, starting transfers between devices, on_device(): got_far = lax.ppermute(far_message, lon, outer)  2.55 us
    pallas_call x2, Pallas kernels, half_features(): pl.pallas_call(body, out_shape=[jax.ShapeDtypeStruct((rows // 2, cols, hi...  2.3 us
    pallas_call x1, Pallas kernels, on_device(): pl.pallas_call(back_body, out_shape=[jax.ShapeDtypeStruct((2 * (pairs - e...  2.21 us
  transfers between devices with their start and end apart: 6, of which 3 were waited for; matrix products, arithmetic and copies ran while one was open for 0% of the time, Pallas kernels for 14%

profile of v8, /device:TPU:0, one launch (start us, length us, event | category | flops | bytes accessed | tf_op | source)
XLA Modules:
  0.0 53.4 jit_solution(2484194180466203618)
XLA Ops:
  0.6 0.8 %pack.1 = (bf16[5,8,128]{2,1,0:T(8,128)(2,1)S(1)}, bf16[4,8,128]{2,1,0:T(8,128)(2,1)S(1)}, bf16[4,8,128]{2,1,0:T(8,128)(2,1)S(1)}, s32[1,32]{1,0:T(1,128)S(1)}, ...) custom-call(bf16[4,8,73]{2,1,0:T(8,128)(2,1)} %bitcast.22, s32[1,32]{1,0:T(1,128)} %bitcast.23, ...), custom_call_target="tpu_custom_call" | custom-call | tf_op jit(solution)/shard_map/pack/pallas_call | solution.py:607
  1.4 0.7 %collective-permute-start = (bf16[4,8,128]{2,1,0:T(8,128)(2,1)S(1)}, bf16[4,8,128]{2,1,0:T(8,128)(2,1)S(1)}, u32[]{:S(2)}, u32[]{:S(2)}) collective-permute-start(bf16[4,8,128]{2,1,0:T(8,128)(2,1)S(1)} %get-tuple-element.44), channel_id=1, source_target_pairs={{8,16},{16,8},{9,17},{17,9},{10,18},{18,10},{11,19},{19,11},{12,20... | collective-permute-start | bytes 24584 | tf_op jit(solution)/shard_map/ppermute | solution.py:625
  2.1 5.7 %collective-permute-start.1 = (bf16[4,8,128]{2,1,0:T(8,128)(2,1)S(1)}, bf16[4,8,128]{2,1,0:T(8,128)(2,1)S(1)}, u32[]{:S(2)}, u32[]{:S(2)}) collective-permute-start(bf16[4,8,128]{2,1,0:T(8,128)(2,1)S(1)} %get-tuple-element.45), channel_id=1, source_target_pairs={{0,8},{8,0},{16,24},{24,16},{1,9},{9,1},{17,25},{25,17},{2,10},{10... | collective-permute-start | bytes 24584 | tf_op jit(solution)/shard_map/ppermute | solution.py:626
  7.8 2.8 %prepare.1 = (bf16[3,2,2592,128]{3,2,1,0:T(8,128)(2,1)S(1)}, bf16[1536,256]{1,0:T(8,128)(2,1)S(1)}, bf16[256,2048]{1,0:T(8,128)(2,1)S(1)}, bf16[32,128,128]{2,1,...) custom-call(bf16[32,128,128]{2,1,0:T(8,128)(2,1)} %cot_hbm.1, ...), custom_call_target="tpu_custom_call" | custom-call | tf_op jit(solution)/shard_map/prepare/pallas_call | solution.py:628
  10.7 0.0 collective-permute-done.outer_ref
  10.7 0.0 collective-permute-done.1.inner_ref
  10.7 2.5 %collective-permute-start.2 = (bf16[6,8,128]{2,1,0:T(8,128)(2,1)S(1)}, bf16[6,8,128]{2,1,0:T(8,128)(2,1)S(1)}, u32[]{:S(2)}, u32[]{:S(2)}) collective-permute-start(bf16[6,8,128]{2,1,0:T(8,128)(2,1)S(1)} %get-tuple-element.47), channel_id=1, source_target_pairs={{0,7},{1,2},{2,1},{3,4},{4,3},{5,6},{6,5},{7,0},{8,15},{9,10},{10,... | collective-permute-start | bytes 36872 | tf_op jit(solution)/shard_map/ppermute | solution.py:659
  13.3 0.0 collective-permute-start.3
  13.3 2.2 %back_hidden.1 = (f32[26,144,128]{2,1,0:T(8,128)S(1)}, bf16[2,240,384]{2,1,0:T(8,128)(2,1)S(1)}, f32[288,128]{1,0:T(8,128)S(1)}, f32[272,384]{1,0:T(8,128)S(1)},...) custom-call(s32[1,32]{1,0:T(1,128)S(1)} %get-tuple-element.54.refs_0_, f32[1,32]{1,0:T(1,128)S(1)} %get-tuple-element.55.refs_1_, ...), custom_call_target="tpu_custom_call" | custom-call | tf_op jit(solution)/shard_map/back_hidden/pallas_call | solution.py:667
  15.5 0.2 collective-permute-done.2.refs_0_
  15.7 0.0 collective-permute-done.3.refs_1_
  15.7 4.3 %tile.1 = (bf16[3,2,2176,128]{3,2,1,0:T(8,128)(2,1)S(1)}, bf16[128,48]{1,0:T(8,128)(2,1)S(1)}, f32[288,128]{1,0:T(8,128)S(1)}, bf16[2,1024,128]{2,1,0:T(8,128)(2,1)S(1)}) custom-call(bf16[6,8,128]{2,1,0:T(8,128)(2,1)S(1)} %collective-permute-done.2.refs_0_, bf16[6,8,128]{2,1,0:T(8,128)(2,1)S(1)} %collective-permute-done.3.refs_1_, ...), custom_call_target="tpu_custom_call" | custom-call | tf_op jit(solution)/shard_map/tile/pallas_call | solution.py:696
  20.1 0.4 collective-permute-start.4
  20.4 1.2 %features_0.1 = (bf16[16,128,128]{2,1,0:T(8,128)(2,1)S(1)}, bf16[1536,256]{1,0:T(8,128)(2,1)S(1)}) custom-call(bf16[9,128,128]{2,1,0:T(8,128)(2,1)S(1)} %get-tuple-element.67.refs_0_, bf16[3,2,2176,128]{3,2,1,0:T(8,128)(2,1)S(1)} %get-tuple-element.68.refs_1_, bf16[128,48]{1,0:T(8,128)(2,1)S(1)} %get-tuple-element.69.refs_2_, ...), custom_call_target="tpu_custom_call" | custom-call | tf_op jit(solution)/shard_map/features_0/pallas_call | solution.py:723
  21.6 0.1 collective-permute-done.4
  21.7 0.1 fusion
  21.7 15.7 %all_to_all.17.in_ref = bf16[16,64,128]{2,1,0:T(8,128)(2,1)S(1)} all-to-all(bf16[16,64,128]{2,1,0:T(8,128)(2,1)S(1)} %bitcast.19), channel_id=1, replica_groups=mesh['lat'=4,'ring'=4,'core'=2] {'lat','ring'}, dimensions={0} | all-to-all | bytes 524288 | tf_op jit(solution)/shard_map/all_to_all | solution.py:743
  37.5 13.0 %all_to_all.18 = bf16[16,64,128]{2,1,0:T(8,128)(2,1)S(1)} all-to-all(bf16[16,64,128]{2,1,0:T(8,128)(2,1)S(1)} %sum_chunks.1), channel_id=1, replica_groups=mesh['lat'=4,'ring'=4,'core'=2] {'lat','ring'}, dimensions={0} | all-to-all | bytes 524288 | tf_op jit(solution)/shard_map/all_to_all | solution.py:750
  50.4 0.0 collective-permute-start.5
  50.4 1.1 %features_8.1 = (bf16[16,128,128]{2,1,0:T(8,128)(2,1)S(1)}, bf16[1152,128]{1,0:T(8,128)(2,1)S(1)}) custom-call(bf16[1536,256]{1,0:T(8,128)(2,1)S(1)} %get-tuple-element.74.refs_0_, bf16[3,2,2176,128]{3,2,1,0:T(8,128)(2,1)S(1)} %get-tuple-element.68.refs_1_, bf16[128,48]{1,0:T(8,128)(2,1)S(1)} %get-tuple-element.69.refs_2_, ...), custom_call_target="tpu_custom_call" | custom-call | tf_op jit(solution)/shard_map/features_8/pallas_call | solution.py:723
  51.5 0.4 collective-permute-done.5.refs_1_
  52.0 1.4 %finish.1 = (bf16[32,128,128]{2,1,0:T(8,128)(2,1)}, f32[73,128]{1,0:T(8,128)}, f32[9,128,128]{2,1,0:T(8,128)}, f32[9,128,128]{2,1,0:T(8,128)}) custom-call(bf16[1024,128]{1,0:T(8,128)(2,1)S(1)} %bitcast.18, bf16[1024,128]{1,0:T(8,128)(2,1)S(1)} %collective-permute-done.5.refs_1_, bf16[128,128]{1,0:T(8,128)(2,1)S(1)} %get-tuple-element.46.ready_ref.refs_9_.refs_4_.refs_2_, ...), custom_call_target="tpu_custom_call" | custom-call | tf_op jit(solution)/shard_map/finish/pallas_call | solution.py:760
  (3 shorter events, 0.1 us)
Async XLA Ops:
  1.4 9.3 %collective-permute-start = (bf16[4,8,128]{2,1,0:T(8,128)(2,1)S(1)}, bf16[4,8,128]{2,1,0:T(8,128)(2,1)S(1)}, u32[]{:S(2)}, u32[]{:S(2)}) collective-permute-start(bf16[4,8,128]{2,1,0:T(8,128)(2,1)S(1)} %get-tuple-element.44), channel_id=1, source_target_pairs={{8,16},{16,8},{9,17},{17,9},{10,18},{18,10},{11,19},{19,11},{12,20... | collective-permute-start | bytes 24584 | tf_op jit(solution)/shard_map/ppermute | solution.py:625
  2.1 8.6 %collective-permute-start.1 = (bf16[4,8,128]{2,1,0:T(8,128)(2,1)S(1)}, bf16[4,8,128]{2,1,0:T(8,128)(2,1)S(1)}, u32[]{:S(2)}, u32[]{:S(2)}) collective-permute-start(bf16[4,8,128]{2,1,0:T(8,128)(2,1)S(1)} %get-tuple-element.45), channel_id=1, source_target_pairs={{0,8},{8,0},{16,24},{24,16},{1,9},{9,1},{17,25},{25,17},{2,10},{10... | collective-permute-start | bytes 24584 | tf_op jit(solution)/shard_map/ppermute | solution.py:626
  10.7 5.0 %collective-permute-start.2 = (bf16[6,8,128]{2,1,0:T(8,128)(2,1)S(1)}, bf16[6,8,128]{2,1,0:T(8,128)(2,1)S(1)}, u32[]{:S(2)}, u32[]{:S(2)}) collective-permute-start(bf16[6,8,128]{2,1,0:T(8,128)(2,1)S(1)} %get-tuple-element.47), channel_id=1, source_target_pairs={{0,7},{1,2},{2,1},{3,4},{4,3},{5,6},{6,5},{7,0},{8,15},{9,10},{10,... | collective-permute-start | bytes 36872 | tf_op jit(solution)/shard_map/ppermute | solution.py:659
  13.3 2.4 %collective-permute-start.3 = (bf16[6,8,128]{2,1,0:T(8,128)(2,1)S(1)}, bf16[6,8,128]{2,1,0:T(8,128)(2,1)S(1)}, u32[]{:S(2)}, u32[]{:S(2)}) collective-permute-start(bf16[6,8,128]{2,1,0:T(8,128)(2,1)S(1)} %get-tuple-element.48), channel_id=1, source_target_pairs={{0,1},{1,0},{2,3},{3,2},{4,5},{5,4},{6,7},{7,6},{8,9},{9,8},{10,11... | collective-permute-start | bytes 36872 | tf_op jit(solution)/shard_map/ppermute | solution.py:660
  20.1 1.6 %collective-permute-start.4 = (bf16[1024,128]{1,0:T(8,128)(2,1)S(1)}, bf16[1024,128]{1,0:T(8,128)(2,1)S(1)}, u32[]{:S(2)}, u32[]{:S(2)}) collective-permute-start(bf16[1024,128]{1,0:T(8,128)(2,1)S(1)} %slice_bitcast_fusion), channel_id=1, source_target_pairs={{0,1},{1,0},{2,3},{3,2},{4,5},{5,4},{6,7},{7,6},{8,9},{9,8},{10,11... | collective-permute-start | bytes 786440 | tf_op jit(solution)/shard_map/ppermute | solution.py:736
  50.4 1.5 %collective-permute-start.5 = (bf16[1024,128]{1,0:T(8,128)(2,1)S(1)}, bf16[1024,128]{1,0:T(8,128)(2,1)S(1)}, u32[]{:S(2)}, u32[]{:S(2)}) collective-permute-start(bf16[1024,128]{1,0:T(8,128)(2,1)S(1)} %bitcast.16), channel_id=1, source_target_pairs={{0,1},{1,0},{2,3},{3,2},{4,5},{5,4},{6,7},{7,6},{8,9},{9,8},{10,11... | collective-permute-start | bytes 786440 | tf_op jit(solution)/shard_map/ppermute | solution.py:751

commit v9 on v8

--- a/solution.py
+++ b/solution.py
@@ -588,7 +588,7 @@
     group = lat_count * ring_count
     wide = cols + 16
     pairs = rows // 2 + 1
-    early_pairs = pairs // 4
+    early_pairs = 1
     depth = band_rows + 2 * ROW_HALO
     params = pltpu.CompilerParams(vmem_limit_bytes=VMEM_BYTES)
     vmem = pl.BlockSpec(memory_space=pltpu.VMEM)

time: 53.7 us -> 53.4 us (level)
  transfers between devices with their start and end apart: 6 -> 6, of which waited for: 3 -> 1; matrix products, arithmetic and copies ran while one was open for 0% -> 0% of each run, Pallas kernels for 14% -> 14%
where the time goes in v9:
time: 53.4 us; the launch traced here: 53.1 us
  blocking collectives  28.3 us (53%)
  Pallas kernels  14 us (26%)
  starting transfers between devices  9.52 us (18%)
  between operations  0.74 us (1%)
    all_to_all x1, blocking collectives, on_device(): parts = lax.all_to_all(pair, axes, 0, 0, tiled=True)  15.4 us
    all_to_all x1, blocking collectives, on_device(): lax.all_to_all(copies.reshape(half_rows, LANES), axes, 0, 0, tiled=True)  13 us
    ppermute x1, starting transfers between devices, on_device(): got_inner = lax.ppermute(to_inner, 'lat', inner)  5.74 us
    pallas_call x1, Pallas kernels, on_device(): pl.pallas_call(body, out_specs=[vmem] * 4, out_shape=[jax.ShapeDtypeStruc...  4.35 us
    ppermute x1, starting transfers between devices, on_device(): got_far = lax.ppermute(far_message, lon, outer)  2.55 us
    pallas_call x1, Pallas kernels, on_device(): pl.pallas_call(back_body, out_shape=[jax.ShapeDtypeStruct((2 * (pairs - e...  2.53 us
    pallas_call x1, Pallas kernels, on_device(): pl.pallas_call(prepare_kernel, out_shape=[jax.ShapeDtypeStruct((3, 2, (pa...  2.49 us
    pallas_call x2, Pallas kernels, half_features(): pl.pallas_call(body, out_shape=[jax.ShapeDtypeStruct((rows // 2, cols, hi...  2.3 us
  transfers between devices with their start and end apart: 6, of which 1 were waited for; matrix products, arithmetic and copies ran while one was open for 0% of the time, Pallas kernels for 14%

profile of v9, /device:TPU:0, one launch (start us, length us, event | category | flops | bytes accessed | tf_op | source)
XLA Modules:
  0.0 53.1 jit_solution(11899828179128156903)
XLA Ops:
  0.6 0.8 %pack.1 = (bf16[5,8,128]{2,1,0:T(8,128)(2,1)S(1)}, bf16[4,8,128]{2,1,0:T(8,128)(2,1)S(1)}, bf16[4,8,128]{2,1,0:T(8,128)(2,1)S(1)}, s32[1,32]{1,0:T(1,128)S(1)}, ...) custom-call(bf16[4,8,73]{2,1,0:T(8,128)(2,1)} %bitcast.22, s32[1,32]{1,0:T(1,128)} %bitcast.23, ...), custom_call_target="tpu_custom_call" | custom-call | tf_op jit(solution)/shard_map/pack/pallas_call | solution.py:607
  1.4 0.7 %collective-permute-start = (bf16[4,8,128]{2,1,0:T(8,128)(2,1)S(1)}, bf16[4,8,128]{2,1,0:T(8,128)(2,1)S(1)}, u32[]{:S(2)}, u32[]{:S(2)}) collective-permute-start(bf16[4,8,128]{2,1,0:T(8,128)(2,1)S(1)} %get-tuple-element.44), channel_id=1, source_target_pairs={{8,16},{16,8},{9,17},{17,9},{10,18},{18,10},{11,19},{19,11},{12,20... | collective-permute-start | bytes 24584 | tf_op jit(solution)/shard_map/ppermute | solution.py:625
  2.1 5.7 %collective-permute-start.1 = (bf16[4,8,128]{2,1,0:T(8,128)(2,1)S(1)}, bf16[4,8,128]{2,1,0:T(8,128)(2,1)S(1)}, u32[]{:S(2)}, u32[]{:S(2)}) collective-permute-start(bf16[4,8,128]{2,1,0:T(8,128)(2,1)S(1)} %get-tuple-element.45), channel_id=1, source_target_pairs={{0,8},{8,0},{16,24},{24,16},{1,9},{9,1},{17,25},{25,17},{2,10},{10... | collective-permute-start | bytes 24584 | tf_op jit(solution)/shard_map/ppermute | solution.py:626
  7.8 2.5 %prepare.1 = (bf16[3,2,2592,128]{3,2,1,0:T(8,128)(2,1)S(1)}, bf16[1536,256]{1,0:T(8,128)(2,1)S(1)}, bf16[256,2048]{1,0:T(8,128)(2,1)S(1)}, bf16[32,128,128]{2,1,...) custom-call(bf16[32,128,128]{2,1,0:T(8,128)(2,1)} %cot_hbm.1, ...), custom_call_target="tpu_custom_call" | custom-call | tf_op jit(solution)/shard_map/prepare/pallas_call | solution.py:628
  10.3 0.0 collective-permute-done.outer_ref
  10.3 0.0 collective-permute-done.1.inner_ref
  10.4 2.5 %collective-permute-start.2 = (bf16[6,8,128]{2,1,0:T(8,128)(2,1)S(1)}, bf16[6,8,128]{2,1,0:T(8,128)(2,1)S(1)}, u32[]{:S(2)}, u32[]{:S(2)}) collective-permute-start(bf16[6,8,128]{2,1,0:T(8,128)(2,1)S(1)} %get-tuple-element.47), channel_id=1, source_target_pairs={{0,7},{1,2},{2,1},{3,4},{4,3},{5,6},{6,5},{7,0},{8,15},{9,10},{10,... | collective-permute-start | bytes 36872 | tf_op jit(solution)/shard_map/ppermute | solution.py:659
  12.9 0.0 collective-permute-start.3
  12.9 2.5 %back_hidden.1 = (f32[32,144,128]{2,1,0:T(8,128)S(1)}, bf16[2,240,384]{2,1,0:T(8,128)(2,1)S(1)}, f32[288,128]{1,0:T(8,128)S(1)}, f32[272,384]{1,0:T(8,128)S(1)},...) custom-call(s32[1,32]{1,0:T(1,128)S(1)} %get-tuple-element.54.refs_0_, f32[1,32]{1,0:T(1,128)S(1)} %get-tuple-element.55.refs_1_, ...), custom_call_target="tpu_custom_call" | custom-call | tf_op jit(solution)/shard_map/back_hidden/pallas_call | solution.py:667
  15.5 0.0 collective-permute-done.2.refs_0_
  15.5 0.0 collective-permute-done.3.refs_1_
  15.5 4.3 %tile.1 = (bf16[3,2,2176,128]{3,2,1,0:T(8,128)(2,1)S(1)}, bf16[128,48]{1,0:T(8,128)(2,1)S(1)}, f32[288,128]{1,0:T(8,128)S(1)}, bf16[2,1024,128]{2,1,0:T(8,128)(2,1)S(1)}) custom-call(bf16[6,8,128]{2,1,0:T(8,128)(2,1)S(1)} %collective-permute-done.2.refs_0_, bf16[6,8,128]{2,1,0:T(8,128)(2,1)S(1)} %collective-permute-done.3.refs_1_, ...), custom_call_target="tpu_custom_call" | custom-call | tf_op jit(solution)/shard_map/tile/pallas_call | solution.py:696
  19.9 0.6 %collective-permute-start.4 = (bf16[1024,128]{1,0:T(8,128)(2,1)S(1)}, bf16[1024,128]{1,0:T(8,128)(2,1)S(1)}, u32[]{:S(2)}, u32[]{:S(2)}) collective-permute-start(bf16[1024,128]{1,0:T(8,128)(2,1)S(1)} %slice_bitcast_fusion), channel_id=1, source_target_pairs={{0,1},{1,0},{2,3},{3,2},{4,5},{5,4},{6,7},{7,6},{8,9},{9,8},{10,11... | collective-permute-start | bytes 786440 | tf_op jit(solution)/shard_map/ppermute | solution.py:736
  20.4 1.2 %features_0.1 = (bf16[16,128,128]{2,1,0:T(8,128)(2,1)S(1)}, bf16[1536,256]{1,0:T(8,128)(2,1)S(1)}) custom-call(bf16[9,128,128]{2,1,0:T(8,128)(2,1)S(1)} %get-tuple-element.67.refs_0_, bf16[3,2,2176,128]{3,2,1,0:T(8,128)(2,1)S(1)} %get-tuple-element.68.refs_1_, bf16[128,48]{1,0:T(8,128)(2,1)S(1)} %get-tuple-element.69.refs_2_, ...), custom_call_target="tpu_custom_call" | custom-call | tf_op jit(solution)/shard_map/features_0/pallas_call | solution.py:723
  21.6 0.0 collective-permute-done.4
  21.6 0.1 fusion
  21.7 15.4 %all_to_all.17.in_ref = bf16[16,64,128]{2,1,0:T(8,128)(2,1)S(1)} all-to-all(bf16[16,64,128]{2,1,0:T(8,128)(2,1)S(1)} %bitcast.19), channel_id=1, replica_groups=mesh['lat'=4,'ring'=4,'core'=2] {'lat','ring'}, dimensions={0} | all-to-all | bytes 524288 | tf_op jit(solution)/shard_map/all_to_all | solution.py:743
  37.1 13.0 %all_to_all.18 = bf16[16,64,128]{2,1,0:T(8,128)(2,1)S(1)} all-to-all(bf16[16,64,128]{2,1,0:T(8,128)(2,1)S(1)} %sum_chunks.1), channel_id=1, replica_groups=mesh['lat'=4,'ring'=4,'core'=2] {'lat','ring'}, dimensions={0} | all-to-all | bytes 524288 | tf_op jit(solution)/shard_map/all_to_all | solution.py:750
  50.1 0.0 collective-permute-start.5
  50.1 1.1 %features_8.1 = (bf16[16,128,128]{2,1,0:T(8,128)(2,1)S(1)}, bf16[1152,128]{1,0:T(8,128)(2,1)S(1)}) custom-call(bf16[1536,256]{1,0:T(8,128)(2,1)S(1)} %get-tuple-element.74.refs_0_, bf16[3,2,2176,128]{3,2,1,0:T(8,128)(2,1)S(1)} %get-tuple-element.68.refs_1_, bf16[128,48]{1,0:T(8,128)(2,1)S(1)} %get-tuple-element.69.refs_2_, ...), custom_call_target="tpu_custom_call" | custom-call | tf_op jit(solution)/shard_map/features_8/pallas_call | solution.py:723
  51.2 0.4 collective-permute-done.5.refs_1_
  51.6 1.4 %finish.1 = (bf16[32,128,128]{2,1,0:T(8,128)(2,1)}, f32[73,128]{1,0:T(8,128)}, f32[9,128,128]{2,1,0:T(8,128)}, f32[9,128,128]{2,1,0:T(8,128)}) custom-call(bf16[1024,128]{1,0:T(8,128)(2,1)S(1)} %bitcast.18, bf16[1024,128]{1,0:T(8,128)(2,1)S(1)} %collective-permute-done.5.refs_1_, bf16[128,128]{1,0:T(8,128)(2,1)S(1)} %get-tuple-element.46.ready_ref.refs_9_.refs_4_.refs_2_, ...), custom_call_target="tpu_custom_call" | custom-call | tf_op jit(solution)/shard_map/finish/pallas_call | solution.py:760
  (3 shorter events, 0.1 us)
Async XLA Ops:
  1.4 8.9 %collective-permute-start = (bf16[4,8,128]{2,1,0:T(8,128)(2,1)S(1)}, bf16[4,8,128]{2,1,0:T(8,128)(2,1)S(1)}, u32[]{:S(2)}, u32[]{:S(2)}) collective-permute-start(bf16[4,8,128]{2,1,0:T(8,128)(2,1)S(1)} %get-tuple-element.44), channel_id=1, source_target_pairs={{8,16},{16,8},{9,17},{17,9},{10,18},{18,10},{11,19},{19,11},{12,20... | collective-permute-start | bytes 24584 | tf_op jit(solution)/shard_map/ppermute | solution.py:625
  2.1 8.3 %collective-permute-start.1 = (bf16[4,8,128]{2,1,0:T(8,128)(2,1)S(1)}, bf16[4,8,128]{2,1,0:T(8,128)(2,1)S(1)}, u32[]{:S(2)}, u32[]{:S(2)}) collective-permute-start(bf16[4,8,128]{2,1,0:T(8,128)(2,1)S(1)} %get-tuple-element.45), channel_id=1, source_target_pairs={{0,8},{8,0},{16,24},{24,16},{1,9},{9,1},{17,25},{25,17},{2,10},{10... | collective-permute-start | bytes 24584 | tf_op jit(solution)/shard_map/ppermute | solution.py:626
  10.4 5.1 %collective-permute-start.2 = (bf16[6,8,128]{2,1,0:T(8,128)(2,1)S(1)}, bf16[6,8,128]{2,1,0:T(8,128)(2,1)S(1)}, u32[]{:S(2)}, u32[]{:S(2)}) collective-permute-start(bf16[6,8,128]{2,1,0:T(8,128)(2,1)S(1)} %get-tuple-element.47), channel_id=1, source_target_pairs={{0,7},{1,2},{2,1},{3,4},{4,3},{5,6},{6,5},{7,0},{8,15},{9,10},{10,... | collective-permute-start | bytes 36872 | tf_op jit(solution)/shard_map/ppermute | solution.py:659
  12.9 2.5 %collective-permute-start.3 = (bf16[6,8,128]{2,1,0:T(8,128)(2,1)S(1)}, bf16[6,8,128]{2,1,0:T(8,128)(2,1)S(1)}, u32[]{:S(2)}, u32[]{:S(2)}) collective-permute-start(bf16[6,8,128]{2,1,0:T(8,128)(2,1)S(1)} %get-tuple-element.48), channel_id=1, source_target_pairs={{0,1},{1,0},{2,3},{3,2},{4,5},{5,4},{6,7},{7,6},{8,9},{9,8},{10,11... | collective-permute-start | bytes 36872 | tf_op jit(solution)/shard_map/ppermute | solution.py:660
  19.9 1.8 %collective-permute-start.4 = (bf16[1024,128]{1,0:T(8,128)(2,1)S(1)}, bf16[1024,128]{1,0:T(8,128)(2,1)S(1)}, u32[]{:S(2)}, u32[]{:S(2)}) collective-permute-start(bf16[1024,128]{1,0:T(8,128)(2,1)S(1)} %slice_bitcast_fusion), channel_id=1, source_target_pairs={{0,1},{1,0},{2,3},{3,2},{4,5},{5,4},{6,7},{7,6},{8,9},{9,8},{10,11... | collective-permute-start | bytes 786440 | tf_op jit(solution)/shard_map/ppermute | solution.py:736
  50.1 1.5 %collective-permute-start.5 = (bf16[1024,128]{1,0:T(8,128)(2,1)S(1)}, bf16[1024,128]{1,0:T(8,128)(2,1)S(1)}, u32[]{:S(2)}, u32[]{:S(2)}) collective-permute-start(bf16[1024,128]{1,0:T(8,128)(2,1)S(1)} %bitcast.16), channel_id=1, source_target_pairs={{0,1},{1,0},{2,3},{3,2},{4,5},{5,4},{6,7},{7,6},{8,9},{9,8},{10,11... | collective-permute-start | bytes 786440 | tf_op jit(solution)/shard_map/ppermute | solution.py:751
